TPU v7x, 32 devices: a whole 2x2x4 slice. The times are simulated.
32 devices in a mesh: dp: 2 (over x), ctx: 16 (over z, y, core).
Axes of the slice: x: 2, y: 2, z: 4, core: 2. Of those that a mesh axis runs over, the one named last changes fastest.
Arguments:
- tokens: bfloat16 [2, 2048, 1024], P('dp', 'ctx'), may hold values from -6 to 6
- segments: int32 [2, 2048], P('dp', 'ctx'), may hold values from 0 to 2, as said below
- cotangent: bfloat16 [2, 2048, 1024], P('dp', 'ctx'), may hold values from -6 to 6
- conv_weights: bfloat16 [1024, 17920], P('ctx'), may hold values from -0.1875 to 0.1875
- attn_weights: bfloat16 [1024, 16896], P('ctx')
- vectors: float32 [7, 1024], replicated, may hold values from 0.5 to 1.5
- head_gains: float32 [2, 64], replicated, may hold values from 0.5 to 1.5
- master_conv: float32 [1024, 17920], P('ctx', 'dp'), may hold values from -0.1875 to 0.1875
- first_conv: float32 [1024, 17920], P('ctx', 'dp'), may hold values from -6 to 6
- second_conv: float32 [1024, 17920], P('ctx', 'dp'), may hold values from 0.1 to 100
- master_attn: float32 [1024, 16896], P('ctx', 'dp'), may hold values from -0.1875 to 0.1875
- first_attn: float32 [1024, 16896], P('ctx', 'dp'), may hold values from -6 to 6
- second_attn: float32 [1024, 16896], P('ctx', 'dp'), may hold values from 0.1 to 100
Outputs:
- out_tokens: bfloat16 [2, 2048, 1024], P('dp', 'ctx')
- grad_tokens: float32 [2, 2048, 1024], P('dp', 'ctx')
- grad_conv: float32 [1024, 17920], P('ctx', 'dp')
- grad_attn: float32 [1024, 16896], P('ctx', 'dp')
- grad_vectors: float32 [7, 1024], replicated
- grad_gains: float32 [2, 64], replicated
- new_master_conv: float32 [1024, 17920], P('ctx', 'dp')
- new_first_conv: float32 [1024, 17920], P('ctx', 'dp')
- new_second_conv: float32 [1024, 17920], P('ctx', 'dp')
- new_master_attn: float32 [1024, 16896], P('ctx', 'dp')
- new_first_attn: float32 [1024, 16896], P('ctx', 'dp')
- new_second_attn: float32 [1024, 16896], P('ctx', 'dp')
- new_conv_weights: bfloat16 [1024, 17920], P('ctx')
- new_attn_weights: bfloat16 [1024, 16896], P('ctx')
Inputs may be any that keep to these rules, and one draw needn't show every extreme that they name: `segments`: within each sequence the segment ids start at 0 and never fall, each of the 3 ids is used; document 1 begins within the first 128 positions and ends within the last 128 positions.
All inputs are finite; a program needn't handle non-finite values.
Results may differ from a plain program's by a relative error of at most 0.025.
Values may be sent and summed in bfloat16 or wider, within the bound.
A program may use at most 640 MiB of HBM per device.

v0:
```python
import jax
import jax.numpy as jnp
from jax import lax
from jax.sharding import PartitionSpec as P

D = 1024
FF = 4608
HEADS = 16
KV_HEADS = 8
HEAD_DIM = 64
STEP = 5
KVW = 512


norm_eps = 1e-05
rope_base = 1000000.0
learn_rate = 0.01
decay_rate = 0.1
beta_one = 0.9
beta_two = 0.95
adam_eps = 1e-08
masked_score = -1e30


def from_behind(block, axis, distance):
    devices = range(lax.axis_size(axis))
    route = [(i - distance, i) for i in devices if i - distance in devices]
    return lax.ppermute(block, axis, route)


def rms_apply(value, gain):
    return value * lax.rsqrt(jnp.mean(value * value, axis=-1, keepdims=True) + norm_eps) * gain


def rotate(value, cosines, sines):
    half_width = value.shape[-1] // 2
    turned = jnp.concatenate([-value[..., half_width:], value[..., :half_width]], axis=-1)
    return value * cosines + turned * sines


def doc_positions(segment):
    places = jnp.arange(segment.shape[0], dtype=jnp.int32)
    starts = jnp.concatenate([jnp.ones((1,), dtype=jnp.bool_), segment[1:] != segment[:-1]])
    return places - lax.cummax(jnp.where(starts, places, 0), axis=0)


def rope_tables(positions):
    inverse_freq = rope_base ** (-(jnp.arange(HEAD_DIM // 2, dtype=jnp.float32) * 2.0) / HEAD_DIM)
    angles = positions.astype(jnp.float32)[:, None] * inverse_freq[None, :]
    cosines = jnp.concatenate([jnp.cos(angles), jnp.cos(angles)], axis=-1)
    sines = jnp.concatenate([jnp.sin(angles), jnp.sin(angles)], axis=-1)
    return (cosines[:, None, :], sines[:, None, :])


def matmul(left, right):
    return jnp.dot(left, right, preferred_element_type=jnp.float32)


def matmul_t(left, right):
    return lax.dot_general(
        left, right, (((1,), (1,)), ((), ())), preferred_element_type=jnp.float32
    )


def tokens_t(left, right):
    return lax.dot_general(
        left, right, (((0,), (0,)), ((), ())), preferred_element_type=jnp.float32
    )


def swiglu(gate_in, up_in):
    return jax.nn.silu(gate_in) * up_in


def ffn_forward(value, gain, matrices, base):
    hidden = rms_apply(value, gain).astype(jnp.bfloat16)
    gate_out = matmul(hidden, matrices[:, base : base + FF])
    up_out = matmul(hidden, matrices[:, base + FF : base + 2 * FF])
    mixed = swiglu(gate_out, up_out).astype(jnp.bfloat16)
    result = value + matmul_t(mixed, matrices[:, base + 2 * FF : base + 3 * FF])
    return (result, (hidden, gate_out, up_out, mixed))


def ffn_backward(value, gain, matrices, base, saved, grad_out):
    hidden, gate_out, up_out, mixed = saved
    down_in = grad_out.astype(jnp.bfloat16)
    grad_down = tokens_t(down_in, mixed)
    grad_mixed = matmul(down_in, matrices[:, base + 2 * FF : base + 3 * FF])
    unused, swiglu_back = jax.vjp(swiglu, gate_out, up_out)
    grad_gate, grad_up = swiglu_back(grad_mixed)
    both_grads = jnp.concatenate([grad_gate, grad_up], axis=1).astype(jnp.bfloat16)
    grad_both = tokens_t(hidden, both_grads)
    grad_hidden = matmul_t(both_grads, matrices[:, base : base + 2 * FF])
    unused, norm_back = jax.vjp(rms_apply, value, gain)
    grad_value, grad_gain = norm_back(grad_hidden)
    return (grad_out + grad_value, grad_gain, (grad_both, grad_down))


def reduce_grads(local_grad):
    row_part = lax.psum_scatter(local_grad, "ctx", scatter_dimension=0, tiled=True)
    return lax.psum_scatter(
        row_part.astype(jnp.bfloat16), "dp", scatter_dimension=1, tiled=True
    ).astype(jnp.float32)


def adam_update(master, first_moment, second, gradient, step_value):
    first_new = beta_one * first_moment + (1.0 - beta_one) * gradient
    second_new = beta_two * second + (1.0 - beta_two) * gradient * gradient
    first_hat = first_new / (1.0 - beta_one**step_value)
    second_hat = second_new / (1.0 - beta_two**step_value)
    master_new = master - learn_rate * (
        first_hat / (jnp.sqrt(second_hat) + adam_eps) + decay_rate * master
    )
    return (master_new, first_new, second_new)


def shards(
    tokens,
    segments,
    cotangent,
    conv_weights,
    attn_weights,
    vectors,
    head_gains,
    master_conv,
    first_conv,
    second_conv,
    master_attn,
    first_attn,
    second_attn,
):
    row_count = tokens.shape[1]
    group = HEADS // KV_HEADS
    qkv_width = D + 2 * KVW
    score_scale = HEAD_DIM ** (-0.5)
    seg_all = lax.all_gather(segments, "ctx", axis=1, tiled=True)[0]
    length = seg_all.shape[0]
    offset = lax.axis_index("ctx") * row_count
    my_seg = lax.dynamic_slice_in_dim(seg_all, offset, row_count)
    padded_seg = jnp.concatenate([jnp.full((2,), -1, jnp.int32), seg_all])
    mask_one = (lax.dynamic_slice_in_dim(padded_seg, offset + 1, row_count) == my_seg).astype(
        jnp.float32
    )[:, None]
    mask_two = (lax.dynamic_slice_in_dim(padded_seg, offset, row_count) == my_seg).astype(
        jnp.float32
    )[:, None]
    my_pos = lax.dynamic_slice_in_dim(doc_positions(seg_all), offset, row_count)
    cosines, sines = rope_tables(my_pos)
    conv_full, attn_full = (
        lax.all_gather(conv_weights, "ctx", axis=0, tiled=True),
        lax.all_gather(attn_weights, "ctx", axis=0, tiled=True),
    )
    x_zero = tokens[0].astype(jnp.float32)
    h_one = rms_apply(x_zero, vectors[0]).astype(jnp.bfloat16)
    w_in = conv_full[:, : 3 * D]
    proj = matmul(h_one, w_in)
    gate_b = proj[:, :D]
    gate_c = proj[:, D : 2 * D]
    inner = proj[:, 2 * D :]
    mixed = gate_b * inner
    rim_rows = from_behind(mixed[row_count - 2 :], "ctx", 1)
    extended = jnp.concatenate([rim_rows, mixed], axis=0)
    prev_one = extended[1 : row_count + 1]
    prev_two = extended[:row_count]
    conv = vectors[4] * mixed + vectors[5] * prev_one * mask_one + vectors[6] * prev_two * mask_two
    outer = (gate_c * conv).astype(jnp.bfloat16)
    w_conv_out = conv_full[:, 3 * D : 4 * D]
    x_one = x_zero + matmul_t(outer, w_conv_out)
    x_two, saved_one = ffn_forward(x_one, vectors[1], conv_full, 4 * D)
    h_three = rms_apply(x_two, vectors[2]).astype(jnp.bfloat16)
    qkv = matmul(h_three, attn_full[:, :qkv_width])
    q_raw = qkv[:, :D].reshape(row_count, HEADS, HEAD_DIM)
    k_raw = qkv[:, D : D + KVW].reshape(row_count, KV_HEADS, HEAD_DIM)

    def prepare(raw_heads, head_gain):
        return rotate(rms_apply(raw_heads, head_gain), cosines, sines)

    query = (
        prepare(q_raw, head_gains[0])
        .astype(jnp.bfloat16)
        .reshape(row_count, KV_HEADS, group, HEAD_DIM)
    )
    keys_mine = prepare(k_raw, head_gains[1]).astype(jnp.bfloat16).reshape(row_count, KVW)
    values_mine = qkv[:, D + KVW :].astype(jnp.bfloat16)
    q_pos = offset + jnp.arange(row_count, dtype=jnp.int32)
    last_query = offset + row_count - 1

    def block_view(keys_piece, values_piece, block_index):
        k_start = block_index * row_count
        key_block = lax.dynamic_slice_in_dim(
            keys_piece, block_index * row_count, row_count
        ).reshape(row_count, KV_HEADS, HEAD_DIM)
        value_block = lax.dynamic_slice_in_dim(
            values_piece, block_index * row_count, row_count
        ).reshape(row_count, KV_HEADS, HEAD_DIM)
        k_seg = lax.dynamic_slice_in_dim(seg_all, k_start, row_count)
        k_pos = k_start + jnp.arange(row_count, dtype=jnp.int32)
        allowed = (k_pos[None, :] <= q_pos[:, None]) & (k_seg[None, :] == my_seg[:, None])
        needed = (k_start <= last_query) & (k_seg[row_count - 1] >= my_seg[0])
        return (key_block, value_block, k_start, allowed, needed)

    start_max = jnp.full((KV_HEADS, group, row_count), masked_score, jnp.float32)
    start_sum = jnp.zeros((KV_HEADS, group, row_count), jnp.float32)
    start_acc = jnp.zeros((KV_HEADS, group, row_count, HEAD_DIM), jnp.float32)
    keys_piece = lax.all_gather(keys_mine, "ctx", axis=0, tiled=True)
    values_piece = lax.all_gather(values_mine, "ctx", axis=0, tiled=True)

    def attend_one_block(block_index, running):
        key_block, value_block, k_start, allowed, needed = block_view(
            keys_piece, values_piece, block_index
        )

        def attend_compute(current):
            run_max, run_sum, run_acc = current
            scores = (
                jnp.einsum("tgrd,ngd->grtn", query, key_block, preferred_element_type=jnp.float32)
                * score_scale
            )
            masked = jnp.where(allowed, scores, masked_score)
            new_max = jnp.maximum(run_max, jnp.max(masked, axis=-1))
            weights = jnp.where(allowed, jnp.exp(masked - new_max[..., None]), 0.0)
            factor = jnp.exp(run_max - new_max)
            new_sum = run_sum * factor + jnp.sum(weights, axis=-1)
            new_acc = run_acc * factor[..., None] + jnp.einsum(
                "grtn,ngd->grtd",
                weights.astype(jnp.bfloat16),
                value_block,
                preferred_element_type=jnp.float32,
            )
            return (new_max, new_sum, new_acc)

        return lax.cond(needed, attend_compute, lambda current: current, running)

    run_max, run_sum, run_acc = lax.fori_loop(
        0, keys_piece.shape[0] // row_count, attend_one_block, (start_max, start_sum, start_acc)
    )
    log_total = run_max + jnp.log(run_sum)
    attended_heads = run_acc / run_sum[..., None]
    attended = attended_heads.transpose(2, 0, 1, 3).reshape(row_count, D).astype(jnp.bfloat16)
    w_attn_out = attn_full[:, qkv_width : qkv_width + D]
    x_three = x_two + matmul_t(attended, w_attn_out)
    x_four, saved_two = ffn_forward(x_three, vectors[3], attn_full, qkv_width + D)
    out_tokens = x_four.astype(jnp.bfloat16)[None]
    grad_four = cotangent[0].astype(jnp.float32)
    grad_three, grad_gain4, ffn_two_grads = ffn_backward(
        x_three, vectors[3], attn_full, qkv_width + D, saved_two, grad_four
    )
    attn_in = grad_three.astype(jnp.bfloat16)
    grad_attn_out = tokens_t(attn_in, attended)
    grad_heads = (
        matmul(attn_in, w_attn_out)
        .astype(jnp.bfloat16)
        .reshape(row_count, KV_HEADS, group, HEAD_DIM)
    )
    delta = jnp.sum(grad_heads.astype(jnp.float32).transpose(1, 2, 0, 3) * attended_heads, axis=-1)
    query_zero = jnp.zeros((KV_HEADS, group, row_count, HEAD_DIM), jnp.float32)
    back_start = (
        query_zero,
        jnp.zeros((length, KVW), jnp.float32),
        jnp.zeros((length, KVW), jnp.float32),
    )
    make_keys_piece = lax.all_gather(keys_mine, "ctx", axis=0, tiled=True)
    make_values_piece = lax.all_gather(values_mine, "ctx", axis=0, tiled=True)

    def make_one_block(block_index, running):
        key_block, value_block, k_start, allowed, needed = block_view(
            make_keys_piece, make_values_piece, block_index
        )

        def make_compute(current):
            scores = (
                jnp.einsum("tgrd,ngd->grtn", query, key_block, preferred_element_type=jnp.float32)
                * score_scale
            )
            probs = jnp.where(
                allowed,
                jnp.exp(jnp.where(allowed, scores, masked_score) - log_total[..., None]),
                0.0,
            )
            grad_probs = jnp.einsum(
                "tgrd,ngd->grtn", grad_heads, value_block, preferred_element_type=jnp.float32
            )
            grad_scores = (probs * (grad_probs - delta[..., None])).astype(jnp.bfloat16)
            grad_query, grad_keys, grad_values = current
            grad_query = grad_query + score_scale * jnp.einsum(
                "grtn,ngd->grtd", grad_scores, key_block, preferred_element_type=jnp.float32
            )
            key_part = score_scale * jnp.einsum(
                "grtn,tgrd->ngd", grad_scores, query, preferred_element_type=jnp.float32
            )
            value_part = jnp.einsum(
                "grtn,tgrd->ngd",
                probs.astype(jnp.bfloat16),
                grad_heads,
                preferred_element_type=jnp.float32,
            )
            old_keys = lax.dynamic_slice_in_dim(grad_keys, k_start, row_count)
            old_values = lax.dynamic_slice_in_dim(grad_values, k_start, row_count)
            grad_keys = lax.dynamic_update_slice_in_dim(
                grad_keys, old_keys + key_part.reshape(row_count, KVW), k_start, 0
            )
            grad_values = lax.dynamic_update_slice_in_dim(
                grad_values, old_values + value_part.reshape(row_count, KVW), k_start, 0
            )
            return (grad_query, grad_keys, grad_values)

        return lax.cond(needed, make_compute, lambda current: current, running)

    grad_query_acc, grad_keys_all, grad_values_all = lax.fori_loop(
        0, make_keys_piece.shape[0] // row_count, make_one_block, back_start
    )
    grad_keys_mine, grad_values_mine = (
        lax.psum_scatter(grad_keys_all, "ctx", scatter_dimension=0, tiled=True),
        lax.psum_scatter(grad_values_all, "ctx", scatter_dimension=0, tiled=True),
    )
    grad_q = grad_query_acc.transpose(2, 0, 1, 3).reshape(row_count, HEADS, HEAD_DIM)
    unused, query_back = jax.vjp(prepare, q_raw, head_gains[0])
    grad_q_raw, grad_qgain = query_back(grad_q)
    unused, key_back = jax.vjp(prepare, k_raw, head_gains[1])
    grad_k_raw, grad_kgain = key_back(grad_keys_mine.reshape(row_count, KV_HEADS, HEAD_DIM))
    grad_qkv = jnp.concatenate(
        [grad_q_raw.reshape(row_count, D), grad_k_raw.reshape(row_count, KVW), grad_values_mine],
        axis=1,
    ).astype(jnp.bfloat16)
    grad_qkv_weights = tokens_t(h_three, grad_qkv)
    grad_h_three = matmul_t(grad_qkv, attn_full[:, :qkv_width])
    unused, norm3_back = jax.vjp(rms_apply, x_two, vectors[2])
    grad_x_norm, grad_gain3 = norm3_back(grad_h_three)
    grad_two = grad_three + grad_x_norm
    grad_attn = reduce_grads(
        jnp.concatenate(
            [grad_qkv_weights, grad_attn_out, ffn_two_grads[0], ffn_two_grads[1]], axis=1
        )
    )
    grad_one, grad_gain2, ffn_one_grads = ffn_backward(
        x_one, vectors[1], conv_full, 4 * D, saved_one, grad_two
    )
    conv_in = grad_one.astype(jnp.bfloat16)
    grad_conv_out = tokens_t(conv_in, outer)
    grad_outer = matmul(conv_in, w_conv_out)
    grad_c = grad_outer * conv
    grad_z = grad_outer * gate_c
    grad_tap0 = jnp.sum(grad_z * mixed, axis=0)
    grad_tap1 = jnp.sum(grad_z * prev_one * mask_one, axis=0)
    grad_tap2 = jnp.sum(grad_z * prev_two * mask_two, axis=0)
    back_one = vectors[5] * grad_z * mask_one
    back_two = vectors[6] * grad_z * mask_two
    ext_grad = jnp.concatenate(
        [back_two, jnp.zeros((2, D), jnp.float32)], axis=0
    ) + jnp.concatenate(
        [jnp.zeros((1, D), jnp.float32), back_one, jnp.zeros((1, D), jnp.float32)], axis=0
    )
    rim_grad = from_behind(ext_grad[:2], "ctx", -1)
    grad_mixed = (
        vectors[4] * grad_z
        + ext_grad[2:]
        + jnp.concatenate([jnp.zeros((row_count - 2, D), jnp.float32), rim_grad], axis=0)
    )
    grad_proj = jnp.concatenate([grad_mixed * inner, grad_c, grad_mixed * gate_b], axis=1).astype(
        jnp.bfloat16
    )
    grad_in_weights = tokens_t(h_one, grad_proj)
    grad_h_one = matmul_t(grad_proj, w_in)
    unused, norm1_back = jax.vjp(rms_apply, x_zero, vectors[0])
    grad_x_zero, grad_gain1 = norm1_back(grad_h_one)
    grad_tokens = (grad_one + grad_x_zero)[None]
    grad_conv = reduce_grads(
        jnp.concatenate(
            [grad_in_weights, grad_conv_out, ffn_one_grads[0], ffn_one_grads[1]], axis=1
        )
    )
    vector_grads = jnp.stack(
        [grad_gain1, grad_gain2, grad_gain3, grad_gain4, grad_tap0, grad_tap1, grad_tap2]
    )
    gain_grads = jnp.stack([grad_qgain, grad_kgain])
    grad_vectors, grad_gains = lax.psum((vector_grads, gain_grads), ("dp", "ctx"))
    step_value = jnp.float32(STEP)
    new_master_conv, new_first_conv, new_second_conv = adam_update(
        master_conv, first_conv, second_conv, grad_conv, step_value
    )
    new_master_attn, new_first_attn, new_second_attn = adam_update(
        master_attn, first_attn, second_attn, grad_attn, step_value
    )
    new_conv_weights, new_attn_weights = (
        lax.all_gather(new_master_conv.astype(jnp.bfloat16), "dp", axis=1, tiled=True),
        lax.all_gather(new_master_attn.astype(jnp.bfloat16), "dp", axis=1, tiled=True),
    )
    return (
        out_tokens,
        grad_tokens,
        grad_conv,
        grad_attn,
        grad_vectors,
        grad_gains,
        new_master_conv,
        new_first_conv,
        new_second_conv,
        new_master_attn,
        new_first_attn,
        new_second_attn,
        new_conv_weights,
        new_attn_weights,
    )


def solution(mesh):
    placed = (
        P("dp", "ctx", None),
        P("dp", "ctx"),
        P("dp", "ctx", None),
        P("ctx", None),
        P("ctx", None),
        P(),
        P(),
        P("ctx", "dp"),
        P("ctx", "dp"),
        P("ctx", "dp"),
        P("ctx", "dp"),
        P("ctx", "dp"),
        P("ctx", "dp"),
    )
    return jax.shard_map(
        shards,
        mesh=mesh,
        in_specs=placed,
        out_specs=(
            P("dp", "ctx", None),
            P("dp", "ctx", None),
            P("ctx", "dp"),
            P("ctx", "dp"),
            P(),
            P(),
            P("ctx", "dp"),
            P("ctx", "dp"),
            P("ctx", "dp"),
            P("ctx", "dp"),
            P("ctx", "dp"),
            P("ctx", "dp"),
            P("ctx", None),
            P("ctx", None),
        ),
        check_vma=False,
    )
```

profile of v0, /device:TPU:10, one launch (start us, length us, event | category | flops | bytes accessed | tf_op | source)
XLA Modules:
  0.0 2360.2 jit_solution(15677862798900852372)
XLA Ops:
  8.8 18.7 all_gather.24
  29.0 164.7 %all-gather.7.cloned.1.call-done = bf16[1024,17920]{1,0:T(8,128)(2,1)} async-done(((bf16[64,17920]{1,0:T(8,128)(2,1)}), bf16[1024,17920]{1,0:T(8,128)(2,1)}) %all-gather.7.cloned.1.call-update) | async-done | bytes 36700176 | tf_op jit(solution)/shard_map/all_gather | solution.py:150
  227.3 141.1 %all-gather.9.cloned.1.call-done = bf16[1024,16896]{1,0:T(8,128)(2,1)} async-done(((bf16[64,16896]{1,0:T(8,128)(2,1)}), bf16[1024,16896]{1,0:T(8,128)(2,1)}) %all-gather.9.cloned.1.call-update) | async-done | bytes 34603024 | tf_op jit(solution)/shard_map/all_gather | solution.py:151
  380.8 32.6 %all-gather.11.cloned.1.call-done = bf16[2048,512]{1,0:T(8,128)(2,1)} async-done(((bf16[128,512]{1,0:T(8,128)(2,1)}), bf16[2048,512]{1,0:T(8,128)(2,1)}) %all-gather.11.cloned.1.call-update) | async-done | bytes 2097168 | tf_op jit(solution)/shard_map/all_gather | solution.py:205
  417.8 38.4 %all-gather.13.cloned.1.call-done = bf16[2048,512]{1,0:T(8,128)(2,1)} async-done(((bf16[128,512]{1,0:T(8,128)(2,1)}), bf16[2048,512]{1,0:T(8,128)(2,1)}) %all-gather.13.cloned.1.call-update) | async-done | bytes 2097168 | tf_op jit(solution)/shard_map/all_gather | solution.py:206
  460.2 33.0 %while.36 = (s32[]{:T(128)}, f32[8,2,128]{2,1,0:T(2,128)S(1)}, f32[8,2,128]{2,1,0:T(2,128)S(1)}, f32[8,2,128,64]{2,3,1,0:T(8,128)S(1)}, s32[]{:T(128)}, /*index=...) while((s32[]{:T(128)}, f32[8,2,128]{2,1,0:T(2,128)S(1)}, ...), condition=%wide.region_12.13_spmd.clone, body=%wide.region_7.12_spmd.clone.sunk | while | flops 69783816 | bytes 5446037 | solution.py:234
  508.2 11.9 multiply_reduce_fusion.4
  528.2 47.7 %while.37 = (s32[]{:T(128)}, f32[8,2,128,64]{2,3,1,0:T(8,128)S(1)}, f32[2048,512]{0,1:T(8,128)}, f32[2048,512]{0,1:T(8,128)}, s32[]{:T(128)}, /*index=5*/s32[204...) while((s32[]{:T(128)}, f32[8,2,128,64]{2,3,1,0:T(8,128)S(1)}, ...), condition=%wide.region_19.20_spmd.clone, body=%wide.region_16.19_spmd.clone.sunk | while | flops 170377488 | bytes 9886191 | solution.py:309
  589.2 14.9 fusion.72
  604.1 127.5 %reduce-scatter.7.cloned.1.call-done = f32[128,512]{0,1:T(8,128)} async-done(((f32[2048,512]{0,1:T(8,128)}), f32[128,512]{0,1:T(8,128)}) %reduce-scatter.7.cloned.1.call-update) | async-done | bytes 262160 | tf_op jit(solution)/shard_map/reduce_scatter | solution.py:313
  734.4 72.9 %reduce-scatter.9.cloned.1.call-done = f32[128,512]{0,1:T(8,128)} async-done(((f32[2048,512]{0,1:T(8,128)}), f32[128,512]{0,1:T(8,128)}) %reduce-scatter.9.cloned.1.call-update) | async-done | bytes 262160 | tf_op jit(solution)/shard_map/reduce_scatter | solution.py:314
  813.1 44.6 %pad_maximum_fusion.1 = f32[1024,16896]{1,0:T(8,128)} fusion(f32[1024,4608]{1,0:T(8,128)} %convolution_bitcast_fusion.2, f32[1024,9216]{1,0:T(8,128)} %fusion.72, f32[1024,1024]{1,0:T(8,128)} %fusion.125, f32[1024,2048]{1,0:T(8,128)} %fusion.117), kind=kLoop, calls=%fused_computation.46 | loop fusion | flops 51904512 | bytes 138412032 | tf_op jit(solution)/shard_map/concatenate | solution.py:331
  869.2 13.5 multiply_reduce_fusion.6
  891.6 11.2 fusion.122
  902.8 22.2 fusion.71
  926.1 8.7 fusion.113
  934.9 52.1 %pad_maximum_fusion = f32[1024,17920]{1,0:T(8,128)} fusion(f32[1024,4608]{1,0:T(8,128)} %fusion.122, f32[1024,9216]{1,0:T(8,128)} %fusion.71, f32[1024,1024]{1,0:T(8,128)} %fusion.119, f32[1024,3072]{1,0:T(8,128)} %fusion.113), kind=kLoop, calls=%fused_computation.45 | loop fusion | flops 55050240 | bytes 146800640 | tf_op jit(solution)/shard_map/concatenate | solution.py:368
  987.1 523.0 %reduce-scatter.15.cloned.1.call-done = f32[64,16896]{1,0:T(8,128)} async-done(((f32[1024,16896]{1,0:T(8,128)}), f32[64,16896]{1,0:T(8,128)}) %reduce-scatter.15.cloned.1.call-update) | async-done | bytes 4325392 | tf_op jit(solution)/shard_map/reduce_scatter | solution.py:100
  1513.9 688.5 %reduce-scatter.11.cloned.1.call-done = f32[64,17920]{1,0:T(8,128)} async-done(((f32[1024,17920]{1,0:T(8,128)}), f32[64,17920]{1,0:T(8,128)}) %reduce-scatter.11.cloned.1.call-update) | async-done | bytes 4587536 | tf_op jit(solution)/shard_map/reduce_scatter | solution.py:100
  2206.6 30.8 %reduce-scatter.17.cloned.1.call-done = bf16[64,8448]{1,0:T(8,128)(2,1)} async-done(((bf16[64,16896]{1,0:T(8,128)(2,1)}), bf16[64,8448]{1,0:T(8,128)(2,1)}) %reduce-scatter.17.cloned.1.call-update) | async-done | bytes 1081360 | tf_op jit(solution)/shard_map/reduce_scatter | solution.py:101
  2245.2 28.9 %reduce-scatter.13.cloned.1.call-done = bf16[64,8960]{1,0:T(8,128)(2,1)} async-done(((bf16[64,17920]{1,0:T(8,128)(2,1)}), bf16[64,8960]{1,0:T(8,128)(2,1)}) %reduce-scatter.13.cloned.1.call-update) | async-done | bytes 1146896 | tf_op jit(solution)/shard_map/reduce_scatter | solution.py:101
  2281.5 8.8 fusion.91
  2295.5 42.4 %all-reduce.7 = (f32[7,1024]{1,0:T(8,128)}, f32[2,64]{1,0:T(2,128)}) all-reduce(f32[7,1024]{1,0:T(8,128)S(1)} %stack.28, f32[2,64]{1,0:T(2,128)S(1)} %pad_maximum_fusion.17), channel_id=1, replica_groups=mesh['dp'=2,'ctx'=16] {'dp','ctx'}, use_global_device_ids=true, to_apply=%region_38.39 | all-reduce | flops 7296 | bytes 58368 | tf_op jit(solution)/shard_map/psum | solution.py:376
  2338.8 9.6 all-gather.15.cloned.1.call-done
  (556 shorter events, 254.0 us)
Async XLA Ops:
  7.2 186.5 %all-gather.7.cloned.1.call-start = ((), (), s32[]{:S(2)}) async-start(), calls=%async_computation.6 | async-start | bytes 38993920 | tf_op jit(solution)/shard_map/all_gather | solution.py:150
  8.0 360.4 %all-gather.9.cloned.1.call-start = ((), (), s32[]{:S(2)}) async-start(), calls=%async_computation.7 | async-start | bytes 36765696 | tf_op jit(solution)/shard_map/all_gather | solution.py:151
  8.7 404.7 %all-gather.11.cloned.1.call-start = ((), (), s32[]{:S(2)}) async-start(), calls=%async_computation.8 | async-start | bytes 2228224 | tf_op jit(solution)/shard_map/all_gather | solution.py:205
  28.5 175.1 %copy-start.54 = (f32[128]{0:T(128)}, f32[128]{0:T(128)S(1)}, u32[]{:S(2)}) copy-start(f32[128]{0:T(128)S(1)} %get-tuple-element.905) | copy-start | bytes 1540
  28.6 169.0 %copy-start.64 = (f32[128]{0:T(128)}, f32[128]{0:T(128)S(1)}, u32[]{:S(2)}) copy-start(f32[128]{0:T(128)S(1)} %fusion.105) | copy-start | bytes 1540
  28.7 174.8 %copy-start.52 = (f32[128]{0:T(128)}, f32[128]{0:T(128)S(1)}, u32[]{:S(2)}) copy-start(f32[128]{0:T(128)S(1)} %compare_convert_fusion) | copy-start | bytes 1540
  28.9 174.6 %copy-start.41 = (f32[1,1024]{1,0:T(1,128)}, f32[1,1024]{1,0:T(1,128)S(1)}, u32[]{:S(2)}) copy-start(f32[1,1024]{1,0:T(1,128)S(1)} %get-tuple-element.935) | copy-start | bytes 12292
  28.9 174.6 %copy-start.43 = (f32[1,1024]{1,0:T(1,128)}, f32[1,1024]{1,0:T(1,128)S(1)}, u32[]{:S(2)}) copy-start(f32[1,1024]{1,0:T(1,128)S(1)} %get-tuple-element.933) | copy-start | bytes 12292
  28.9 174.6 %copy-start.45 = (f32[1,1024]{1,0:T(1,128)}, f32[1,1024]{1,0:T(1,128)S(1)}, u32[]{:S(2)}) copy-start(f32[1,1024]{1,0:T(1,128)S(1)} %get-tuple-element.934) | copy-start | bytes 12292
  29.0 178.4 %copy-start.47 = (f32[1,1024]{1,0:T(1,128)}, f32[1,1024]{1,0:T(1,128)S(1)}, u32[]{:S(2)}) copy-start(f32[1,1024]{1,0:T(1,128)S(1)} %get-tuple-element.932) | copy-start | bytes 12292
  197.7 5.9 collective-permute-start
  227.3 266.0 %copy-start.6 = (f32[128,1024]{1,0:T(8,128)}, f32[128,1024]{1,0:T(8,128)S(1)}, u32[]{:S(2)}) copy-start(f32[128,1024]{1,0:T(8,128)S(1)} %get-tuple-element.947) | copy-start | bytes 1572868
  372.8 83.4 %all-gather.13.cloned.1.call-start = ((), (), s32[]{:S(2)}) async-start(), calls=%async_computation.9 | async-start | bytes 2228224 | tf_op jit(solution)/shard_map/all_gather | solution.py:206
  373.5 358.1 %reduce-scatter.7.cloned.1.call-start = ((), (), s32[]{:S(2)}) async-start(), calls=%async_computation.10 | async-start | bytes 4456448 | tf_op jit(solution)/shard_map/reduce_scatter | solution.py:313
  575.9 231.4 %reduce-scatter.9.cloned.1.call-start = ((), (), s32[]{:S(2)}) async-start(), calls=%async_computation.11 | async-start | bytes 4456448 | tf_op jit(solution)/shard_map/reduce_scatter | solution.py:314
  576.5 933.5 %reduce-scatter.15.cloned.1.call-start = ((), (), s32[]{:S(2)}) async-start(), calls=%async_computation.14 | async-start | bytes 73531392 | tf_op jit(solution)/shard_map/reduce_scatter | solution.py:100
  604.1 204.2 %copy-start.7 = (f32[128,1024]{1,0:T(8,128)S(1)}, f32[128,1024]{1,0:T(8,128)}, u32[]{:S(2)}) copy-start(f32[128,1024]{1,0:T(8,128)} %copy-done.6) | copy-start | bytes 1572868
  604.1 204.2 %copy-start.33 = (bf16[128,16,64]{0,2,1:T(8,128)(2,1)S(1)}, bf16[128,16,64]{0,2,1:T(8,128)(2,1)}, u32[]{:S(2)}) copy-start(bf16[128,16,64]{0,2,1:T(8,128)(2,1)} %fusion.100) | copy-start | bytes 786436
  857.6 1344.7 %reduce-scatter.11.cloned.1.call-start = ((), (), s32[]{:S(2)}) async-start(), calls=%async_computation.12 | async-start | bytes 77987840 | tf_op jit(solution)/shard_map/reduce_scatter | solution.py:100
  886.5 38.7 %collective-permute-start.1 = (f32[2,1024]{1,0:T(2,128)S(1)}, f32[2,1024]{1,0:T(2,128)S(1)}, u32[]{:S(2)}, u32[]{:S(2)}) collective-permute-start(f32[2,1024]{1,0:T(2,128)S(1)} %pad_add_fusion.1), channel_id=1, source_target_pairs={{1,0},{2,1},{3,2},{4,3},{5,4},{6,5},{7,6},{8,7},{9,8},{10,9},{11,1... | collective-permute-start | bytes 24584 | tf_op jit(solution)/shard_map/ppermute | solution.py:28
  987.0 1250.3 %reduce-scatter.17.cloned.1.call-start = ((), (), s32[]{:S(2)}) async-start(), calls=%async_computation.15 | async-start | bytes 3244032 | tf_op jit(solution)/shard_map/reduce_scatter | solution.py:101
  1513.8 760.2 %reduce-scatter.13.cloned.1.call-start = ((), (), s32[]{:S(2)}) async-start(), calls=%async_computation.13 | async-start | bytes 3440640 | tf_op jit(solution)/shard_map/reduce_scatter | solution.py:101
  2206.3 132.6 %all-gather.17.cloned.1.call-start = ((), (), s32[]{:S(2)}) async-start(), calls=%async_computation.17 | async-start | bytes 3244032 | tf_op jit(solution)/shard_map/all_gather | solution.py:386
  2245.1 103.2 %all-gather.15.cloned.1.call-start = ((), (), s32[]{:S(2)}) async-start(), calls=%async_computation.16 | async-start | bytes 3440640 | tf_op jit(solution)/shard_map/all_gather | solution.py:385
  (65 other events, 1019.9 us)
Sparse Core Ops, SparseCore 0:
  9.7 184.0 all-gather.6
  195.3 173.0 all-gather.8
  372.9 40.4 all-gather.10
  416.0 40.1 all-gather.12
  576.0 155.5 reduce-scatter.6
  735.8 71.4 reduce-scatter.8
  857.8 652.2 reduce-scatter.14
  1514.4 687.9 reduce-scatter.10
  2205.3 32.0 reduce-scatter.16
  2240.0 33.9 reduce-scatter.12
  2275.7 34.4 all-gather.16
  2312.2 36.1 all-gather.14
where the time goes:
time: 2370 us; the launch traced here: 2360 us
  waiting for transfers between devices  1860 us (78%)
  matrix products  193 us (8%)
  other arithmetic  143 us (6%)
  blocking collectives  61.1 us (3%)
  local copies, waits for them, and re-layouts  56.2 us (2%)
    reduce_scatter x2, waiting for transfers between devices, reduce_grads(): lax.psum_scatter(local_grad, 'ctx', scatter_dimension=0, tiled=True)  1210 us
    all_gather x1, waiting for transfers between devices, shards(): lax.all_gather(conv_weights, 'ctx', axis=0, tiled=True)  165 us
    all_gather x1, waiting for transfers between devices, shards(): lax.all_gather(attn_weights, 'ctx', axis=0, tiled=True)  141 us
    reduce_scatter x1, waiting for transfers between devices, shards(): lax.psum_scatter(grad_keys_all, 'ctx', scatter_dimension=0, tiled=True)  128 us
    dot_general x8, matrix products, tokens_t(): lax.dot_general(left, right, (((0,), (0,)), ((), ())), preferred_element_...  75.5 us
    reduce_scatter x1, waiting for transfers between devices, shards(): lax.psum_scatter(grad_values_all, 'ctx', scatter_dimension=0, tiled=True)  72.9 us
    reduce_scatter x2, waiting for transfers between devices, reduce_grads(): lax.psum_scatter(row_part.astype(jnp.bfloat16), 'dp', scatter_dimension=1...  59.6 us
    dot_general x8, matrix products, matmul_t(): lax.dot_general(left, right, (((1,), (1,)), ((), ())), preferred_element_...  54.9 us
  transfers between devices with their start and end apart: 14, of which 12 were waited for; matrix products, arithmetic and copies ran while one was open for 10% of the time, Pallas kernels for 0%

commit v1 on v0

v1 whole, which is shorter than its diff:
```python
import functools
import jax
import jax.numpy as jnp
from jax import lax
from jax.sharding import Mesh, PartitionSpec as P
import jax.experimental.pallas as pl
import jax.experimental.pallas.tpu as pltpu

D = 1024
FF = 4608
HEADS = 16
KV_HEADS = 8
HEAD_DIM = 64
STEP = 5
KVW = 512
T = 128
QF = FF // 4
QD = D // 4
CW = 4 * QD + 3 * QF
AW = 3 * QD + 3 * QF

norm_eps = 1e-05
rope_base = 1000000.0
learn_rate = 0.01
decay_rate = 0.1
beta_one = 0.9
beta_two = 0.95
adam_eps = 1e-08

MESH = pl.DeviceIdType.MESH
BF = jnp.bfloat16
F32 = jnp.float32
PLANE = ((1, 1), (1, 0), (0, 1))

CONV_PARTS = (
    (0, QD, 0, 0),
    (D, QD, QD, 0),
    (2 * D, QD, 2 * QD, 0),
    (3 * D, QD, 3 * QD, 1),
    (4 * D, QF, 4 * QD, 2),
    (4 * D + FF, QF, 4 * QD + QF, 3),
    (4 * D + 2 * FF, QF, 4 * QD + 2 * QF, 4),
)
ATTN_PARTS = (
    (0, QD, 0, 0),
    (D, KVW // 4, QD, 0),
    (D + KVW, KVW // 4, QD + KVW // 4, 0),
    (2 * D, QD, 2 * QD, 1),
    (3 * D, QF, 3 * QD, 2),
    (3 * D + FF, QF, 3 * QD + QF, 3),
    (3 * D + 2 * FF, QF, 3 * QD + 2 * QF, 4),
)
CONV_SPANS = ((0, 768), (768, 256), (1024, QF), (1024 + QF, QF), (1024 + 2 * QF, QF))
ATTN_SPANS = ((0, 512), (512, 256), (768, QF), (768 + QF, QF), (768 + 2 * QF, QF))


def nn(a, b):
    return jnp.dot(a, b, preferred_element_type=F32)


def nt(a, b):
    return lax.dot_general(a, b, (((1,), (1,)), ((), ())), preferred_element_type=F32)


def tn(a, b):
    return lax.dot_general(a, b, (((0,), (0,)), ((), ())), preferred_element_type=F32)


def rms_scale(v):
    return lax.rsqrt(jnp.mean(v * v, axis=-1, keepdims=True) + norm_eps)


class Place:
    def __init__(self, O):
        self.O = O
        self.x, self.z = lax.axis_index("dp"), lax.axis_index("z")
        self.y, self.c = lax.axis_index("y"), lax.axis_index("c")
        self.r = self.x * 2 + self.y

    def at(self, dx=0, dz=0, dy=0, dc=0):
        out = {}
        if not (isinstance(dx, int) and dx == 0):
            out["dp"] = lax.rem(self.x + dx, 2)
        if not (isinstance(dz, int) and dz == 0):
            out["z"] = lax.rem(self.z + dz, self.O)
        if not (isinstance(dy, int) and dy == 0):
            out["y"] = lax.rem(self.y + dy, 2)
        if not (isinstance(dc, int) and dc == 0):
            out["c"] = lax.rem(self.c + dc, 2)
        return out

    def block(self, dx, dy):
        return lax.rem(self.x + dx, 2) * 2 + lax.rem(self.y + dy, 2)


def greet(here):
    O = here.O
    barrier = pltpu.get_barrier_semaphore()

    def hello(**k):
        pl.semaphore_signal(barrier, inc=1, device_id=here.at(**k), device_id_type=MESH)

    hello(dx=1, dy=1)
    hello(dx=1)
    hello(dy=1)
    hello(dc=1)
    hello(dz=1, dc=1)
    hello(dz=O - 1, dc=1)

    def along(dz, carry):
        for dy in (0, 1):
            hello(dz=dz, dy=dy)
        return carry

    lax.fori_loop(1, O, along, 0)
    pl.semaphore_wait(barrier, 6 + 2 * (O - 1))


def remote(src, dst, ss, rs, dev):
    return pltpu.make_async_remote_copy(
        src_ref=src, dst_ref=dst, send_sem=ss, recv_sem=rs, device_id=dev, device_id_type=MESH
    )


def gather_block(here, H, ss, rs):
    out = []
    for k, (dx, dy) in enumerate(PLANE):
        cp = remote(H.at[here.r], H.at[here.r], ss.at[k], rs.at[k], here.at(dx=dx, dy=dy))
        cp.start()
        out.append(cp)
    return out


def wait_all(copies):
    for cp in copies:
        cp.wait()


def scatter_sums(here, tile_fn, part, own, S, R, ss, rs):
    out = []
    for n in (0, 1):
        part[...] = tile_fn(n).reshape(4, T, D // 2)
        for k, (dx, dy) in enumerate(PLANE):
            S[n, k] = part[here.block(dx, dy)].astype(BF)
            cp = remote(S.at[n, k], R.at[n, k], ss.at[n, k], rs.at[n, k], here.at(dx=dx, dy=dy))
            cp.start()
            out.append(cp)
        own[:, n * (D // 2) : (n + 1) * (D // 2)] = part[here.r]
    return out


def sum_blocks(own, R):
    halves = []
    for n in (0, 1):
        t = own[:, n * (D // 2) : (n + 1) * (D // 2)]
        for k in range(3):
            t = t + R[n, k].astype(F32)
        halves.append(t)
    return jnp.concatenate(halves, axis=1)


class Weights:
    def __init__(self, here, hbm, W, parts, spans, ls, ss, rs, cs, cr):
        self.here, self.hbm, self.W = here, hbm, W
        self.parts, self.spans = parts, spans
        self.ls, self.ss, self.rs, self.cs, self.cr = ls, ss, rs, cs, cr

    def source(self, part, dy):
        base, width, _, _ = part
        chip = self.here.x * 2 + lax.rem(self.here.y + dy, 2)
        return self.hbm.at[:, pl.ds(pl.multiple_of(base + chip * width, 128), width)]

    def target(self, part):
        _, width, place, _ = part
        h = self.here
        return self.W.at[h.z * 2 + h.y, h.c, :, pl.ds(place, width)]

    def start(self):
        h = self.here
        for part in self.parts:
            g = part[3]
            pltpu.make_async_copy(self.source(part, 0), self.target(part), self.ls.at[g]).start()
        for part in self.parts:
            g = part[3]
            remote(self.source(part, 1), self.target(part), self.ss.at[g], self.rs.at[g], h.at(dy=1)).start()

            def along(dz, carry):
                for dy in (0, 1):
                    remote(
                        self.source(part, dy), self.target(part), self.ss.at[g], self.rs.at[g], h.at(dz=dz, dy=dy)
                    ).start()
                return carry

            lax.fori_loop(1, h.O, along, 0)

    def bytes_of(self, g, shards):
        place, width = self.spans[g]
        return self.W.at[pl.ds(0, shards), 0, :, pl.ds(place, width)]

    def arrive(self, g):
        h = self.here
        place, width = self.spans[g]
        one = self.bytes_of(g, 1)
        pltpu.make_async_copy(one, one, self.ls.at[g]).wait()
        rest = self.bytes_of(g, 2 * h.O - 1)
        pltpu.make_async_copy(rest, rest, self.rs.at[g]).wait()
        mine = self.W.at[:, h.c, :, pl.ds(place, width)]
        cp = remote(mine, mine, self.cs.at[g], self.cr.at[g], h.at(dc=1))
        cp.start()
        cp.wait()

    def finish(self):
        for g in range(5):
            rest = self.bytes_of(g, 2 * self.here.O - 1)
            pltpu.make_async_copy(rest, rest, self.ss.at[g]).wait()


def cols(W, place, width):
    v = W[:, :, :, pl.ds(place, width)]
    return v.reshape(D, width)


def rows_of(W, n, place, width):
    h = W.shape[0] // 2
    v = W[n * h : (n + 1) * h, :, :, pl.ds(place, width)]
    return v.reshape(D // 2, width)


def lane_low(shape):
    return lax.broadcasted_iota(jnp.int32, shape, len(shape) - 1) < 64


def lane_first(shape):
    return lax.rem(lax.broadcasted_iota(jnp.int32, shape, len(shape) - 1), 64) < 32


def head_mean(v):
    low = lane_low(v.shape)
    a = jnp.sum(jnp.where(low, v, 0.0), axis=-1, keepdims=True)
    b = jnp.sum(jnp.where(low, 0.0, v), axis=-1, keepdims=True)
    return jnp.where(low, a, b) * (1.0 / HEAD_DIM)


def turn(v):
    return jnp.where(lane_first(v.shape), pltpu.roll(v, 96, 1), pltpu.roll(v, 32, 1))


def to_pairs(left, right):
    low = lane_low(left.shape)
    a = jnp.where(low, left, pltpu.roll(right, 64, 1))
    b = jnp.where(low, pltpu.roll(left, 64, 1), right)
    return a, b


def stacked(a, b):
    low = lane_low(a.shape)
    zero = jnp.zeros_like(a)
    return (jnp.where(low, a, zero), jnp.where(low, b, zero), jnp.where(low, zero, a), jnp.where(low, zero, b))


def ffn_forward_tile(H, W, gate_at, up_at, gu, u, n):
    w = QF // 3
    h = H[...].reshape(4 * T, D)
    at = pl.multiple_of(n * w, 128)
    gate = nn(h, cols(W, gate_at + at, w))
    up = nn(h, cols(W, up_at + at, w))
    gu[0, :, pl.ds(at, w)] = gate
    gu[1, :, pl.ds(at, w)] = up
    u[:, pl.ds(at, w)] = (gate / (1.0 + jnp.exp(-gate)) * up).astype(BF)


def taps(here, vec):
    at = pl.ds(pl.multiple_of(here.r * QD, 128), QD)
    return tuple(vec[4 + i : 5 + i, at] for i in range(3))


def behind(here, b, mine, from_c, from_z, start):
    z, c, yb = here.z, here.c, b % 2
    if yb:
        before = jnp.where(c == 1, from_c[2 * b : 2 * b + 2], from_c[2 * b - 2 : 2 * b])
    else:
        before = jnp.where(c == 1, from_c[2 * b : 2 * b + 2], from_z[2 * b + 2 : 2 * b + 4])
    row = lax.broadcasted_iota(jnp.int32, (T, QD), 0)
    one = jnp.where(row == 0, before[1:2], pltpu.roll(mine, 1, 0))
    two = jnp.where(row == 0, before[0:1], jnp.where(row == 1, before[1:2], pltpu.roll(mine, 2, 0)))
    t = z * 512 + yb * 256 + c * T + lax.broadcasted_iota(jnp.int32, (T, 1), 0)
    pos = t - start[b * T : (b + 1) * T, 0:1]
    return one, two, jnp.where(pos >= 1, 1.0, 0.0), jnp.where(pos >= 2, 1.0, 0.0)


def forward_kernel(
    O, tok, vec, hg, cosb, sinb, start, wc_hbm, wa_hbm,
    out_tok, x1, x2, x3, h1, h2, h3, h4, bcx, cz, gu1, gu2, qkr, kv, oab, lse, wc, wa, Q, tail_c, tail_z,
    u, part, own, S, R, tails, acc,
    ags, agr, rss, rsr, hs, hr, kvs, kvr, wls, wss, wrs, wcs, wcr,
):
    here = Place(O)
    x, y, z, c, r = here.x, here.y, here.z, here.c, here.r
    greet(here)
    conv = Weights(here, wc_hbm, wc, CONV_PARTS, CONV_SPANS, wls.at[0], wss.at[0], wrs.at[0], wcs.at[0], wcr.at[0])
    attn = Weights(here, wa_hbm, wa, ATTN_PARTS, ATTN_SPANS, wls.at[1], wss.at[1], wrs.at[1], wcs.at[1], wcr.at[1])
    conv.start()

    x0 = tok[...].astype(F32)
    h1[r] = (x0 * rms_scale(x0) * vec[0:1, :]).astype(BF)
    copies = gather_block(here, h1, ags.at[0], agr.at[0])
    attn.start()
    conv.arrive(0)
    wait_all(copies)

    h = h1[...].reshape(4 * T, D)
    for i in range(3):
        bcx[i] = nn(h, cols(wc, i * QD, QD))
    bx = bcx[0] * bcx[2]
    for b in range(4):
        tails[2 * b : 2 * b + 2, :] = bx[b * T + T - 2 : b * T + T, :]
    over = remote(tails, tail_c, hs.at[0], hr.at[0], here.at(dc=1))
    over.start()
    ahead = remote(tails, tail_z, hs.at[1], hr.at[1], here.at(dz=1, dc=1))

    @pl.when((c == 1) & (z < O - 1))
    def _():
        ahead.start()

    over.wait()

    @pl.when((c == 0) & (z > 0))
    def _():
        ahead.wait_recv()

    @pl.when((c == 1) & (z < O - 1))
    def _():
        ahead.wait_send()

    tap0, tap1, tap2 = taps(here, vec)
    from_c, from_z = tail_c[...], jnp.where(z > 0, tail_z[...], 0.0)
    for b in range(4):
        mine = bx[b * T : (b + 1) * T, :]
        one, two, m1, m2 = behind(here, b, mine, from_c, from_z, start)
        cz[b * T : (b + 1) * T, :] = tap0 * mine + tap1 * one * m1 + tap2 * two * m2
    yc = (bcx[1] * cz[...]).astype(BF)
    conv.arrive(1)
    copies = scatter_sums(
        here, lambda n: nt(yc, rows_of(wc, n, 3 * QD, QD)), part, own, S.at[0], R.at[0], rss.at[0], rsr.at[0]
    )
    wait_all(copies)
    xn = tok[...].astype(F32) + sum_blocks(own, R.at[0])
    x1[...] = xn
    h2[r] = (xn * rms_scale(xn) * vec[1:2, :]).astype(BF)
    copies = gather_block(here, h2, ags.at[1], agr.at[1])
    conv.arrive(2)
    conv.arrive(3)
    wait_all(copies)

    def ffn1(n, carry):
        ffn_forward_tile(h2, wc, 4 * QD, 4 * QD + QF, gu1, u, n)
        return carry

    lax.fori_loop(0, 3, ffn1, 0)
    conv.arrive(4)
    copies = scatter_sums(
        here, lambda n: nt(u[...], rows_of(wc, n, 4 * QD + 2 * QF, QF)), part, own, S.at[1], R.at[1], rss.at[1], rsr.at[1]
    )
    wait_all(copies)
    xn = x1[...] + sum_blocks(own, R.at[1])
    x2[...] = xn
    h3[r] = (xn * rms_scale(xn) * vec[2:3, :]).astype(BF)
    copies = gather_block(here, h3, ags.at[2], agr.at[2])
    attn.arrive(0)
    wait_all(copies)

    qkv = nn(h3[...].reshape(4 * T, D), cols(wa, 0, 512))
    qa, qb = to_pairs(qkv[:, 0:128], qkv[:, 128:256])
    raw = (qa, qb, qkv[:, 256:384])
    turned = []
    for i in range(3):
        qkr[i] = raw[i]
        gain = hg[0:1, :] if i < 2 else hg[1:2, :]
        w = raw[i] * lax.rsqrt(head_mean(raw[i] * raw[i]) + norm_eps) * gain
        turned.append(w * cosb[...] + turn(w) * sinb[...])
    keys = turned[2].astype(BF)
    values = qkv[:, 384:512].astype(BF)
    for b in range(4):
        kv[z, b, c, :, 0:128] = keys[b * T : (b + 1) * T]
        kv[z, b, c, :, 128:256] = values[b * T : (b + 1) * T]
    mine = kv.at[z, :, c]

    def send_up(dz, carry):
        @pl.when(z + dz < O)
        def _():
            remote(mine, mine, kvs.at[dz], kvr.at[dz], here.at(dz=dz)).start()

        return carry

    lax.fori_loop(1, O, send_up, 0)
    pair0 = remote(mine, mine, kvs.at[0], kvr.at[0], here.at(dc=1))
    pair0.start()
    for s in (0, 1):
        low4 = stacked(*(
            (turned[i][s * 256 : (s + 1) * 256] * (HEAD_DIM ** -0.5)).astype(BF) for i in (0, 1)
        ))
        for g in range(4):
            Q[s, g] = low4[g]

    def pass_on(dz, carry):
        @pl.when(z - dz >= 0)
        def _():
            got = kv.at[z - dz, :, c]
            remote(mine, mine, kvs.at[dz], kvr.at[dz], here.at(dz=dz)).wait_recv()
            remote(got, got, kvs.at[O + dz], kvr.at[O + dz], here.at(dc=1)).start()

        return carry

    lax.fori_loop(1, O, pass_on, 0)
    pair0.wait()

    def pass_wait(dz, carry):
        @pl.when(z - dz >= 0)
        def _():
            got = kv.at[z - dz, :, c]
            remote(got, got, kvs.at[O + dz], kvr.at[O + dz], here.at(dc=1)).wait()

        @pl.when(z + dz < O)
        def _():
            remote(mine, mine, kvs.at[dz], kvr.at[dz], here.at(dz=dz)).wait_send()

        return carry

    lax.fori_loop(1, O, pass_wait, 0)

    low = lane_low((256, 128))
    for s in (0, 1):
        acc[...] = jnp.zeros_like(acc)
        first_of = start[s * 256 : (s + 1) * 256, 0:1]
        row = lax.broadcasted_iota(jnp.int32, (256, 1), 0)
        t = z * 512 + lax.div(row, T) * 256 + c * T + lax.rem(row, T)

        def chunk(j, carry):
            block = kv[lax.div(j, 2), 2 * s + lax.rem(j, 2)].reshape(256, 256)
            k, v = block[:, 0:128], block[:, 128:256]
            one = jnp.ones_like(v)
            v_low = jnp.where(low, v, one)
            v_high = jnp.where(low, one, v)
            at = j * 256 + lax.broadcasted_iota(jnp.int32, (256, 256), 1)
            allowed = (at >= first_of) & (at <= t)
            for g in range(4):
                sc = nt(Q[s, g], k)
                p = jnp.where(allowed, jnp.exp(sc), 0.0).astype(BF)
                acc[g] += nn(p, v_low if g < 2 else v_high)
            return carry

        lax.fori_loop(0, 2 * z + 2, chunk, 0)
        heads = []
        for g in range(4):
            a = acc[g]
            other = pltpu.roll(a, 64, 1)
            heads.append(a / other)
            total = jnp.where(low, other, a) if g < 2 else jnp.where(low, a, other)
            lse[s, :, g * 256 : (g + 1) * 256] = jnp.transpose(jnp.log(total))[0:8, :]
        oab[0, s * 256 : (s + 1) * 256, :] = jnp.where(low, heads[0], heads[2])
        oab[1, s * 256 : (s + 1) * 256, :] = jnp.where(low, heads[1], heads[3])
    left, right = to_pairs(oab[0], oab[1])
    ao = jnp.concatenate([left, right], axis=1).astype(BF)
    attn.arrive(1)
    copies = scatter_sums(
        here, lambda n: nt(ao, rows_of(wa, n, 2 * QD, QD)), part, own, S.at[0], R.at[0], rss.at[2], rsr.at[2]
    )
    wait_all(copies)
    xn = x2[...] + sum_blocks(own, R.at[0])
    x3[...] = xn
    h4[r] = (xn * rms_scale(xn) * vec[3:4, :]).astype(BF)
    copies = gather_block(here, h4, ags.at[3], agr.at[3])
    attn.arrive(2)
    attn.arrive(3)
    wait_all(copies)

    def ffn2(n, carry):
        ffn_forward_tile(h4, wa, 3 * QD, 3 * QD + QF, gu2, u, n)
        return carry

    lax.fori_loop(0, 3, ffn2, 0)
    attn.arrive(4)
    copies = scatter_sums(
        here, lambda n: nt(u[...], rows_of(wa, n, 3 * QD + 2 * QF, QF)), part, own, S.at[1], R.at[1], rss.at[3], rsr.at[3]
    )
    wait_all(copies)
    out_tok[...] = (x3[...] + sum_blocks(own, R.at[1])).astype(BF)
    conv.finish()
    attn.finish()


def any_spec():
    return pl.BlockSpec(memory_space=pl.ANY)


def vmem():
    return pl.BlockSpec(memory_space=pltpu.VMEM)


def forward(O, tok, vec, hg, cosb, sinb, start, wc_hbm, wa_hbm):
    sds = jax.ShapeDtypeStruct
    G = 4 * T
    outs = (
        sds((T, D), BF),
        *(sds((T, D), F32) for _ in range(3)),
        *(sds((4, T, D), BF) for _ in range(4)),
        sds((3, G, QD), F32), sds((G, QD), F32),
        sds((2, G, QF), F32), sds((2, G, QF), F32),
        sds((3, G, 128), F32), sds((O, 4, 2, T, 256), BF), sds((2, G, 128), F32), sds((2, 8, 2 * G), F32),
        sds((2 * O, 2, D // (4 * O), CW), BF), sds((2 * O, 2, D // (4 * O), AW), BF),
        sds((2, 4, 256, 128), BF), sds((8, QD), F32), sds((8, QD), F32),
    )
    dma = pltpu.SemaphoreType.DMA
    return pl.pallas_call(
        functools.partial(forward_kernel, O),
        out_shape=outs,
        in_specs=[vmem()] * 6 + [any_spec()] * 2,
        out_specs=tuple(vmem() for _ in outs),
        scratch_shapes=[
            pltpu.VMEM((G, QF), BF), pltpu.VMEM((4, T, D // 2), F32), pltpu.VMEM((T, D), F32),
            pltpu.VMEM((2, 2, 3, T, D // 2), BF), pltpu.VMEM((2, 2, 3, T, D // 2), BF),
            pltpu.VMEM((8, QD), F32), pltpu.VMEM((4, 256, 128), F32),
            dma((4, 3)), dma((4, 3)), dma((4, 2, 3)), dma((4, 2, 3)), dma((2,)), dma((2,)),
            dma((2 * O,)), dma((2 * O,)),
            dma((2, 5)), dma((2, 5)), dma((2, 5)), dma((2, 5)), dma((2, 5)),
        ],
        compiler_params=pltpu.CompilerParams(
            collective_id=1, has_side_effects=True, vmem_limit_bytes=61 * 2**20
        ),
        cost_estimate=pl.CostEstimate(flops=10**10, bytes_accessed=6 * 10**7, transcendentals=10**7),
        name="forward",
    )(tok, vec, hg, cosb, sinb, start, wc_hbm, wa_hbm)


def tables(O, segments):
    seg = lax.all_gather(segments, ("dp", "z", "y", "c"), axis=0, tiled=True).reshape(2, O * 512)
    n0 = jnp.sum((seg < 1).astype(jnp.int32), axis=1)
    n1 = jnp.sum((seg < 2).astype(jnp.int32), axis=1)
    z, c = lax.axis_index("z"), lax.axis_index("c")
    own = lax.dynamic_slice(
        seg.reshape(2, O, 2, 2, T), (0, z, 0, c, 0), (2, 1, 2, 1, T)
    ).reshape(2, 2, T)
    first = jnp.where(own == 0, 0, jnp.where(own == 1, n0[:, None, None], n1[:, None, None]))
    t = z * 512 + c * T + jnp.arange(2, dtype=jnp.int32)[None, :, None] * 256 + jnp.arange(T, dtype=jnp.int32)[None, None]
    pos = (t - first).reshape(4 * T)
    inverse_freq = rope_base ** (-(jnp.arange(HEAD_DIM // 2, dtype=F32) * 2.0) / HEAD_DIM)
    angles = pos.astype(F32)[:, None] * inverse_freq[None, :]
    cosines, sines = jnp.cos(angles), jnp.sin(angles)
    cosb = jnp.concatenate([cosines] * 4, axis=1)
    sinb = jnp.concatenate([-sines, sines] * 2, axis=1)
    return cosb, sinb, jnp.broadcast_to(first.reshape(4 * T, 1), (4 * T, 128))


def rms_back(x, gain, dh):
    r = rms_scale(x)
    inner = jnp.mean(x * gain * dh, axis=-1, keepdims=True)
    return r * gain * dh - x * (r * r * r) * inner, jnp.sum(dh * x * r, axis=0, keepdims=True)


class Keep:
    def __init__(self, stage, sem):
        self.stage, self.sem, self.flying = stage, sem, [None, None]
        self.turn = 0

    def put(self, left, right, out, place, width, step=384):
        i = self.turn
        self.turn = 1 - i
        if self.flying[i] is not None:
            self.flying[i].wait()
        step = min(step, width)
        stage = self.stage.at[i]
        shape = (*self.stage.shape[1:4], step)

        def body(n, carry):
            at = pl.multiple_of(n * step, 128)
            stage[:, :, :, pl.ds(at, step)] = nn(left[...], right(at, step)).astype(BF).reshape(shape)
            return carry

        lax.fori_loop(0, width // step, body, 0)
        cp = pltpu.make_async_copy(
            stage.at[:, :, :, pl.ds(0, width)], out.at[:, :, :, pl.ds(place, width)], self.sem.at[i]
        )
        cp.start()
        self.flying[i] = cp

    def finish(self):
        for cp in self.flying:
            if cp is not None:
                cp.wait()


def ffn_back_tile(DF, W, down_at, gu, dg, du, mx, n):
    w = QF // 3
    at = pl.multiple_of(n * w, 128)
    d = nn(DF[...].reshape(4 * T, D), cols(W, down_at + at, w))
    gate, up = gu[0, :, pl.ds(at, w)], gu[1, :, pl.ds(at, w)]
    sig = 1.0 / (1.0 + jnp.exp(-gate))
    silu = gate * sig
    dg[:, pl.ds(at, w)] = (d * up * (sig * (1.0 + gate * (1.0 - sig)))).astype(BF)
    du[:, pl.ds(at, w)] = (d * silu).astype(BF)
    mx[:, pl.ds(at, w)] = (silu * up).astype(BF)


def backward_kernel(
    O, cot, tok, vec, hg, cosb, sinb, start, start_row, x1, x2, x3, h1, h2, h3, h4, bcx, cz, gu1, gu2, qkr, kv, oab,
    lse, wc, wa, Q, tail_c, tail_z,
    dtok, vg, dwc, dwa,
    W, gu, DG, HH, dg, du, mx, LT, stage, part, own, S, R, dO, delta, dq, dqab, dkv, dkc, dkz, dkk, heads, head_c, head_z, dprev,
    ags, agr, rss, rsr, hs, hr, kvs, kvr, wls, gls, sts, hls,
):
    here = Place(O)
    x, y, z, c, r = here.x, here.y, here.z, here.c, here.r
    loads = [pltpu.make_async_copy(h, HH, hls.at[i]) for i, h in enumerate((h4, h3, h2, h1))]
    loads[0].start()

    def transposed(i):
        loads[i].wait()
        LT[...] = jnp.transpose(flat(HH))
        if i < 3:
            loads[i + 1].start()

    load_w = pltpu.make_async_copy(wa, W.at[:, :, :, pl.ds(0, AW)], wls.at[0])
    load_w.start()
    load_g = pltpu.make_async_copy(gu2, gu, gls.at[0])
    load_g.start()
    load_kv = pltpu.make_async_copy(kv, dkv, gls.at[2])
    load_kv.start()
    greet(here)
    keep = Keep(stage, sts)
    vg[...] = jnp.zeros_like(vg)

    DF = DG.at[0]
    DF[r] = cot[...]
    copies = gather_block(here, DF, ags.at[0], agr.at[0])
    load_w.wait()
    load_g.wait()
    wait_all(copies)

    def flat(H):
        return H[...].reshape(4 * T, D)

    def ffn_back(i, DF, at, x_in, gain_row, out, dy):
        def tile(n, carry):
            ffn_back_tile(DF, W, at + 2 * QF, gu, dg, du, mx, n)
            return carry

        lax.fori_loop(0, 3, tile, 0)
        copies = scatter_sums(
            here,
            lambda n: nt(dg[...], rows_of(W, n, at, QF)) + nt(du[...], rows_of(W, n, at + QF, QF)),
            part, own, S.at[i % 2], R.at[i % 2], rss.at[i], rsr.at[i],
        )
        LT[...] = jnp.transpose(flat(DF))
        keep.put(LT, lambda a, w: mx[:, pl.ds(a, w)], out, at + 2 * QF, QF)
        wait_all(copies)
        dx, dgain = rms_back(x_in[...], vec[gain_row : gain_row + 1, :], sum_blocks(own, R.at[i % 2]))
        vg[gain_row : gain_row + 1, :] = dgain
        dprev[...] = dy + dx
        H2 = DG.at[i + 1]
        H2[r] = dprev[...].astype(BF)
        copies = gather_block(here, H2, ags.at[i + 1], agr.at[i + 1])
        transposed(i)
        keep.put(LT, lambda a, w: dg[:, pl.ds(a, w)], out, at, QF)
        keep.put(LT, lambda a, w: du[:, pl.ds(a, w)], out, at + QF, QF)
        wait_all(copies)

    ffn_back(0, DF, 3 * QD, x3, 3, dwa, cot[...].astype(F32))
    load_g = pltpu.make_async_copy(gu1, gu, gls.at[1])
    load_g.start()

    DA = DG.at[1]
    d_out = nn(flat(DA), cols(W, 2 * QD, QD)).astype(BF).astype(F32)
    left, right = to_pairs(oab[0], oab[1])
    ao = jnp.concatenate([left, right], axis=1).astype(BF)
    mx[:, 0:QD] = ao
    LT[...] = jnp.transpose(flat(DA))
    keep.put(LT, lambda a, w: mx[:, pl.ds(a, w)], dwa, 2 * QD, QD, QD)
    da, db = to_pairs(d_out[:, 0:128], d_out[:, 128:256])
    for s in (0, 1):
        rows = slice(s * 256, (s + 1) * 256)
        four = stacked(da[rows], db[rows])
        o_of = (oab[0, rows, :], oab[1, rows, :])
        for g in range(4):
            dO[s, g] = four[g].astype(BF)
            dl = jnp.sum(four[g] * o_of[g % 2], axis=-1, keepdims=True)
            delta[s, :, g * 256 : (g + 1) * 256] = jnp.transpose(jnp.broadcast_to(dl, (256, 128)))[0:8, :]
    load_kv.wait()
    low = lane_low((256, 128))
    for s in (0, 1):
        dq[...] = jnp.zeros_like(dq)
        first_of = start_row[0:1, s * 256 : (s + 1) * 256]
        col = lax.broadcasted_iota(jnp.int32, (1, 256), 1)
        t = z * 512 + lax.div(col, T) * 256 + c * T + lax.rem(col, T)

        def chunk(j, carry):
            block = dkv[lax.div(j, 2), 2 * s + lax.rem(j, 2)].reshape(256, 256)
            k, v = block[:, 0:128], block[:, 128:256]
            at = j * 256 + lax.broadcasted_iota(jnp.int32, (256, 256), 0)
            allowed = (at >= first_of) & (at <= t)
            dk = jnp.zeros((256, 128), F32)
            dv = jnp.zeros((256, 128), F32)
            for g in range(4):
                span = slice(g * 256, (g + 1) * 256)
                p = jnp.where(allowed, jnp.exp(nt(k, Q[s, g]) - lse[s, 0:1, span]), 0.0)
                ds = (p * (nt(v, dO[s, g]) - delta[s, 0:1, span])).astype(BF)
                dv = dv + nn(p.astype(BF), dO[s, g])
                dk = dk + nn(ds, Q[s, g])
                dq[g] += tn(ds, k)
            dkv[lax.div(j, 2), 2 * s + lax.rem(j, 2)] = (
                jnp.concatenate([dk, dv], axis=1).astype(BF).reshape(2, T, 256)
            )
            return carry

        lax.fori_loop(0, 2 * z + 2, chunk, 0)
        rows = slice(s * 256, (s + 1) * 256)
        dqab[0, rows, :] = jnp.where(low, dq[0], dq[2]) * (HEAD_DIM ** -0.5)
        dqab[1, rows, :] = jnp.where(low, dq[1], dq[3]) * (HEAD_DIM ** -0.5)

    over = remote(dkv.at[:, :, 1 - c], dkc, kvs.at[0], kvr.at[0], here.at(dc=1))
    over.start()
    over.wait()

    def send_down(zz, carry):
        dkv[zz, :, c] = (dkv[zz, :, c].astype(F32) + dkc[zz].astype(F32)).astype(BF)
        d = z - zz
        remote(dkv.at[zz, :, c], dkz.at[z], kvs.at[d], kvr.at[d], here.at(dz=O - d)).start()
        return carry

    lax.fori_loop(0, z, send_down, 0)
    dkk[...] = (dkv[z, :, c].astype(F32) + dkc[z].astype(F32)).reshape(4 * T, 256)

    def take(d, carry):
        @pl.when(z + d < O)
        def _():
            remote(dkv.at[z, :, c], dkz.at[z + d], kvs.at[d], kvr.at[d], here.at(dz=O - d)).wait_recv()
            dkk[...] += dkz[z + d].astype(F32).reshape(4 * T, 256)

        return carry

    lax.fori_loop(1, O, take, 0)

    def sent(zz, carry):
        d = z - zz
        remote(dkv.at[zz, :, c], dkz.at[z], kvs.at[d], kvr.at[d], here.at(dz=O - d)).wait_send()
        return carry

    lax.fori_loop(0, z, sent, 0)

    for i in range(3):
        up = dqab[i] if i < 2 else dkk[:, 0:128]
        raw = qkr[i]
        gain = hg[0:1, :] if i < 2 else hg[1:2, :]
        dw = up * cosb[...] + turn(up * sinb[...])
        rr = lax.rsqrt(head_mean(raw * raw) + norm_eps)
        dgain = jnp.sum(dw * raw * rr, axis=0, keepdims=True)
        row = 8 if i < 2 else 9
        vg[row : row + 1, 0:128] += dgain
        draw = rr * gain * dw - raw * (rr * rr * rr) * head_mean(raw * gain * dw)
        if i < 2:
            dqab[i] = draw
        else:
            dg[:, 256:384] = draw.astype(BF)
    left, right = to_pairs(dqab[0], dqab[1])
    dg[:, 0:128] = left.astype(BF)
    dg[:, 128:256] = right.astype(BF)
    dg[:, 384:512] = dkk[:, 128:256].astype(BF)
    copies = scatter_sums(
        here, lambda n: nt(dg[:, 0:512], rows_of(W, n, 0, 512)), part, own, S.at[1], R.at[1], rss.at[1], rsr.at[1]
    )
    load_w = pltpu.make_async_copy(wc, W, wls.at[1])
    load_w.start()
    transposed(1)
    keep.put(LT, lambda a, w: dg[:, pl.ds(a, w)], dwa, 0, 512, 256)
    wait_all(copies)
    dx, dgain = rms_back(x2[...], vec[2:3, :], sum_blocks(own, R.at[1]))
    vg[2:3, :] = dgain
    dprev[...] += dx
    D2 = DG.at[2]
    D2[r] = dprev[...].astype(BF)
    copies = gather_block(here, D2, ags.at[2], agr.at[2])
    load_w.wait()
    load_g.wait()
    wait_all(copies)

    ffn_back(2, D2, 4 * QD, x1, 1, dwc, dprev[...])

    DD = DG.at[3]
    tap0, tap1, tap2 = taps(here, vec)
    from_c, from_z = tail_c[...], jnp.where(z > 0, tail_z[...], 0.0)
    dyc = nn(flat(DD), cols(W, 3 * QD, QD))
    mx[:, 0:QD] = (bcx[1] * cz[...]).astype(BF)
    dg[:, QD : 2 * QD] = (dyc * cz[...]).astype(BF)
    dzs = dyc * bcx[1]
    bx = bcx[0] * bcx[2]
    row = lax.broadcasted_iota(jnp.int32, (T, QD), 0)
    g0, g1, g2 = (jnp.zeros((1, QD), F32) for _ in range(3))
    for b in range(4):
        mine = bx[b * T : (b + 1) * T, :]
        dzb = dzs[b * T : (b + 1) * T, :]
        one, two, m1, m2 = behind(here, b, mine, from_c, from_z, start)
        g0 = g0 + jnp.sum(dzb * mine, axis=0, keepdims=True)
        g1 = g1 + jnp.sum(dzb * one * m1, axis=0, keepdims=True)
        g2 = g2 + jnp.sum(dzb * two * m2, axis=0, keepdims=True)
        b1 = tap1 * dzb * m1
        b2 = tap2 * dzb * m2
        heads[2 * b : 2 * b + 1, :] = b2[0:1]
        heads[2 * b + 1 : 2 * b + 2, :] = b1[0:1] + b2[1:2]
        dkk[b * T : (b + 1) * T, :] = (
            tap0 * dzb
            + jnp.where(row < T - 1, pltpu.roll(b1, T - 1, 0), 0.0)
            + jnp.where(row < T - 2, pltpu.roll(b2, T - 2, 0), 0.0)
        )
    over = remote(heads, head_c, hs.at[0], hr.at[0], here.at(dc=1))
    over.start()
    back = remote(heads, head_z, hs.at[1], hr.at[1], here.at(dz=O - 1, dc=1))

    @pl.when((c == 0) & (z > 0))
    def _():
        back.start()

    tap_at = pl.ds(pl.multiple_of(r * QD, 128), QD)
    vg[4:5, tap_at] = g0
    vg[5:6, tap_at] = g1
    vg[6:7, tap_at] = g2
    over.wait()

    @pl.when((c == 1) & (z < O - 1))
    def _():
        back.wait_recv()

    @pl.when((c == 0) & (z > 0))
    def _():
        back.wait_send()

    to_c, to_z = head_c[...], jnp.where(z < O - 1, head_z[...], 0.0)
    for b in range(4):
        rows = slice(b * T, (b + 1) * T)
        if b % 2:
            e = jnp.where(c == 0, to_c[2 * b : 2 * b + 2], to_z[2 * b - 2 : 2 * b])
        else:
            e = jnp.where(c == 0, to_c[2 * b : 2 * b + 2], to_c[2 * b + 2 : 2 * b + 4])
        dbx = dkk[rows, :] + jnp.where(row == T - 2, e[0:1], jnp.where(row == T - 1, e[1:2], 0.0))
        dg[rows, 0:QD] = (dbx * bcx[2, rows, :]).astype(BF)
        dg[rows, 2 * QD : 3 * QD] = (dbx * bcx[0, rows, :]).astype(BF)
    copies = scatter_sums(
        here, lambda n: nt(dg[:, 0:768], rows_of(W, n, 0, 768)), part, own, S.at[1], R.at[1], rss.at[3], rsr.at[3]
    )
    LT[...] = jnp.transpose(flat(DD))
    keep.put(LT, lambda a, w: mx[:, pl.ds(a, w)], dwc, 3 * QD, QD, QD)
    transposed(3)
    keep.put(LT, lambda a, w: dg[:, pl.ds(a, w)], dwc, 0, 768, 384)
    wait_all(copies)
    dx, dgain = rms_back(tok[...].astype(F32), vec[0:1, :], sum_blocks(own, R.at[1]))
    vg[0:1, :] = dgain
    dtok[...] = dprev[...] + dx
    keep.finish()


def backward(O, cot, tok, vec, hg, cosb, sinb, start, start_row, saved):
    (x1, x2, x3, h1, h2, h3, h4, bcx, cz, gu1, gu2, qkr, kv, oab, lse, wc, wa, Q, tail_c, tail_z) = saved
    sds = jax.ShapeDtypeStruct
    G = 4 * T
    rows = D // (4 * O)
    outs = (
        sds((T, D), F32), sds((16, D), F32),
        sds((2 * O, 2, rows, CW), BF), sds((2 * O, 2, rows, AW), BF),
    )
    dma = pltpu.SemaphoreType.DMA
    V = pltpu.VMEM
    args = (cot, tok, vec, hg, cosb, sinb, start, start_row, *saved)
    hbm = {id(a) for a in (gu1, gu2, wc, wa, kv, h1, h2, h3, h4)}
    return pl.pallas_call(
        functools.partial(backward_kernel, O),
        out_shape=outs,
        in_specs=[any_spec() if id(a) in hbm else vmem() for a in args],
        out_specs=(vmem(), vmem(), any_spec(), any_spec()),
        scratch_shapes=[
            V((2 * O, 2, rows, CW), BF), V((2, G, QF), F32), V((4, 4, T, D), BF), V((4, T, D), BF),
            V((G, QF), BF), V((G, QF), BF), V((G, QF), BF), V((D, G), BF), V((2, 2 * O, 2, rows, QF), BF),
            V((4, T, D // 2), F32), V((T, D), F32), V((2, 2, 3, T, D // 2), BF), V((2, 2, 3, T, D // 2), BF),
            V((2, 4, 256, 128), BF), V((2, 8, 2 * G), F32), V((4, 256, 128), F32), V((2, G, 128), F32),
            V((O, 4, 2, T, 256), BF), V((O, 4, T, 256), BF), V((O, 4, T, 256), BF), V((G, 256), F32),
            V((8, QD), F32), V((8, QD), F32), V((8, QD), F32), V((T, D), F32),
            dma((4, 3)), dma((4, 3)), dma((4, 2, 3)), dma((4, 2, 3)), dma((2,)), dma((2,)),
            dma((O,)), dma((O,)), dma((2,)), dma((3,)), dma((2,)), dma((4,)),
        ],
        compiler_params=pltpu.CompilerParams(
            collective_id=2, has_side_effects=True, vmem_limit_bytes=62 * 2**20
        ),
        cost_estimate=pl.CostEstimate(flops=2 * 10**10, bytes_accessed=10**8, transcendentals=10**7),
        name="backward",
    )(*args)


class Owners:
    def __init__(self, here, G, own, got, out, parts, spans, half, ls, cs, cr, ss, rs):
        self.here, self.G, self.own, self.got, self.out = here, G, own, got, out
        self.parts, self.spans, self.half = parts, spans, half
        self.ls, self.cs, self.cr, self.ss, self.rs = ls, cs, cr, ss, rs

    def span(self, g):
        place, width = self.spans[g]
        return pl.ds(place, width)

    def pair(self, g):
        h, at = self.here, self.span(g)
        return (
            pltpu.make_async_copy(self.G.at[:, h.c, :, at], self.own.at[:, :, at], self.ls.at[g]),
            remote(self.G.at[:, 1 - h.c, :, at], self.got.at[:, :, at], self.cs.at[g], self.cr.at[g], h.at(dc=1)),
        )

    def pieces(self, g):
        r, half = self.here.r, self.half
        out = []
        for base, width, place, group in self.parts:
            if group != g:
                continue
            first = half - base
            if 0 < first < 4 * width:
                assert first < width
                out.append((place, first, jnp.where(r == 0, 0, 1), jnp.where(r == 0, base, base + r * width - half)))
                out.append((place + first, width - first, 1, base + r * width + first - half))
            elif first >= 4 * width:
                out.append((place, width, 0, base + r * width))
            else:
                out.append((place, width, 1, base + r * width - half))
        return out

    def each(self, g, act, local):
        h = self.here
        for place, width, owner, at in self.pieces(g):
            dx = lax.rem(owner + h.x, 2)
            at = pl.multiple_of(at, 128)

            def one(dz, dy):
                shard = lax.rem(h.z + dz, h.O) * 2 + lax.rem(h.y + dy, 2)
                return (
                    self.own.at[shard, :, pl.ds(place, width)],
                    self.out.at[h.z, :, pl.ds(at, width)],
                )

            def along(dz, carry):
                for dy in (0, 1):
                    src, dst = one(dz, dy)
                    act(remote(src, dst, self.ss.at[g], self.rs, h.at(dx=dx, dz=dz, dy=dy)))
                return carry

            src, dst = one(0, 0)

            @pl.when(dx != 0)
            def _():
                act(remote(src, dst, self.ss.at[g], self.rs, h.at(dx=dx)))

            if local:

                @pl.when(dx == 0)
                def _():
                    pltpu.make_async_copy(src, dst, self.rs).start()

            src, dst = one(0, 1)
            act(remote(src, dst, self.ss.at[g], self.rs, h.at(dx=dx, dy=1)))
            lax.fori_loop(1, h.O, along, 0)

    def begin(self):
        for g in self.order:
            a, b = self.pair(g)
            a.start()
            b.start()

    order = (4, 2, 3, 1, 0)

    def send(self):
        for g in self.order:
            a, b = self.pair(g)
            a.wait()
            b.wait()
            at = self.span(g)
            self.own[:, :, at] = (self.own[:, :, at].astype(F32) + self.got[:, :, at].astype(F32)).astype(BF)
            self.each(g, lambda cp: cp.start(), True)

    def finish(self):
        for g in self.order:
            self.each(g, lambda cp: cp.wait_send(), False)
        pltpu.make_async_copy(self.out, self.out, self.rs).wait()


def owners_kernel(O, dwa, dwc, vg, ga, gc, total, own_a, got_a, own_c, got_c, v0, v1, v2, ls, cs, cr, ss, rs, vs, vr):
    here = Place(O)
    x, y, z, c, r = here.x, here.y, here.z, here.c, here.r
    barrier = pltpu.get_barrier_semaphore()

    def hello(**k):
        pl.semaphore_signal(barrier, inc=1, device_id=here.at(**k), device_id_type=MESH)

    def greet_all(dz, carry):
        for dx in (0, 1):
            for dy in (0, 1):
                hello(dx=dx, dz=dz, dy=dy)
        return carry

    for dx, dy in PLANE:
        hello(dx=dx, dy=dy)
    hello(dc=1)
    lax.fori_loop(1, O, greet_all, 0)
    pl.semaphore_wait(barrier, 4 + 4 * (O - 1))
    A = Owners(here, dwa, own_a, got_a, ga, ATTN_PARTS, ATTN_SPANS, (2 * D + D + 3 * FF) // 2, ls.at[0], cs.at[0], cr.at[0], ss.at[0], rs.at[0])
    Cv = Owners(here, dwc, own_c, got_c, gc, CONV_PARTS, CONV_SPANS, (4 * D + 3 * FF) // 2, ls.at[1], cs.at[1], cr.at[1], ss.at[1], rs.at[1])
    A.begin()
    Cv.begin()
    v0[c] = vg[...]
    cp = remote(v0.at[c], v0.at[c], vs.at[0], vr.at[0], here.at(dc=1))
    cp.start()
    A.send()
    cp.wait()
    v1[r] = v0[0] + v0[1]
    copies = []
    for k, (dx, dy) in enumerate(PLANE):
        cp = remote(v1.at[r], v1.at[r], vs.at[1 + k], vr.at[1 + k], here.at(dx=dx, dy=dy))
        cp.start()
        copies.append(cp)
    Cv.send()
    wait_all(copies)
    v2[z] = v1[0] + v1[1] + v1[2] + v1[3]

    def start(dz, carry):
        remote(v2.at[z], v2.at[z], vs.at[3 + dz], vr.at[3 + dz], here.at(dz=dz)).start()
        return carry

    lax.fori_loop(1, O, start, 0)

    def wait(dz, carry):
        remote(v2.at[z], v2.at[z], vs.at[3 + dz], vr.at[3 + dz], here.at(dz=dz)).wait()
        return carry

    lax.fori_loop(1, O, wait, 0)
    t = v2[0]
    for i in range(1, O):
        t = t + v2[i]
    total[...] = t
    A.finish()
    Cv.finish()


def owners(O, dwa, dwc, vg):
    sds = jax.ShapeDtypeStruct
    rows = D // (4 * O)
    dma = pltpu.SemaphoreType.DMA
    V = pltpu.VMEM
    return pl.pallas_call(
        functools.partial(owners_kernel, O),
        out_shape=(sds((O, rows, 2 * AW), BF), sds((O, rows, 2 * CW), BF), sds((16, D), F32)),
        in_specs=[any_spec(), any_spec(), vmem()],
        out_specs=(any_spec(), any_spec(), vmem()),
        scratch_shapes=[
            V((2 * O, rows, AW), BF), V((2 * O, rows, AW), BF), V((2 * O, rows, CW), BF), V((2 * O, rows, CW), BF),
            V((2, 16, D), F32), V((4, 16, D), F32), V((O, 16, D), F32),
            dma((2, 5)), dma((2, 5)), dma((2, 5)), dma((2, 5)), dma((2,)), dma((O + 3,)), dma((O + 3,)),
        ],
        compiler_params=pltpu.CompilerParams(
            collective_id=3, has_side_effects=True, vmem_limit_bytes=60 * 2**20
        ),
        cost_estimate=pl.CostEstimate(flops=10**8, bytes_accessed=6 * 10**7, transcendentals=0),
        name="owners",
    )(dwa, dwc, vg)


def adam_update(master, first_moment, second, gradient, step_value):
    first_new = beta_one * first_moment + (1.0 - beta_one) * gradient
    second_new = beta_two * second + (1.0 - beta_two) * gradient * gradient
    first_hat = first_new / (1.0 - beta_one**step_value)
    second_hat = second_new / (1.0 - beta_two**step_value)
    master_new = master - learn_rate * (
        first_hat / (jnp.sqrt(second_hat) + adam_eps) + decay_rate * master
    )
    return (master_new, first_new, second_new)


def shards(
    tokens, segments, cotangent, conv_weights, attn_weights, vectors, head_gains,
    master_conv, first_conv, second_conv, master_attn, first_attn, second_attn,
):
    O = lax.axis_size("z")
    cosb, sinb, start = tables(O, segments)
    start_row = jnp.broadcast_to(start[:, 0][None, :], (8, 4 * T))
    hg = jnp.concatenate([head_gains, head_gains], axis=1)
    tok = tokens[0]
    out_tok, *saved = forward(O, tok, vectors, hg, cosb, sinb, start, conv_weights, attn_weights)
    dtok, vg, dwc, dwa = backward(O, cotangent[0], tok, vectors, hg, cosb, sinb, start, start_row, saved)
    ga, gc, total = owners(O, dwa, dwc, vg)
    grad_attn = jnp.sum(ga.astype(F32), axis=0)
    grad_conv = jnp.sum(gc.astype(F32), axis=0)
    grad_vectors = total[0:7]
    grad_gains = total[8:10, 0:64] + total[8:10, 64:128]
    step_value = jnp.float32(STEP)
    new_conv = adam_update(master_conv, first_conv, second_conv, grad_conv, step_value)
    new_attn = adam_update(master_attn, first_attn, second_attn, grad_attn, step_value)
    return (
        out_tok[None], dtok[None], grad_conv, grad_attn, grad_vectors, grad_gains, *new_conv, *new_attn,
        lax.all_gather(new_conv[0].astype(BF), "dp", axis=1, tiled=True),
        lax.all_gather(new_attn[0].astype(BF), "dp", axis=1, tiled=True),
    )


def solution(mesh):
    outer = mesh.shape["ctx"] // 4
    split = Mesh(mesh.devices.reshape(mesh.shape["dp"], outer, 2, 2), ("dp", "z", "y", "c"))
    ctx = ("z", "y", "c")
    seq, rows, state = P("dp", ctx, None), P(ctx, None), P(ctx, "dp")
    return jax.shard_map(
        shards,
        mesh=split,
        in_specs=(seq, P("dp", ctx), seq, rows, rows, P(), P(), *([state] * 6)),
        out_specs=(seq, seq, state, state, P(), P(), *([state] * 6), rows, rows),
        check_vma=False,
    )
```

time: 2370 us -> 893 us (0.38)
  waiting for transfers between devices: 1860 us -> 62.6 us
  Pallas kernels: 0 us -> 736 us
  matrix products: 193 us -> 0 us
  other arithmetic: 143 us -> 21.1 us
  local copies, waits for them, and re-layouts: 56.2 us -> 10.4 us
  blocking collectives: 61.1 us -> 37.1 us
    reduce_scatter x6 -> x0, waiting for transfers between devices: 1470 us -> none  [the longest x2 1210 us: reduce_grads(): lax.psum_scatter(local_grad, 'ctx', scatter_dimension=0, tiled=True)]
    pallas_call x0 -> x3, Pallas kernels: none -> 736 us  [the longest x1 345 us: forward(): pl.pallas_call(functools.partial(forward_kernel, O), out_shape=outs, in_s...]
    all_gather x6 -> x2, waiting for transfers between devices: 386 us -> 62.6 us  [the longest x1 37.5 us: shards(): lax.all_gather(new_conv[0].astype(BF), 'dp', axis=1, tiled=True)]
    dot_general x61 -> x0, matrix products: 193 us -> none  [the longest x8 75.5 us: tokens_t(): lax.dot_general(left, right, (((0,), (0,)), ((), ())), preferred_element_...]
    concatenate x3 -> x2, other arithmetic: 96.7 us -> 2.66 us  [the longest x1 1.39 us: shards(): hg = jnp.concatenate([head_gains, head_gains], axis=1)]
    psum x1 -> x0, blocking collectives: 42.4 us -> none  [shards(): lax.psum((vector_grads, gain_grads), ('dp', 'ctx'))]
  transfers between devices with their start and end apart: 14 -> 2, of which waited for: 12 -> 2; matrix products, arithmetic and copies ran while one was open for 10% -> 1% of each run, Pallas kernels for 0% -> 0%
where the time goes in v1:
time: 893 us; the launch traced here: 882 us
  Pallas kernels  736 us (82%)
  waiting for transfers between devices  62.6 us (7%)
  blocking collectives  37.1 us (4%)
  other arithmetic  21.1 us (2%)
  between operations  14.4 us (2%)
  local copies, waits for them, and re-layouts  10.4 us (1%)
    pallas_call x1, Pallas kernels, forward(): pl.pallas_call(functools.partial(forward_kernel, O), out_shape=outs, in_s...  345 us
    pallas_call x1, Pallas kernels, owners(): pl.pallas_call(functools.partial(owners_kernel, O), out_shape=(sds((O, ro...  211 us
    pallas_call x1, Pallas kernels, backward(): pl.pallas_call(functools.partial(backward_kernel, O), out_shape=outs, in_...  180 us
    all_gather x1, waiting for transfers between devices, shards(): lax.all_gather(new_conv[0].astype(BF), 'dp', axis=1, tiled=True)  37.5 us
    all_gather x1, blocking collectives, tables(): lax.all_gather(segments, ('dp', 'z', 'y', 'c'), axis=0, tiled=True)  37.1 us
    all_gather x1, waiting for transfers between devices, shards(): lax.all_gather(new_attn[0].astype(BF), 'dp', axis=1, tiled=True)  25.1 us
  transfers between devices with their start and end apart: 2, of which 2 were waited for; matrix products, arithmetic and copies ran while one was open for 1% of the time, Pallas kernels for 0%

profile of v1, /device:TPU:10, one launch (start us, length us, event | category | flops | bytes accessed | tf_op | source)
XLA Modules:
  0.0 881.7 jit_solution(8008555285274216033)
XLA Ops:
  7.3 1.4 pad_maximum_fusion.2.hg
  8.7 37.1 %all-gather = s32[32,1,128]{2,1,0:T(1,128)S(1)} all-gather(s32[1,1,128]{2,1,0:T(1,128)} %bitcast.21), channel_id=1, replica_groups=mesh['dp'=2,'z'=4,'y'=2,'c'=2] {'dp','z','y','c'}, dimensions={0}, use_global_device_ids=true | all-gather | bytes 16896 | tf_op jit(solution)/shard_map/all_gather | solution.py:536
  45.8 1.2 fusion.4
  47.7 1.0 fusion.2
  48.7 1.3 pad_maximum_fusion
  49.9 0.8 broadcast_in_dim.48.start
  50.8 344.7 %forward.1 = (bf16[128,1024]{1,0:T(8,128)(2,1)}, f32[128,1024]{1,0:T(8,128)}, f32[128,1024]{1,0:T(8,128)}, f32[128,1024]{1,0:T(8,128)}, bf16[4,128,1024]{2,1,0:T...) custom-call(bf16[128,1024]{1,0:T(8,128)(2,1)} %bitcast.22, ...), custom_call_target="tpu_custom_call" | custom-call | flops 10000000000 | bytes 60000000 | tf_op jit(solution)/shard_map/forward/pallas_call | solution.py:514
  395.4 0.6 broadcast_in_dim.50.start_row
  396.0 180.3 %backward.1 = (f32[128,1024]{1,0:T(8,128)}, f32[16,1024]{1,0:T(8,128)}, bf16[8,2,64,4480]{3,2,1,0:T(8,128)(2,1)}, bf16[8,2,64,4224]{3,2,1,0:T(8,128)(2,1)}) custom-call(bf16[128,1024]{1,0:T(8,128)(2,1)} %bitcast.24, bf16[128,1024]{1,0:T(8,128)(2,1)} %bitcast.23, f32[7,1024]{1,0:T(8,128)} %vec.3, f32[2,128]{1,0:T(2,128)} %pad_maximum_fusion.2.hg, ...), custom_call_target="tpu_custom_call" | custom-call | flops 20000000000 | bytes 100000000 | tf_op jit(solution)/shard_map/backward/pallas_call | solution.py:872
  576.3 211.0 %owners.1 = (bf16[4,64,8448]{2,1,0:T(8,128)(2,1)}, bf16[4,64,8960]{2,1,0:T(8,128)(2,1)}, f32[16,1024]{1,0:T(8,128)}) custom-call(bf16[8,2,64,4224]{3,2,1,0:T(8,128)(2,1)} %get-tuple-element.64.dwa, bf16[8,2,64,4480]{3,2,1,0:T(8,128)(2,1)} %get-tuple-element.65.dwc, f32[16,1024]{1,0:T(8,128)} %get-tuple-element.66.vg), custom_call_target="tpu_custom_call" | custom-call | flops 100000000 | bytes 60000000 | tf_op jit(solution)/shard_map/owners/pallas_call | solution.py:1049
  787.4 3.3 convert_reduce_fusion.1
  790.9 0.7 copy-done.7
  791.6 4.1 fusion.5
  795.8 3.4 convert_reduce_fusion
  799.5 0.7 copy-done.4
  800.2 4.4 fusion.7
  804.6 0.6 slice.10
  805.2 0.6 slice_add_fusion
  805.9 25.1 %all-gather.6.cloned.1.call-done = bf16[64,16896]{1,0:T(8,128)(2,1)} async-done(((bf16[64,8448]{1,0:T(8,128)(2,1)}), bf16[64,16896]{1,0:T(8,128)(2,1)}) %all-gather.6.cloned.1.call-update) | async-done | bytes 2162704 | tf_op jit(solution)/shard_map/all_gather | solution.py:1100
  831.0 37.5 %all-gather.4.cloned.1.call-done = bf16[64,17920]{1,0:T(8,128)(2,1)} async-done(((bf16[64,8960]{1,0:T(8,128)(2,1)}), bf16[64,17920]{1,0:T(8,128)(2,1)}) %all-gather.4.cloned.1.call-update) | async-done | bytes 2293776 | tf_op jit(solution)/shard_map/all_gather | solution.py:1099
  868.5 0.7 copy.36
  869.2 0.8 copy.37
  870.0 3.3 copy.38
  873.3 1.3 copy.39
  (41 shorter events, 1.3 us)
Async XLA Ops:
  7.2 823.8 %all-gather.6.cloned.1.call-start = ((), (), s32[]{:S(2)}) async-start(), calls=%async_computation.1 | async-start | bytes 3244032 | tf_op jit(solution)/shard_map/all_gather | solution.py:1100
  787.3 3.4 copy-start.5
  787.3 3.6 copy-start.6
  787.4 4.2 copy-start.7
  791.6 4.1 copy-start.1
  795.7 72.8 %all-gather.4.cloned.1.call-start = ((), (), s32[]{:S(2)}) async-start(), calls=%async_computation | async-start | bytes 3440640 | tf_op jit(solution)/shard_map/all_gather | solution.py:1099
  795.7 3.5 copy-start.2
  795.7 3.7 copy-start.3
  795.8 4.4 copy-start.4
  800.2 4.4 copy-start
  800.2 4.5 copy-start.11
  800.2 68.3 %copy-start.10 = (bf16[128,1024]{1,0:T(8,128)(2,1)S(1)}, bf16[128,1024]{1,0:T(8,128)(2,1)}, u32[]{:S(2)}) copy-start(bf16[128,1024]{1,0:T(8,128)(2,1)} %get-tuple-element.42) | copy-start | bytes 786436
  800.2 69.0 %copy-start.9 = (f32[128,1024]{1,0:T(8,128)S(1)}, f32[128,1024]{1,0:T(8,128)}, u32[]{:S(2)}) copy-start(f32[128,1024]{1,0:T(8,128)} %get-tuple-element.63) | copy-start | bytes 1572868
  870.0 3.3 copy-start.8
Sparse Core Ops, SparseCore 0:
  795.8 35.1 all-gather.5
  833.1 35.3 all-gather.3

commit v2 on v1

v2 whole, which is shorter than its diff:
```python
import functools
import jax
import jax.numpy as jnp
from jax import lax
from jax.sharding import Mesh, PartitionSpec as P
import jax.experimental.pallas as pl
import jax.experimental.pallas.tpu as pltpu

D = 1024
FF = 4608
HEADS = 16
KV_HEADS = 8
HEAD_DIM = 64
STEP = 5
KVW = 512
T = 128
QF = FF // 4
QD = D // 4
CW = 4 * QD + 3 * QF
AW = 3 * QD + 3 * QF

norm_eps = 1e-05
rope_base = 1000000.0
learn_rate = 0.01
decay_rate = 0.1
beta_one = 0.9
beta_two = 0.95
adam_eps = 1e-08

MESH = pl.DeviceIdType.MESH

SCHEDULE = {
    "in": ("f0", "f1",),
    "start": ("p0", "p1", "f2",),
    "h1 sent": ("f3", "p2",),
    "h1 relayed": ("f4", "b0", "p3",),
    "h1": ("f5", "l0", "p4", "l1", "r0",),
    "conv": ("r1", "p5",),
    "x1 sent": (),
    "x1 relayed": ("b2", "f6", "f7",),
    "h2 sent": (),
    "h2 relayed": ("b3", "f8",),
    "gate1 0": ("l2", "r2",),
    "gate1 1": ("l3", "r3",),
    "gate1 2": ("l4", "r4",),
    "down1": ("p6", "l5", "p7", "r5", "p8",),
    "x2 sent": (),
    "x2 relayed": ("f9", "b6",),
    "h3 sent": ("p9", "f10", "b7",),
    "h3 relayed": ("f11", "l6", "l7",),
    "qkv": ("r6",),
    "kv sent": ("b8",),
    "kv": ("p10",),
    "half": ("p11", "b9",),
    "attended": ("l8", "r7",),
    "x3 sent": ("b10",),
    "x3 relayed": ("l9",),
    "h4 sent": ("b11",),
    "h4 relayed": (),
    "gate2 0": ("l10", "r8",),
    "gate2 1": ("l11", "r9",),
    "gate2 2": ("r10",),
    "down2": ("r11",),
    "x4 sent": (),
    "x4 relayed": (),
}
BF = jnp.bfloat16
F32 = jnp.float32
PLANE = ((1, 1), (1, 0), (0, 1))

TILE = 384
WIDE = 2 * QF


def packed(lead, base, place):
    parts, spans = list(lead), []
    for n in range(3):
        for k in (0, 1):
            parts.append((base + k * FF + n * TILE, QF, TILE, place + (2 * n + k) * TILE, 2 + n))
    parts.append((base + 2 * FF, QF, QF, place + WIDE, 5))
    for g in range(6):
        mine = [p for p in parts if p[4] == g]
        spans.append((mine[0][3], sum(p[2] for p in mine)))
    return tuple(parts), tuple(spans)


CONV_PARTS, CONV_SPANS = packed(
    ((0, QD, QD, 0, 0), (D, QD, QD, QD, 0), (2 * D, QD, QD, 2 * QD, 0), (3 * D, QD, QD, 3 * QD, 1)), 4 * D, 4 * QD
)
KQ = KVW // 4
ATTN_PARTS, ATTN_SPANS = packed(
    ((0, QD, QD, 0, 0), (D, KQ, KQ, QD, 0), (D + KVW, KQ, KQ, QD + KQ, 0), (2 * D, QD, QD, 2 * QD, 1)), 3 * D, 3 * QD
)


def nn(a, b):
    return jnp.dot(a, b, preferred_element_type=F32)


def nt(a, b):
    return lax.dot_general(a, b, (((1,), (1,)), ((), ())), preferred_element_type=F32)


def tn(a, b):
    return lax.dot_general(a, b, (((0,), (0,)), ((), ())), preferred_element_type=F32)


def rms_scale(v):
    return lax.rsqrt(jnp.mean(v * v, axis=-1, keepdims=True) + norm_eps)


class Place:
    def __init__(self, O):
        self.O = O
        self.x, self.z = lax.axis_index("dp"), lax.axis_index("z")
        self.y, self.c = lax.axis_index("y"), lax.axis_index("c")
        self.r = self.x * 2 + self.y

    def at(self, dx=0, dz=0, dy=0, dc=0):
        out = {}
        if not (isinstance(dx, int) and dx == 0):
            out["dp"] = lax.rem(self.x + dx, 2)
        if not (isinstance(dz, int) and dz == 0):
            out["z"] = lax.rem(self.z + dz, self.O)
        if not (isinstance(dy, int) and dy == 0):
            out["y"] = lax.rem(self.y + dy, 2)
        if not (isinstance(dc, int) and dc == 0):
            out["c"] = lax.rem(self.c + dc, 2)
        return out

    def block(self, dx, dy):
        return lax.rem(self.x + dx, 2) * 2 + lax.rem(self.y + dy, 2)


def greet(here):
    O = here.O
    barrier = pltpu.get_barrier_semaphore()

    def hello(**k):
        pl.semaphore_signal(barrier, inc=1, device_id=here.at(**k), device_id_type=MESH)

    hello(dx=1, dy=1)
    hello(dx=1)
    hello(dy=1)
    hello(dc=1)
    hello(dz=1, dc=1)
    hello(dz=O - 1, dc=1)

    def along(dz, carry):
        for dy in (0, 1):
            hello(dz=dz, dy=dy)
        return carry

    lax.fori_loop(1, O, along, 0)
    pl.semaphore_wait(barrier, 6 + 2 * (O - 1))


def remote(src, dst, ss, rs, dev):
    return pltpu.make_async_remote_copy(
        src_ref=src, dst_ref=dst, send_sem=ss, recv_sem=rs, device_id=dev, device_id_type=MESH
    )


HALF = (slice(0, T // 2), slice(T // 2, T))


class Gather:
    def __init__(self, here, H, ss, rs):
        self.here = here
        r, rx, ry = here.r, here.block(1, 0), here.block(0, 1)
        to_x, to_y = here.at(dx=1), here.at(dy=1)

        def cp(i, block, half, dev):
            rows = pl.ds(half * (T // 2), T // 2)
            return remote(H.at[block, rows], H.at[block, rows], ss.at[i], rs.at[i], dev)

        self.first = (cp(0, r, 0, to_x), cp(1, r, 1, to_y), cp(2, r, 1, to_x), cp(3, r, 0, to_y))
        self.then = (cp(4, rx, 0, to_y), cp(5, ry, 1, to_x))
        for c in self.first:
            c.start()

    def relay(self):
        for i in (0, 1):
            self.first[i].wait_recv()
            self.then[i].start()

    def wait(self):
        for c in self.first[2:]:
            c.wait_recv()
        for c in self.then:
            c.wait_recv()
        for c in self.first + self.then:
            c.wait_send()


class Sums:
    def __init__(self, here, part, S, R, ss, rs):
        self.here, self.part, self.S, self.R, self.ss, self.rs = here, part, S, R, ss, rs

    def cp(self, n, i):
        h = self.here
        dev = h.at(dx=1) if i % 2 == 0 else h.at(dy=1)
        return remote(self.S.at[n, i], self.R.at[n, i], self.ss.at[n, i], self.rs.at[n, i], dev)

    def put(self, n, i, block, half):
        self.S[n, i] = self.part[n, block, HALF[half], :].astype(BF)
        self.cp(n, i).start()

    def begin(self, tile_fn):
        h = self.here
        rx, ry, rd = h.block(1, 0), h.block(0, 1), h.block(1, 1)
        for n in (0, 1):
            self.part[n] = tile_fn(n).reshape(4, T, D // 2)
            self.put(n, 0, rd, 0)
            self.put(n, 1, rd, 1)
            self.put(n, 2, rx, 0)
            self.put(n, 3, ry, 1)

    def relay(self):
        h = self.here
        rx, ry = h.block(1, 0), h.block(0, 1)
        for n in (0, 1):
            for i, block, half in ((0, ry, 0), (1, rx, 1)):
                self.cp(n, i).wait_recv()
                at = 5 - i
                both = self.part[n, block, HALF[half], :] + self.R[n, i].astype(F32)
                self.S[n, at] = both.astype(BF)
                self.cp(n, at).start()

    def wait(self):
        out = []
        for n in (0, 1):
            for i in (2, 3, 4, 5):
                self.cp(n, i).wait_recv()
            for i in range(6):
                self.cp(n, i).wait_send()
            mine = self.part[n, self.here.r]
            R = self.R
            low = mine[HALF[0]] + R[n, 2].astype(F32) + R[n, 5].astype(F32)
            high = mine[HALF[1]] + R[n, 4].astype(F32) + R[n, 3].astype(F32)
            out.append(jnp.concatenate([low, high], axis=0))
        return jnp.concatenate(out, axis=1)


def wait_all(copies):
    for cp in copies:
        cp.wait()


class Weights:
    def __init__(self, here, hbm, W, parts, spans, ls, ys, yr, zs, zr, cs, cr):
        self.here, self.hbm, self.W = here, hbm, W
        self.parts, self.spans = parts, spans
        self.ls, self.ys, self.yr, self.zs, self.zr, self.cs, self.cr = ls, ys, yr, zs, zr, cs, cr
        self.relayed = here.O == 4
        self.passed = set()

    def source(self, part, dy):
        base, stride, width, _, _ = part
        chip = self.here.x * 2 + lax.rem(self.here.y + dy, 2)
        return self.hbm.at[:, pl.ds(pl.multiple_of(base + chip * stride, 128), width)]

    def target(self, part):
        _, _, width, place, _ = part
        h = self.here
        return self.W.at[h.z * 2 + h.y, h.c, :, pl.ds(place, width)]

    def fetch(self, g):
        h = self.here
        for part in self.parts:
            if part[4] != g:
                continue
            pltpu.make_async_copy(self.source(part, 0), self.target(part), self.ls.at[g]).start()
            remote(self.source(part, 1), self.target(part), self.ys.at[g], self.yr.at[g], h.at(dy=1)).start()

    def shards(self, g, first, count):
        place, width = self.spans[g]
        return self.W.at[pl.ds(first, count), self.here.c, :, pl.ds(place, width)]

    def hop(self, g, dz, owner):
        src = self.shards(g, 2 * owner, 2)
        return remote(src, src, self.zs.at[g, dz], self.zr.at[g, dz], self.here.at(dz=dz))

    def near(self, dz):
        z = self.here.z
        return z < 3 if dz == 1 else z > 0 if dz == 3 else z >= 0

    def came(self, dz):
        z = self.here.z
        return z > 0 if dz == 1 else z < 3 if dz == 3 else z >= 0

    def bridge(self, g, owner, dz):
        src = self.shards(g, 2 * owner, 2)
        return remote(src, src, self.zs.at[g, 0], self.zr.at[g, 0], self.here.at(dz=dz))

    def push(self, g):
        h = self.here
        one = self.shards(g, 0, 1)
        pltpu.make_async_copy(one, one, self.ls.at[g]).wait()
        pltpu.make_async_copy(one, one, self.yr.at[g]).wait()
        self.core_copy(g, h.z).start()
        if self.relayed:
            for dz in (2, 1, 3):

                @pl.when(self.near(dz))
                def _():
                    self.hop(g, dz, h.z).start()
        else:

            def along(dz, carry):
                self.hop(g, dz, h.z).start()
                return carry

            lax.fori_loop(1, h.O, along, 0)

    def core_copy(self, g, owner):
        mine = self.shards(g, 2 * owner, 2)
        return remote(mine, mine, self.cs.at[g], self.cr.at[g], self.here.at(dc=1))

    def behind(self, dz):
        return lax.rem(self.here.z + self.here.O - dz, self.here.O)

    def pass_far(self, g):
        h = self.here
        if not self.relayed:
            return
        self.passed.add(g)
        self.hop(g, 2, h.z).wait_recv()

        @pl.when(h.z == 2)
        def _():
            self.bridge(g, 0, 1).start()

        @pl.when(h.z == 1)
        def _():
            self.bridge(g, 3, 3).start()

        self.core_copy(g, self.behind(2)).start()

    def land(self, g):
        h = self.here
        if self.relayed:
            if g not in self.passed:
                self.pass_far(g)
            for dz in (1, 3):

                @pl.when(self.came(dz))
                def _():
                    self.hop(g, dz, h.z).wait_recv()
                    self.core_copy(g, self.behind(dz)).start()

            @pl.when((h.z == 0) | (h.z == 3))
            def _():
                self.bridge(g, 0, 1).wait_recv()
                self.core_copy(g, 3 - h.z).start()

        else:

            def along(dz, carry):
                self.hop(g, dz, h.z).wait_recv()
                self.core_copy(g, self.behind(dz)).start()
                return carry

            lax.fori_loop(1, h.O, along, 0)

    def ready(self, g):
        place, width = self.spans[g]
        half = self.W.at[:, 0, :, pl.ds(place, width)]
        pltpu.make_async_copy(half, half, self.cs.at[g]).wait()
        pltpu.make_async_copy(half, half, self.cr.at[g]).wait()

    def finish(self):
        h = self.here
        for g in range(6):
            one = self.shards(g, 0, 1)
            pltpu.make_async_copy(one, one, self.ys.at[g]).wait()
            if self.relayed:
                for dz in (1, 2, 3):

                    @pl.when(self.near(dz))
                    def _():
                        self.hop(g, dz, h.z).wait_send()

                @pl.when((h.z == 1) | (h.z == 2))
                def _():
                    self.bridge(g, 0, 1).wait_send()

            else:

                def along(dz, carry):
                    self.hop(g, dz, h.z).wait_send()
                    return carry

                lax.fori_loop(1, h.O, along, 0)


def cols(W, place, width):
    v = W[:, :, :, pl.ds(place, width)]
    return v.reshape(D, width)


def rows_of(W, n, place, width):
    h = W.shape[0] // 2
    v = W[n * h : (n + 1) * h, :, :, pl.ds(place, width)]
    return v.reshape(D // 2, width)


def lane_low(shape):
    return lax.broadcasted_iota(jnp.int32, shape, len(shape) - 1) < 64


def lane_first(shape):
    return lax.rem(lax.broadcasted_iota(jnp.int32, shape, len(shape) - 1), 64) < 32


def head_mean(v):
    low = lane_low(v.shape)
    a = jnp.sum(jnp.where(low, v, 0.0), axis=-1, keepdims=True)
    b = jnp.sum(jnp.where(low, 0.0, v), axis=-1, keepdims=True)
    return jnp.where(low, a, b) * (1.0 / HEAD_DIM)


def turn(v):
    return jnp.where(lane_first(v.shape), pltpu.roll(v, 96, 1), pltpu.roll(v, 32, 1))


def to_pairs(left, right):
    low = lane_low(left.shape)
    a = jnp.where(low, left, pltpu.roll(right, 64, 1))
    b = jnp.where(low, pltpu.roll(left, 64, 1), right)
    return a, b


def stacked(a, b):
    low = lane_low(a.shape)
    zero = jnp.zeros_like(a)
    return (jnp.where(low, a, zero), jnp.where(low, b, zero), jnp.where(low, zero, a), jnp.where(low, zero, b))


def ffn_forward_tile(H, W, at, gu, u, n):
    both = nn(H[...].reshape(4 * T, D), cols(W, at + 2 * n * TILE, 2 * TILE))
    gu[:, 2 * n * TILE : 2 * (n + 1) * TILE] = both
    gate, up = both[:, 0:TILE], both[:, TILE:]
    u[:, n * TILE : (n + 1) * TILE] = (gate / (1.0 + jnp.exp(-gate)) * up).astype(BF)


def taps(here, vec):
    at = pl.ds(pl.multiple_of(here.r * QD, 128), QD)
    return tuple(vec[4 + i : 5 + i, at] for i in range(3))


def behind(here, b, mine, from_c, from_z, start):
    z, c, yb = here.z, here.c, b % 2
    if yb:
        before = jnp.where(c == 1, from_c[2 * b : 2 * b + 2], from_c[2 * b - 2 : 2 * b])
    else:
        before = jnp.where(c == 1, from_c[2 * b : 2 * b + 2], from_z[2 * b + 2 : 2 * b + 4])
    row = lax.broadcasted_iota(jnp.int32, (T, QD), 0)
    one = jnp.where(row == 0, before[1:2], pltpu.roll(mine, 1, 0))
    two = jnp.where(row == 0, before[0:1], jnp.where(row == 1, before[1:2], pltpu.roll(mine, 2, 0)))
    t = z * 512 + yb * 256 + c * T + lax.broadcasted_iota(jnp.int32, (T, 1), 0)
    pos = t - start[b * T : (b + 1) * T, 0:1]
    return one, two, jnp.where(pos >= 1, 1.0, 0.0), jnp.where(pos >= 2, 1.0, 0.0)


def meta_copies(here, M1, M2, M3, ms, mr):
    def along(act):
        def body(dz, carry):
            act(remote(M1.at[here.z], M1.at[here.z], ms.at[dz], mr.at[dz], here.at(dz=dz)))
            return carry

        lax.fori_loop(1, here.O, body, 0)

    core = remote(M2.at[here.c], M2.at[here.c], ms.at[0], mr.at[0], here.at(dc=1))
    plane = [
        remote(M3.at[here.r], M3.at[here.r], ms.at[here.O + k], mr.at[here.O + k], here.at(dx=dx, dy=dy))
        for k, (dx, dy) in enumerate(PLANE)
    ]
    return along, core, plane


def write_starts(here, M3, start, start_row):
    counts = jnp.sum(M3[...].reshape(4, 2 * here.O, 8, T), axis=1)
    for b in range(4):
        xb = b // 2
        pair = counts[2 * xb] + counts[2 * xb + 1]
        begin, end = pair[1:2, :], here.O * 4 * T - pair[2:3, :]
        seg = M3[b, here.c, here.z, 0:1, :]
        start_row[:, b * T : (b + 1) * T] = jnp.broadcast_to(
            jnp.where(seg == 0, 0, jnp.where(seg == 1, begin, end)), (8, T)
        )
        ids = jnp.transpose(jnp.broadcast_to(seg.astype(F32), (T, T)))
        first = jnp.where(ids < 0.5, 0, jnp.where(ids < 1.5, begin, end))
        start[b * T : (b + 1) * T, :] = first


def write_rotary(here, start, freq, cosb, sinb):
    for b in range(4):
        rows = slice(b * T, (b + 1) * T)
        t = here.z * 512 + (b % 2) * 256 + here.c * T + lax.broadcasted_iota(jnp.int32, (T, T), 0)
        angle = (t - start[rows, :]).astype(F32) * freq[0:1, :]
        cosb[rows, :] = jnp.cos(angle)
        sinb[rows, :] = jnp.sin(angle) * freq[1:2, :]


def forward_kernel(
    O, tok, cot, vec, hg, meta, freq, wc_hbm, wa_hbm,
    out_tok, x1, x2, x3, h1_out, h2_out, h3_out, h4_out, bcx, cz, gu1_out, gu2_out, qkr, kv_out, oab, lse, wc_out, wa_out, Q,
    tail_c, tail_z, cosb, sinb, start, start_row, cots_out,
    cots, h1, h2, h3, h4, gu1, gu2, kv, wc, wa,
    u, part, S, R, tails, acc, M1, M2, M3,
    ags, agr, rss, rsr, hs, hr, kvs, kvr, wls, wys, wyr, wzs, wzr, wcs, wcr, ms, mr, outs,
):
    here = Place(O)
    x, y, z, c, r = here.x, here.y, here.z, here.c, here.r
    greet(here)
    sets = []
    for i, (hbm, W, parts, spans) in enumerate(
        ((wc_hbm, wc, CONV_PARTS, CONV_SPANS), (wa_hbm, wa, ATTN_PARTS, ATTN_SPANS))
    ):
        sets.append(
            Weights(here, hbm, W, parts, spans, *(a.at[i] for a in (wls, wys, wyr, wzs, wzr, wcs, wcr)))
        )
    queue = [(w, g) for w in sets for g in range(6)]

    def at(point):
        for step in SCHEDULE[point]:
            w, g = queue[int(step[1:])]
            {"f": w.fetch, "p": w.push, "b": w.pass_far, "l": w.land, "r": w.ready}[step[0]](g)

    z_meta, core_meta, plane_meta = meta_copies(here, M1, M2, M3, ms, mr)
    M1[z] = meta[...]
    z_meta(lambda cp: cp.start())
    saving = []

    def save(i, src, dst):
        cp = pltpu.make_async_copy(src, dst, outs.at[i])
        cp.start()
        saving.append(cp)

    at("in")
    x0 = tok[...].astype(F32)
    h1[r] = (x0 * rms_scale(x0) * vec[0:1, :]).astype(BF)
    blocks = Gather(here, h1, ags.at[0], agr.at[0])
    at("start")
    z_meta(lambda cp: cp.wait())
    M2[c] = M1[...]
    core_meta.start()
    at("h1 sent")
    blocks.relay()
    core_meta.wait()
    M3[r] = M2[...]
    for cp in plane_meta:
        cp.start()
    at("h1 relayed")
    blocks.wait()
    wait_all(plane_meta)
    write_starts(here, M3, start, start_row)
    at("h1")

    save(0, h1, h1_out)
    h = h1[...].reshape(4 * T, D)
    for i in range(3):
        bcx[i] = nn(h, cols(wc, i * QD, QD))
    bx = bcx[0] * bcx[2]
    for b in range(4):
        tails[2 * b : 2 * b + 2, :] = bx[b * T + T - 2 : b * T + T, :]
    over = remote(tails, tail_c, hs.at[0], hr.at[0], here.at(dc=1))
    over.start()
    ahead = remote(tails, tail_z, hs.at[1], hr.at[1], here.at(dz=1, dc=1))

    @pl.when((c == 1) & (z < O - 1))
    def _():
        ahead.start()

    over.wait()

    @pl.when((c == 0) & (z > 0))
    def _():
        ahead.wait_recv()

    @pl.when((c == 1) & (z < O - 1))
    def _():
        ahead.wait_send()

    tap0, tap1, tap2 = taps(here, vec)
    from_c, from_z = tail_c[...], jnp.where(z > 0, tail_z[...], 0.0)
    for b in range(4):
        mine = bx[b * T : (b + 1) * T, :]
        one, two, m1, m2 = behind(here, b, mine, from_c, from_z, start)
        cz[b * T : (b + 1) * T, :] = tap0 * mine + tap1 * one * m1 + tap2 * two * m2
    yc = (bcx[1] * cz[...]).astype(BF)
    at("conv")
    sums = Sums(here, part, S, R, rss.at[0], rsr.at[0])
    sums.begin(lambda n: nt(yc, rows_of(wc, n, 3 * QD, QD)))
    at("x1 sent")
    sums.relay()
    at("x1 relayed")
    xn = tok[...].astype(F32) + sums.wait()
    x1[...] = xn
    h2[r] = (xn * rms_scale(xn) * vec[1:2, :]).astype(BF)
    blocks = Gather(here, h2, ags.at[1], agr.at[1])
    at("h2 sent")
    blocks.relay()
    at("h2 relayed")
    write_rotary(here, start, freq, cosb, sinb)
    blocks.wait()
    cots[r] = cot[...]
    cot_blocks = Gather(here, cots, ags.at[4], agr.at[4])
    for n in range(3):
        at("gate1 %d" % n)
        if n == 1:
            cot_blocks.relay()
        ffn_forward_tile(h2, wc, 4 * QD, gu1, u, n)
    cot_blocks.wait()
    save(9, cots, cots_out)
    save(1, h2, h2_out)
    save(2, gu1, gu1_out)
    at("down1")
    sums = Sums(here, part, S, R, rss.at[1], rsr.at[1])
    sums.begin(lambda n: nt(u[...], rows_of(wc, n, 4 * QD + WIDE, QF)))
    save(3, wc, wc_out)
    at("x2 sent")
    sums.relay()
    at("x2 relayed")
    xn = x1[...] + sums.wait()
    x2[...] = xn
    h3[r] = (xn * rms_scale(xn) * vec[2:3, :]).astype(BF)
    blocks = Gather(here, h3, ags.at[2], agr.at[2])
    at("h3 sent")
    blocks.relay()
    at("h3 relayed")
    blocks.wait()
    at("qkv")

    qkv = nn(h3[...].reshape(4 * T, D), cols(wa, 0, 512))
    qa, qb = to_pairs(qkv[:, 0:128], qkv[:, 128:256])
    raw = (qa, qb, qkv[:, 256:384])
    turned = []
    for i in range(3):
        qkr[i] = raw[i]
        gain = hg[0:1, :] if i < 2 else hg[1:2, :]
        w = raw[i] * lax.rsqrt(head_mean(raw[i] * raw[i]) + norm_eps) * gain
        turned.append(w * cosb[...] + turn(w) * sinb[...])
    keys = turned[2].astype(BF)
    values = qkv[:, 384:512].astype(BF)
    for b in range(4):
        kv[z, b, c, :, 0:128] = keys[b * T : (b + 1) * T]
        kv[z, b, c, :, 128:256] = values[b * T : (b + 1) * T]
    mine = kv.at[z, :, c]

    bridged = O == 4

    def far(dz):
        return bridged and dz == 3

    def up(dz):
        return remote(mine, mine, kvs.at[dz], kvr.at[dz], here.at(dz=dz))

    def over_far():
        got = kv.at[0, :, c]
        return remote(got, got, kvs.at[2 * O], kvr.at[2 * O], here.at(dz=1))

    def along_z(act):
        if bridged:
            for dz in range(1, O):
                act(dz)
        else:

            def body(dz, carry):
                act(dz)
                return carry

            lax.fori_loop(1, O, body, 0)

    def send_up(dz):
        if not far(dz):

            @pl.when(z + dz < O)
            def _():
                up(dz).start()

    along_z(send_up)
    at("kv sent")
    pair0 = remote(mine, mine, kvs.at[0], kvr.at[0], here.at(dc=1))
    pair0.start()
    for s in (0, 1):
        low4 = stacked(*(
            (turned[i][s * 256 : (s + 1) * 256] * (HEAD_DIM ** -0.5)).astype(BF) for i in (0, 1)
        ))
        for g in range(4):
            Q[s, g] = low4[g]

    def passed(dz):
        got = kv.at[z - dz, :, c]
        return remote(got, got, kvs.at[O + dz], kvr.at[O + dz], here.at(dc=1))

    if bridged:

        @pl.when(z == 2)
        def _():
            up(2).wait_recv()
            over_far().start()

    def pass_on(dz):
        @pl.when(z - dz >= 0)
        def _():
            if far(dz):
                over_far().wait_recv()
            elif bridged and dz == 2:

                @pl.when(z != 2)
                def _():
                    up(dz).wait_recv()

            else:
                up(dz).wait_recv()
            passed(dz).start()

    along_z(pass_on)
    pair0.wait()

    def pass_wait(dz):
        @pl.when(z - dz >= 0)
        def _():
            passed(dz).wait()

    along_z(pass_wait)
    at("kv")
    save(4, h3, h3_out)
    save(5, kv, kv_out)

    low = lane_low((256, 128))
    for s in (0, 1):
        if s:
            at("half")
        acc[...] = jnp.zeros_like(acc)
        first_of = start[s * 256 : (s + 1) * 256, 0:1]
        row = lax.broadcasted_iota(jnp.int32, (256, 1), 0)
        t = z * 512 + lax.div(row, T) * 256 + c * T + lax.rem(row, T)

        def chunk(j, carry):
            block = kv[lax.div(j, 2), 2 * s + lax.rem(j, 2)].reshape(256, 256)
            k, v = block[:, 0:128], block[:, 128:256]
            one = jnp.ones_like(v)
            v_low = jnp.where(low, v, one)
            v_high = jnp.where(low, one, v)
            at = j * 256 + lax.broadcasted_iota(jnp.int32, (256, 256), 1)
            allowed = (at >= first_of) & (at <= t)
            for g in range(4):
                sc = nt(Q[s, g], k)
                p = jnp.where(allowed, jnp.exp(sc), 0.0).astype(BF)
                acc[g] += nn(p, v_low if g < 2 else v_high)
            return carry

        lax.fori_loop(0, 2 * z + 2, chunk, 0)
        heads = []
        for g in range(4):
            a = acc[g]
            other = pltpu.roll(a, 64, 1)
            heads.append(a / other)
            total = jnp.where(low, other, a) if g < 2 else jnp.where(low, a, other)
            lse[s, :, g * 256 : (g + 1) * 256] = jnp.transpose(jnp.log(total))[0:8, :]
        oab[0, s * 256 : (s + 1) * 256, :] = jnp.where(low, heads[0], heads[2])
        oab[1, s * 256 : (s + 1) * 256, :] = jnp.where(low, heads[1], heads[3])
    at("attended")
    left, right = to_pairs(oab[0], oab[1])
    ao = jnp.concatenate([left, right], axis=1).astype(BF)
    sums = Sums(here, part, S, R, rss.at[2], rsr.at[2])
    sums.begin(lambda n: nt(ao, rows_of(wa, n, 2 * QD, QD)))
    at("x3 sent")
    sums.relay()
    at("x3 relayed")
    xn = x2[...] + sums.wait()
    x3[...] = xn
    h4[r] = (xn * rms_scale(xn) * vec[3:4, :]).astype(BF)
    blocks = Gather(here, h4, ags.at[3], agr.at[3])
    at("h4 sent")
    blocks.relay()
    at("h4 relayed")
    blocks.wait()
    for n in range(3):
        at("gate2 %d" % n)
        ffn_forward_tile(h4, wa, 3 * QD, gu2, u, n)
    save(6, h4, h4_out)
    save(7, gu2, gu2_out)
    at("down2")
    sums = Sums(here, part, S, R, rss.at[3], rsr.at[3])
    sums.begin(lambda n: nt(u[...], rows_of(wa, n, 3 * QD + WIDE, QF)))
    save(8, wa, wa_out)
    at("x4 sent")
    sums.relay()
    at("x4 relayed")
    out_tok[...] = (x3[...] + sums.wait()).astype(BF)

    def up_sent(dz):
        if not far(dz):

            @pl.when(z + dz < O)
            def _():
                up(dz).wait_send()

    along_z(up_sent)
    if bridged:

        @pl.when(z == 2)
        def _():
            over_far().wait_send()

    for w in sets:
        w.finish()
    wait_all(saving)


def any_spec():
    return pl.BlockSpec(memory_space=pl.ANY)


def vmem():
    return pl.BlockSpec(memory_space=pltpu.VMEM)


def forward(O, tok, cot, vec, hg, meta, freq, wc_hbm, wa_hbm):
    sds = jax.ShapeDtypeStruct
    G = 4 * T
    outs = (
        sds((T, D), BF),
        *(sds((T, D), F32) for _ in range(3)),
        *(sds((4, T, D), BF) for _ in range(4)),
        sds((3, G, QD), F32), sds((G, QD), F32),
        sds((G, WIDE), F32), sds((G, WIDE), F32),
        sds((3, G, 128), F32), sds((O, 4, 2, T, 256), BF), sds((2, G, 128), F32), sds((2, 8, 2 * G), F32),
        sds((2 * O, 2, D // (4 * O), CW), BF), sds((2 * O, 2, D // (4 * O), AW), BF),
        sds((2, 4, 256, 128), BF), sds((8, QD), F32), sds((8, QD), F32),
        sds((G, T), F32), sds((G, T), F32), sds((G, T), jnp.int32), sds((8, G), jnp.int32),
        sds((4, T, D), BF),
    )
    big = (len(outs) - 1, 4, 5, 6, 7, 10, 11, 13, 16, 17)
    dma = pltpu.SemaphoreType.DMA
    return pl.pallas_call(
        functools.partial(forward_kernel, O),
        out_shape=outs,
        in_specs=[vmem()] * 6 + [any_spec()] * 2,
        out_specs=tuple(any_spec() if i in big else vmem() for i in range(len(outs))),
        scratch_shapes=[
            *(pltpu.VMEM(outs[i].shape, outs[i].dtype) for i in big),
            pltpu.VMEM((G, QF), BF), pltpu.VMEM((2, 4, T, D // 2), F32),
            pltpu.VMEM((2, 6, T // 2, D // 2), BF), pltpu.VMEM((2, 6, T // 2, D // 2), BF),
            pltpu.VMEM((8, QD), F32), pltpu.VMEM((4, 256, 128), F32),
            pltpu.VMEM((O, 8, T), jnp.int32), pltpu.VMEM((2, O, 8, T), jnp.int32), pltpu.VMEM((4, 2, O, 8, T), jnp.int32),
            dma((5, 6)), dma((5, 6)), dma((4, 2, 6)), dma((4, 2, 6)), dma((2,)), dma((2,)),
            dma((2 * O + 1,)), dma((2 * O + 1,)),
            dma((2, 6)), dma((2, 6)), dma((2, 6)), dma((2, 6, O)), dma((2, 6, O)), dma((2, 6)), dma((2, 6)), dma((O + 3,)), dma((O + 3,)), dma((10,)),
        ],
        compiler_params=pltpu.CompilerParams(
            collective_id=1, has_side_effects=True, vmem_limit_bytes=61 * 2**20
        ),
        cost_estimate=pl.CostEstimate(flops=10**10, bytes_accessed=6 * 10**7, transcendentals=10**7),
        name="forward",
    )(tok, cot, vec, hg, meta, freq, wc_hbm, wa_hbm)


def tables(segments):
    zero = jnp.sum((segments == 0).astype(jnp.int32))
    two = jnp.sum((segments == 2).astype(jnp.int32))
    row = lax.broadcasted_iota(jnp.int32, (8, T), 0)
    meta = jnp.where(row == 0, segments, jnp.where(row == 1, zero, two))
    inverse_freq = rope_base ** (-(jnp.arange(HEAD_DIM // 2, dtype=F32) * 2.0) / HEAD_DIM)
    sign = jnp.where(jnp.arange(T) % HEAD_DIM < HEAD_DIM // 2, -1.0, 1.0).astype(F32)
    return meta, jnp.stack([jnp.concatenate([inverse_freq] * 4), sign])


def rms_back(x, gain, dh):
    r = rms_scale(x)
    inner = jnp.mean(x * gain * dh, axis=-1, keepdims=True)
    return r * gain * dh - x * (r * r * r) * inner, jnp.sum(dh * x * r, axis=0, keepdims=True)


def ffn_back_tile(DF, W, at, gu, dgu, mx, n):
    d = nn(DF[...].reshape(4 * T, D), cols(W, at + WIDE + n * TILE, TILE))
    two = slice(2 * n * TILE, (2 * n + 1) * TILE), slice((2 * n + 1) * TILE, 2 * (n + 1) * TILE)
    gate, up = gu[:, two[0]], gu[:, two[1]]
    sig = 1.0 / (1.0 + jnp.exp(-gate))
    silu = gate * sig
    dgu[:, two[0]] = (d * up * (sig * (1.0 + gate * (1.0 - sig)))).astype(BF)
    dgu[:, two[1]] = (d * silu).astype(BF)
    mx[:, n * TILE : (n + 1) * TILE] = (silu * up).astype(BF)


class Reduce:
    def __init__(self, here, parts, units, half, own, zb, off, zv, za, plane, out, zs, zr, ld, ps, pr):
        self.here, self.parts, self.units, self.half = here, parts, units, half
        self.own, self.zb, self.off, self.zv, self.za = own, zb, off, zv, za
        self.plane, self.out, self.zs, self.zr, self.ld, self.ps, self.pr = plane, out, zs, zr, ld, ps, pr
        self.few = here.O == 4

    def make(self, u, left, left_other, right, right_other, at):
        h = self.here
        place, width = self.units[u]
        step = TILE if width % TILE == 0 else 256
        rows = self.own.shape[1]

        def body(n, carry):
            o = pl.multiple_of(n * step, 128)
            a = nn(left[:, h.c].reshape(D // 2, 4 * T), right[:, pl.ds(at + o, step)])
            b = nn(left_other[...].reshape(D // 2, 4 * T), right_other[:, pl.ds(at + o, step)])
            self.own[:, :, pl.ds(place + o, step)] = (a + b).astype(BF).reshape(2 * h.O, rows, step)
            return carry

        lax.fori_loop(0, width // step, body, 0)

    def span(self, u):
        place, width = self.units[u]
        return pl.ds(place, width)

    def slot(self, u, dz):
        place, width = self.units[u]
        return self.zb.at[dz, :, :, pl.ds(self.off + place, width)]

    def hop(self, u, dz, plane):
        src = self.own.at[pl.ds(2 * plane, 2), :, self.span(u)]
        return remote(src, self.slot(u, dz), self.zs.at[u, dz], self.zr.at[u, dz], self.here.at(dz=dz))

    def far(self, u):
        h = self.here
        src = self.own.at[pl.ds(2 * (3 - h.z), 2), :, self.span(u)]
        to = h.at(dz=jnp.where(h.z == 0, 1, 3))
        return remote(src, self.slot(u, 0), self.zs.at[u, 0], self.zr.at[u, 0], to)

    def ends(self):
        return (self.here.z == 0) | (self.here.z == 3)

    def middle(self):
        return (self.here.z == 1) | (self.here.z == 2)

    def send(self, u):
        h = self.here
        if not self.few:

            def along(dz, carry):
                self.hop(u, dz, lax.rem(h.z + dz, h.O)).start()
                return carry

            lax.fori_loop(1, h.O, along, 0)
            return

        @pl.when(self.ends())
        def _():
            self.far(u).start()
            self.hop(u, 2, lax.rem(h.z + 2, 4)).start()

        @pl.when(h.z < 3)
        def _():
            self.hop(u, 1, h.z + 1).start()

        @pl.when(h.z > 0)
        def _():
            self.hop(u, 3, h.z - 1).start()

    def load(self, u, dz):
        _, width = self.units[u]
        return pltpu.make_async_copy(self.slot(u, dz), self.zv.at[dz, :, :, pl.ds(0, width)], self.ld.at[dz])

    def relay(self, u):
        if not self.few:
            return
        h = self.here
        _, width = self.units[u]

        @pl.when(self.middle())
        def _():
            self.far(u).wait_recv()
            self.load(u, 0).start()
            self.load(u, 0).wait()
            rows = pl.ds(2 * jnp.where(h.z == 1, 3, 0), 2)
            both = self.own[rows, :, self.span(u)].astype(F32) + self.zv[0, :, :, 0:width].astype(F32)
            self.own[rows, :, self.span(u)] = both.astype(BF)
            self.hop(u, 2, jnp.where(h.z == 1, 3, 0)).start()

    def total(self, u):
        h = self.here
        _, width = self.units[u]
        za = self.za.at[:, :, pl.ds(0, width)]
        za[...] = self.own[pl.ds(2 * h.z, 2), :, self.span(u)].astype(F32)

        def add(dz):
            za[...] += self.zv[dz, :, :, 0:width].astype(F32)

        if self.few:
            came = ((1, h.z > 0), (3, h.z < 3))
            self.hop(u, 2, 0).wait_recv()
            self.load(u, 2).start()
            for dz, there in came:

                @pl.when(there)
                def _():
                    self.hop(u, dz, 0).wait_recv()
                    self.load(u, dz).start()

            self.load(u, 2).wait()
            add(2)
            for dz, there in came:

                @pl.when(there)
                def _():
                    self.load(u, dz).wait()
                    add(dz)

        else:

            def along(dz, carry):
                self.hop(u, dz, 0).wait_recv()
                self.load(u, dz).start()
                self.load(u, dz).wait()
                add(dz)
                return carry

            lax.fori_loop(1, h.O, along, 0)
        self.plane[:, :, self.span(u)] = za[...].astype(BF)
        self.each(u, lambda cp: cp.start(), True)

    def pieces(self, u):
        r, half = self.here.r, self.half
        begin, size = self.units[u]
        out = []
        for base, stride, width, place, _ in self.parts:
            if not begin <= place < begin + size:
                continue
            first = half - base
            if base + 3 * stride + width <= half:
                out.append((place, width, 0, base + r * stride))
            elif first <= 0:
                out.append((place, width, 1, base + r * stride - half))
            else:
                assert base + stride >= half
                cut = min(first, width)
                out.append((place, cut, jnp.where(r == 0, 0, 1), jnp.where(r == 0, base, base + r * stride - half)))
                if cut < width:
                    out.append((place + cut, width - cut, 1, base + r * stride + cut - half))
        return out

    def each(self, u, act, local):
        h = self.here
        for place, width, owner, at in self.pieces(u):
            dx = lax.rem(owner + h.x, 2)
            dst = self.out.at[:, pl.ds(pl.multiple_of(at, 128), width)]
            for dy in (1, 0):
                src = self.plane.at[lax.rem(h.y + dy, 2), :, pl.ds(place, width)]
                cp = remote(src, dst, self.ps.at[u], self.pr, h.at(dx=dx, dy=dy))
                if dy:
                    act(cp)
                    continue

                @pl.when(dx != 0)
                def _():
                    act(cp)

                if local:

                    @pl.when(dx == 0)
                    def _():
                        pltpu.make_async_copy(src, dst, self.pr).start()

    def sent(self):
        h = self.here
        for u in range(len(self.units)):
            if not self.few:

                def along(dz, carry):
                    self.hop(u, dz, 0).wait_send()
                    return carry

                lax.fori_loop(1, h.O, along, 0)
                continue

            @pl.when(self.ends())
            def _():
                self.far(u).wait_send()

            self.hop(u, 2, 0).wait_send()

            @pl.when(h.z < 3)
            def _():
                self.hop(u, 1, 0).wait_send()

            @pl.when(h.z > 0)
            def _():
                self.hop(u, 3, 0).wait_send()

    def finish(self):
        for u in range(len(self.units)):
            self.each(u, lambda cp: cp.wait_send(), False)
        pltpu.make_async_copy(self.out, self.out, self.pr).wait()


class Slots:
    def __init__(self, ref, room, sem):
        self.ref, self.room, self.sem = ref, room, sem

    def read(self, i, s):
        if self.room is None:
            return self.ref[i, 2 * s : 2 * s + 2]
        cp = pltpu.make_async_copy(self.ref.at[i, pl.ds(2 * s, 2)], self.room, self.sem)
        cp.start()
        cp.wait()
        return self.room[...]


ATTN_UNITS = ((768 + WIDE, QF), (768, QF), (768 + QF, QF), (512, 256), (0, 512))
CONV_UNITS = ((1024 + WIDE, QF), (1024, QF), (1024 + QF, QF), (768, 256), (0, 768))


class Renew:
    def __init__(self, here, g, w, m, v, out, f32_room, bf_room, new, ls, ss, rs):
        self.here, self.g, self.state, self.out = here, g, (w, m, v), out
        self.f32_room, self.bf_room, self.new = f32_room, bf_room, new
        self.ls, self.ss, self.rs = ls, ss, rs
        self.flying = []

    def loads(self, k, at, width):
        rows = self.g.shape[0]
        slot = k % 2
        cols = pl.ds(at, width)
        out = [
            pltpu.make_async_copy(
                a.at[:, cols], self.f32_room.at[pl.ds((3 * slot + i) * rows, rows), pl.ds(0, width)], self.ls.at[slot, i]
            )
            for i, a in enumerate(self.state)
        ]
        out.append(
            pltpu.make_async_copy(
                self.g.at[:, cols], self.bf_room.at[pl.ds(slot * rows, rows), pl.ds(0, width)], self.ls.at[slot, 3]
            )
        )
        return out

    def run(self, spans):
        rows = self.g.shape[0]
        x = self.here.x
        half = self.g.shape[1]
        for cp in self.loads(0, *spans[0][1:]):
            cp.start()
        for k, (n, at, width) in enumerate(spans):
            if k + 1 < len(spans):
                for cp in self.loads(k + 1, *spans[k + 1][1:]):
                    cp.start()
            wait_all(self.loads(k, at, width))
            slot = k % 2
            w, m, v = (self.f32_room[(3 * slot + i) * rows : (3 * slot + i + 1) * rows, 0:width] for i in range(3))
            g = self.bf_room[slot * rows : (slot + 1) * rows, 0:width].astype(F32)
            new, _, _ = adam_update(w, m, v, g, STEP)
            place = self.new.at[n, 0, :, pl.ds(0, width)]
            place[...] = new.astype(BF)
            to = self.out.at[:, pl.ds(pl.multiple_of(x * half + at, 128), width)]
            self.flying.append(pltpu.make_async_copy(place, to, self.ls.at[2 + n, 0]))
            self.flying.append(remote(place, to, self.ss.at[n], self.rs.at[n], self.here.at(dx=1)))
            self.flying[-2].start()
            self.flying[-1].start()


def backward_kernel(
    O, cot, tok, vec, hg, x1, x2, x3, h1, h2, h3, h4, bcx, cz, gu1, gu2, qkr, kv, oab, lse, wc, wa, Q, tail_c, tail_z,
    cosb, sinb, start, start_row, cots,
    w_attn, m_attn, v_attn,
    dtok, total, ga, gc, new_attn, zb, dkc, dkz,
    W, gu, DG, HH, dgu, mx, sm, LT, other_lt, other_mx, other_sm, other_gu, own_a, *rest,
):
    few = O == 4
    own_c, rest = (rest[0], rest[1:]) if few else (own_a, rest)
    (zv, za, plane_a, plane_c, part, S, R, dO, delta, dq, dqab, dkv, dkk, heads, head_c, head_z, dprev, vg, v0, v1, v2,
     room, ags, agr, rss, rsr, hs, hr, kvs, kvr, wls, gls, hls, xs, xr, zs, zr, ld, ps, pr, vs, vr, rl, rls, rss2, rrs) = rest
    here = Place(O)
    x, y, z, c, r = here.x, here.y, here.z, here.c, here.r
    core_keys = Slots(dkc, None if few else room, rl)
    z_keys = Slots(dkz, None if few else room, rl)
    A = Reduce(here, ATTN_PARTS, ATTN_UNITS, (3 * D + 3 * FF) // 2, own_a, zb, 0, zv, za, plane_a, ga,
               zs.at[0], zr.at[0], ld, ps.at[0], pr.at[0])
    C = Reduce(here, CONV_PARTS, CONV_UNITS, (4 * D + 3 * FF) // 2, own_c, zb, AW, zv, za, plane_c, gc,
               zs.at[1], zr.at[1], ld, ps.at[1], pr.at[1])
    loads = [pltpu.make_async_copy(h, HH, hls.at[i]) for i, h in enumerate((h4, h3, h2, h1))]
    load_w = pltpu.make_async_copy(wa, W.at[:, :, :, pl.ds(0, AW)], wls.at[0])
    load_g = pltpu.make_async_copy(gu2, gu, gls.at[0])
    load_kv = pltpu.make_async_copy(kv, dkv, gls.at[2])
    load_d = pltpu.make_async_copy(cots, DG.at[0], gls.at[3])
    for cp in (load_d, load_w, load_g, loads[0], load_kv):
        cp.start()
    greet(here)
    vg[...] = jnp.zeros_like(vg)

    done = []

    def at(point):
        for step in REDUCTIONS[point]:
            red = A if step[1] == "a" else C
            {"s": red.send, "r": red.relay, "t": red.total}[step[0]](int(step[2]))

    def flat(H):
        return H[...].reshape(4 * T, D)

    def swap(i, src, dst):
        cp = remote(src, dst, xs.at[i], xr.at[i], here.at(dc=1))
        cp.start()
        return cp

    def turned(e, H):
        if done:
            done.pop().wait_send()
        LT[...] = jnp.transpose(flat(H)).reshape(LT.shape)
        cp = swap(e, LT.at[:, 1 - c], other_lt.at[e % 4])
        done.append(cp)
        return cp

    def turned_saved(i, e):
        loads[i].wait()
        cp = turned(e, HH)
        if i < 3:
            loads[i + 1].start()
        return cp

    def ffn_back(i, e, DF, base, x_in, gain_row, red, dy, name):
        lt = turned(e, DF)
        for n in range(3):
            ffn_back_tile(DF, W, base, gu, dgu, mx, n)
        mixed = swap(8 + e, mx, other_mx)
        grads = swap(9 + e, dgu, other_gu)
        sums = Sums(here, part, S, R, rss.at[i], rsr.at[i])
        sums.begin(lambda n: nt(dgu[...], rows_of(W, n, base, WIDE)))
        lt.wait_recv()
        mixed.wait()
        at(name + " down")
        if i and not few:
            A.sent()
        red.make(0, LT, other_lt.at[e % 4], mx, other_mx, 0)
        red.send(0)
        sums.relay()
        dx, dgain = rms_back(x_in[...], vec[gain_row : gain_row + 1, :], sums.wait())
        vg[gain_row : gain_row + 1, :] = dgain
        dprev[...] = dy + dx
        H2 = DG.at[(i + 1) % 2]
        H2[r] = dprev[...].astype(BF)
        blocks = Gather(here, H2, ags.at[i + 1], agr.at[i + 1])
        lt = turned_saved(i, e + 1)
        blocks.relay()
        lt.wait_recv()
        grads.wait()
        red.make(1, LT, other_lt.at[(e + 1) % 4], dgu, other_gu, 0)
        at(name + " wide")
        red.make(2, LT, other_lt.at[(e + 1) % 4], dgu, other_gu, QF)
        blocks.wait()
        at(name + " end")

    DF = DG.at[0]
    load_d.wait()
    load_w.wait()
    load_g.wait()
    ffn_back(0, 0, DF, 3 * QD, x3, 3, A, cot[...].astype(F32), "ffn2")
    load_g = pltpu.make_async_copy(gu1, gu, gls.at[1])
    load_g.start()

    DA = DG.at[1]
    d_out = nn(flat(DA), cols(W, 2 * QD, QD)).astype(BF).astype(F32)
    left, right = to_pairs(oab[0], oab[1])
    sm[:, 0:QD] = jnp.concatenate([left, right], axis=1).astype(BF)
    attended = swap(10, sm.at[:, 0:QD], other_sm.at[:, 0:QD])
    lt = turned(2, DA)
    da, db = to_pairs(d_out[:, 0:128], d_out[:, 128:256])
    for s in (0, 1):
        rows = slice(s * 256, (s + 1) * 256)
        four = stacked(da[rows], db[rows])
        o_of = (oab[0, rows, :], oab[1, rows, :])
        for g in range(4):
            dO[s, g] = four[g].astype(BF)
            dl = jnp.sum(four[g] * o_of[g % 2], axis=-1, keepdims=True)
            delta[s, :, g * 256 : (g + 1) * 256] = jnp.transpose(jnp.broadcast_to(dl, (256, 128)))[0:8, :]
    load_kv.wait()
    low = lane_low((256, 128))

    def pair_keys(s):
        two = pl.ds(2 * s, 2)
        return remote(dkv.at[:, two, 1 - c], dkc.at[:, two], kvs.at[s, 0], kvr.at[s, 0], here.at(dc=1))

    def down(s, d, owner):
        two = pl.ds(2 * s, 2)
        return remote(dkv.at[owner, two, c], dkz.at[z, two], kvs.at[s, d], kvr.at[s, d], here.at(dz=O - d))

    def send_keys(s):
        two = pl.ds(2 * s, 2)
        pair_keys(s).wait()

        def send_down(zz, carry):
            dkv[zz, two, c] = (dkv[zz, two, c].astype(F32) + core_keys.read(zz, s).astype(F32)).astype(BF)
            down(s, z - zz, zz).start()
            return carry

        lax.fori_loop(0, z, send_down, 0)
        dkk[s * 256 : (s + 1) * 256, :] = (
            dkv[z, two, c].astype(F32) + core_keys.read(z, s).astype(F32)
        ).reshape(256, 256)

    for s in (0, 1):
        at("attention %d" % s)
        dq[...] = jnp.zeros_like(dq)
        first_of = start_row[0:1, s * 256 : (s + 1) * 256]
        col = lax.broadcasted_iota(jnp.int32, (1, 256), 1)
        t = z * 512 + lax.div(col, T) * 256 + c * T + lax.rem(col, T)

        def chunk(j, carry):
            block = dkv[lax.div(j, 2), 2 * s + lax.rem(j, 2)].reshape(256, 256)
            k, v = block[:, 0:128], block[:, 128:256]
            key = j * 256 + lax.broadcasted_iota(jnp.int32, (256, 256), 0)
            allowed = (key >= first_of) & (key <= t)
            dk = jnp.zeros((256, 128), F32)
            dv = jnp.zeros((256, 128), F32)
            for g in range(4):
                span = slice(g * 256, (g + 1) * 256)
                p = jnp.where(allowed, jnp.exp(nt(k, Q[s, g]) - lse[s, 0:1, span]), 0.0)
                ds = (p * (nt(v, dO[s, g]) - delta[s, 0:1, span])).astype(BF)
                dv = dv + nn(p.astype(BF), dO[s, g])
                dk = dk + nn(ds, Q[s, g])
                dq[g] += tn(ds, k)
            dkv[lax.div(j, 2), 2 * s + lax.rem(j, 2)] = (
                jnp.concatenate([dk, dv], axis=1).astype(BF).reshape(2, T, 256)
            )
            return carry

        if s:
            lax.fori_loop(0, z + 1, chunk, 0)
            send_keys(0)
            lax.fori_loop(z + 1, 2 * z + 2, chunk, 0)
        else:
            lax.fori_loop(0, 2 * z + 2, chunk, 0)
        pair_keys(s).start()
        rows = slice(s * 256, (s + 1) * 256)
        dqab[0, rows, :] = jnp.where(low, dq[0], dq[2]) * (HEAD_DIM ** -0.5)
        dqab[1, rows, :] = jnp.where(low, dq[1], dq[3]) * (HEAD_DIM ** -0.5)
    lt.wait_recv()
    attended.wait()
    A.make(3, LT, other_lt.at[2], sm, other_sm, 0)
    send_keys(1)
    at("keys sent")

    def take(d, carry):
        @pl.when(z + d < O)
        def _():
            for s in (0, 1):
                down(s, d, z).wait_recv()
                dkk[s * 256 : (s + 1) * 256, :] += z_keys.read(z + d, s).astype(F32).reshape(256, 256)

        return carry

    lax.fori_loop(1, O, take, 0)
    at("keys")

    for i in range(3):
        up = dqab[i] if i < 2 else dkk[:, 0:128]
        raw = qkr[i]
        gain = hg[0:1, :] if i < 2 else hg[1:2, :]
        dw = up * cosb[...] + turn(up * sinb[...])
        rr = lax.rsqrt(head_mean(raw * raw) + norm_eps)
        dgain = jnp.sum(dw * raw * rr, axis=0, keepdims=True)
        row = 8 if i < 2 else 9
        vg[row : row + 1, 0:128] += dgain
        draw = rr * gain * dw - raw * (rr * rr * rr) * head_mean(raw * gain * dw)
        if i < 2:
            dqab[i] = draw
        else:
            sm[:, 512:640] = draw.astype(BF)
    left, right = to_pairs(dqab[0], dqab[1])
    sm[:, 256:384] = left.astype(BF)
    sm[:, 384:512] = right.astype(BF)
    sm[:, 640:768] = dkk[:, 128:256].astype(BF)
    grads = swap(11, sm.at[:, 256:768], other_sm.at[:, 256:768])
    sums = Sums(here, part, S, R, rss.at[1], rsr.at[1])
    sums.begin(lambda n: nt(sm[:, 256:768], rows_of(W, n, 0, 512)))
    load_w = pltpu.make_async_copy(wc, W, wls.at[1])
    load_w.start()
    lt = turned_saved(1, 3)
    sums.relay()
    lt.wait_recv()
    grads.wait()
    A.make(4, LT, other_lt.at[3], sm, other_sm, 256)
    at("qkv")
    dx, dgain = rms_back(x2[...], vec[2:3, :], sums.wait())
    vg[2:3, :] = dgain
    dprev[...] += dx
    D2 = DG.at[0]
    D2[r] = dprev[...].astype(BF)
    blocks = Gather(here, D2, ags.at[2], agr.at[2])
    blocks.relay()
    at("d2 relayed")
    load_w.wait()
    load_g.wait()
    blocks.wait()
    ffn_back(2, 4, D2, 4 * QD, x1, 1, C, dprev[...], "ffn1")

    DD = DG.at[1]
    tap0, tap1, tap2 = taps(here, vec)
    from_c, from_z = tail_c[...], jnp.where(z > 0, tail_z[...], 0.0)
    dyc = nn(flat(DD), cols(W, 3 * QD, QD))
    sm[:, 0:QD] = (bcx[1] * cz[...]).astype(BF)
    mixed = swap(14, sm.at[:, 0:QD], other_sm.at[:, 0:QD])
    sm[:, 2 * QD : 3 * QD] = (dyc * cz[...]).astype(BF)
    dzs = dyc * bcx[1]
    bx = bcx[0] * bcx[2]
    row = lax.broadcasted_iota(jnp.int32, (T, QD), 0)
    g0, g1, g2 = (jnp.zeros((1, QD), F32) for _ in range(3))
    for b in range(4):
        mine = bx[b * T : (b + 1) * T, :]
        dzb = dzs[b * T : (b + 1) * T, :]
        one, two, m1, m2 = behind(here, b, mine, from_c, from_z, start)
        g0 = g0 + jnp.sum(dzb * mine, axis=0, keepdims=True)
        g1 = g1 + jnp.sum(dzb * one * m1, axis=0, keepdims=True)
        g2 = g2 + jnp.sum(dzb * two * m2, axis=0, keepdims=True)
        b1 = tap1 * dzb * m1
        b2 = tap2 * dzb * m2
        heads[2 * b : 2 * b + 1, :] = b2[0:1]
        heads[2 * b + 1 : 2 * b + 2, :] = b1[0:1] + b2[1:2]
        dkk[b * T : (b + 1) * T, :] = (
            tap0 * dzb
            + jnp.where(row < T - 1, pltpu.roll(b1, T - 1, 0), 0.0)
            + jnp.where(row < T - 2, pltpu.roll(b2, T - 2, 0), 0.0)
        )
    over = remote(heads, head_c, hs.at[0], hr.at[0], here.at(dc=1))
    over.start()
    back = remote(heads, head_z, hs.at[1], hr.at[1], here.at(dz=O - 1, dc=1))

    @pl.when((c == 0) & (z > 0))
    def _():
        back.start()

    at("halo")
    lt = turned(6, DD)
    tap_at = pl.ds(pl.multiple_of(r * QD, 128), QD)
    vg[4:5, tap_at] = g0
    vg[5:6, tap_at] = g1
    vg[6:7, tap_at] = g2
    over.wait()

    @pl.when((c == 1) & (z < O - 1))
    def _():
        back.wait_recv()

    to_c, to_z = head_c[...], jnp.where(z < O - 1, head_z[...], 0.0)
    for b in range(4):
        rows = slice(b * T, (b + 1) * T)
        if b % 2:
            e = jnp.where(c == 0, to_c[2 * b : 2 * b + 2], to_z[2 * b - 2 : 2 * b])
        else:
            e = jnp.where(c == 0, to_c[2 * b : 2 * b + 2], to_c[2 * b + 2 : 2 * b + 4])
        dbx = dkk[rows, :] + jnp.where(row == T - 2, e[0:1], jnp.where(row == T - 1, e[1:2], 0.0))
        sm[rows, QD : 2 * QD] = (dbx * bcx[2, rows, :]).astype(BF)
        sm[rows, 3 * QD : 4 * QD] = (dbx * bcx[0, rows, :]).astype(BF)
    grads = swap(15, sm.at[:, QD : 4 * QD], other_sm.at[:, QD : 4 * QD])
    sums = Sums(here, part, S, R, rss.at[3], rsr.at[3])
    sums.begin(lambda n: nt(sm[:, QD : 4 * QD], rows_of(W, n, 0, 768)))
    lt.wait_recv()
    mixed.wait()
    C.make(3, LT, other_lt.at[2], sm, other_sm, 0)
    C.send(3)
    sums.relay()
    lt = turned_saved(3, 7)
    lt.wait_recv()
    grads.wait()
    C.make(4, LT, other_lt.at[3], sm, other_sm, QD)
    C.send(4)
    dx, dgain = rms_back(tok[...].astype(F32), vec[0:1, :], sums.wait())
    vg[0:1, :] = dgain
    dtok[...] = dprev[...] + dx

    v0[c] = vg[...]
    cp = remote(v0.at[c], v0.at[c], vs.at[0], vr.at[0], here.at(dc=1))
    cp.start()
    at("end")
    A.finish()
    renew = Renew(here, ga, w_attn, m_attn, v_attn, new_attn, gu, dgu, W, rls, rss2, rrs)
    step = 2 * AW // 6
    renew.run([(k, k * step, step) for k in range(6)])
    at("end 0")
    cp.wait()
    v1[r] = v0[0] + v0[1]
    copies = [
        remote(v1.at[r], v1.at[r], vs.at[1 + k], vr.at[1 + k], here.at(dx=dx, dy=dy)) for k, (dx, dy) in enumerate(PLANE)
    ]
    for cp in copies:
        cp.start()
    at("end 1")
    wait_all(copies)
    v2[z] = v1[0] + v1[1] + v1[2] + v1[3]

    def start_z(dz, carry):
        remote(v2.at[z], v2.at[z], vs.at[3 + dz], vr.at[3 + dz], here.at(dz=dz)).start()
        return carry

    lax.fori_loop(1, O, start_z, 0)
    at("end 2")

    def wait_z(dz, carry):
        remote(v2.at[z], v2.at[z], vs.at[3 + dz], vr.at[3 + dz], here.at(dz=dz)).wait()
        return carry

    lax.fori_loop(1, O, wait_z, 0)
    t = v2[0]
    for i in range(1, O):
        t = t + v2[i]
    total[...] = t

    def keys_sent(zz, carry):
        for s in (0, 1):
            down(s, z - zz, zz).wait_send()
        return carry

    lax.fori_loop(0, z, keys_sent, 0)
    @pl.when((c == 0) & (z > 0))
    def _():
        back.wait_send()

    for cp in done:
        cp.wait_send()
    if few:
        A.sent()
    C.sent()
    C.finish()
    wait_all(renew.flying)


def backward(O, cot, tok, vec, hg, saved, state):
    (x1, x2, x3, h1, h2, h3, h4, bcx, cz, gu1, gu2, qkr, kv, oab, lse, wc, wa, Q, tail_c, tail_z, cosb, sinb, start,
     start_row, cots) = saved
    sds = jax.ShapeDtypeStruct
    G = 4 * T
    rows = D // (4 * O)
    few = O == 4
    dma = pltpu.SemaphoreType.DMA
    V = pltpu.VMEM
    keys = sds((O, 4, T, 256), BF)
    outs = (
        sds((T, D), F32), sds((16, D), F32), sds((rows, 2 * AW), BF), sds((rows, 2 * CW), BF),
        sds((rows, 4 * AW), BF), sds((O, 2, rows, AW + CW), BF), keys, keys,
    )
    args = (cot, tok, vec, hg, *saved, *state)
    hbm = {id(a) for a in (*state, gu1, gu2, wc, wa, kv, h1, h2, h3, h4, cots)}
    keys_at = vmem() if few else any_spec()
    return pl.pallas_call(
        functools.partial(backward_kernel, O),
        out_shape=outs,
        in_specs=[any_spec() if id(a) in hbm else vmem() for a in args],
        out_specs=(vmem(), vmem(), *[any_spec()] * 4, keys_at, keys_at),
        scratch_shapes=[
            V((2 * O, 2, rows, CW), BF), V((G, WIDE), F32), V((2, 4, T, D), BF), V((4, T, D), BF),
            V((G, WIDE), BF), V((G, QF), BF), V((G, D), BF), V((2 * O, 2, rows, G), BF),
            V((4, 2 * O, rows, G), BF), V((G, QF), BF), V((G, D), BF), V((G, WIDE), BF),
            V((2 * O, rows, CW), BF), *([V((2 * O, rows, CW), BF)] if few else []),
            V((O, 2, rows, QF), BF), V((2, rows, QF), F32), V((2, rows, AW), BF), V((2, rows, CW), BF),
            V((2, 4, T, D // 2), F32), V((2, 6, T // 2, D // 2), BF), V((2, 6, T // 2, D // 2), BF),
            V((2, 4, 256, 128), BF), V((2, 8, 2 * G), F32), V((4, 256, 128), F32), V((2, G, 128), F32),
            V((O, 4, 2, T, 256), BF), V((G, 256), F32),
            V((8, QD), F32), V((8, QD), F32), V((8, QD), F32), V((T, D), F32), V((16, D), F32),
            V((2, 16, D), F32), V((4, 16, D), F32), V((O, 16, D), F32), V((2, T, 256), BF),
            dma((4, 6)), dma((4, 6)), dma((4, 2, 6)), dma((4, 2, 6)), dma((2,)), dma((2,)),
            dma((2, O)), dma((2, O)), dma((2,)), dma((4,)), dma((4,)), dma((16,)), dma((16,)),
            dma((2, 5, O)), dma((2, 5, O)), dma((O,)), dma((2, 5)), dma((2,)), dma((O + 3,)), dma((O + 3,)), dma,
            dma((8, 4)), dma((6,)), dma((6,)),
        ],
        compiler_params=pltpu.CompilerParams(
            collective_id=2, has_side_effects=True, vmem_limit_bytes=int(63.5 * 2**20)
        ),
        cost_estimate=pl.CostEstimate(flops=2 * 10**10, bytes_accessed=10**8, transcendentals=10**7),
        name="backward",
    )(*args)[:5]


REDUCTIONS = {
    "ffn2 down": (),
    "ffn2 wide": ("sa1",),
    "ffn2 end": (),
    "attention 0": (),
    "attention 1": ("ra0",),
    "keys sent": ("ta0", "ra1"),
    "keys": (),
    "qkv": ("sa2", "sa3", "sa4", "ta1"),
    "d2 relayed": ("ra2", "ra3", "ra4"),
    "ffn1 down": ("ta2", "ta3", "ta4"),
    "ffn1 wide": (),
    "ffn1 end": ("rc0",),
    "halo": ("sc1", "sc2"),
    "end": ("rc1", "rc2"),
    "end 0": ("tc0",),
    "end 1": ("tc1",),
    "end 2": ("rc3", "rc4", "tc2", "tc3", "tc4"),
}


def adam_update(master, first_moment, second, gradient, step_value):
    first_new = beta_one * first_moment + (1.0 - beta_one) * gradient
    second_new = beta_two * second + (1.0 - beta_two) * gradient * gradient
    first_hat = first_new / (1.0 - beta_one**step_value)
    second_hat = second_new / (1.0 - beta_two**step_value)
    master_new = master - learn_rate * (
        first_hat / (jnp.sqrt(second_hat) + adam_eps) + decay_rate * master
    )
    return (master_new, first_new, second_new)


def halves_kernel(half, whole, ls, ss, rs):
    x = lax.axis_index("dp")
    other = {"dp": 1 - x}
    barrier = pltpu.get_barrier_semaphore()
    pl.semaphore_signal(barrier, inc=1, device_id=other, device_id_type=MESH)
    pl.semaphore_wait(barrier, 1)
    width = half.shape[1]
    at = whole.at[:, pl.ds(pl.multiple_of(x * width, 128), width)]
    flying = [remote(half, at, ss, rs, other), pltpu.make_async_copy(half, at, ls)]
    for cp in flying:
        cp.start()
    wait_all(flying)


def halves(half):
    dma = pltpu.SemaphoreType.DMA
    return pl.pallas_call(
        halves_kernel,
        out_shape=jax.ShapeDtypeStruct((half.shape[0], 2 * half.shape[1]), half.dtype),
        in_specs=[any_spec()],
        out_specs=any_spec(),
        scratch_shapes=[dma, dma, dma],
        compiler_params=pltpu.CompilerParams(collective_id=3, has_side_effects=True),
        cost_estimate=pl.CostEstimate(flops=0, bytes_accessed=10**7, transcendentals=0),
        name="halves",
    )(half)


def shards(
    tokens, segments, cotangent, conv_weights, attn_weights, vectors, head_gains,
    master_conv, first_conv, second_conv, master_attn, first_attn, second_attn,
):
    O = lax.axis_size("z")
    hg = jnp.concatenate([head_gains, head_gains], axis=1)
    tok = tokens[0]
    out_tok, *saved = forward(O, tok, cotangent[0], vectors, hg, *tables(segments), conv_weights, attn_weights)
    dtok, total, ga, gc, attn_all = backward(
        O, cotangent[0], tok, vectors, hg, saved, (master_attn, first_attn, second_attn)
    )
    grad_attn, grad_conv = ga.astype(F32), gc.astype(F32)
    grad_vectors = total[0:7]
    grad_gains = total[8:10, 0:64] + total[8:10, 64:128]
    step_value = jnp.float32(STEP)
    new_conv = adam_update(master_conv, first_conv, second_conv, grad_conv, step_value)
    new_attn = adam_update(master_attn, first_attn, second_attn, grad_attn, step_value)
    conv_all = halves(new_conv[0].astype(BF))
    return (
        out_tok[None], dtok[None], grad_conv, grad_attn, grad_vectors, grad_gains, *new_conv, *new_attn,
        conv_all, attn_all,
    )


def solution(mesh):
    outer = mesh.shape["ctx"] // 4
    split = Mesh(mesh.devices.reshape(mesh.shape["dp"], outer, 2, 2), ("dp", "z", "y", "c"))
    ctx = ("z", "y", "c")
    seq, rows, state = P("dp", ctx, None), P(ctx, None), P(ctx, "dp")
    return jax.shard_map(
        shards,
        mesh=split,
        in_specs=(seq, P("dp", ctx), seq, rows, rows, P(), P(), *([state] * 6)),
        out_specs=(seq, seq, state, state, P(), P(), *([state] * 6), rows, rows),
        check_vma=False,
    )
```

time: 893 us -> 513 us (0.57)
  the two profiles are of different devices: /device:TPU:10 before, /device:TPU:26 now
where the time goes in v2:
time: 513 us; the launch traced here: 504 us
  Pallas kernels  476 us (93%)
  other arithmetic  19.1 us (4%)
  local copies, waits for them, and re-layouts  7.6 us (1%)
    pallas_call x1, Pallas kernels, backward(): pl.pallas_call(functools.partial(backward_kernel, O), out_shape=outs, in_...  220 us
    pallas_call x1, Pallas kernels, forward(): pl.pallas_call(functools.partial(forward_kernel, O), out_shape=outs, in_s...  216 us
    pallas_call x1, Pallas kernels, halves(): pl.pallas_call(halves_kernel, out_shape=jax.ShapeDtypeStruct((half.shape[...  40 us

profile of v2, /device:TPU:26, one launch (start us, length us, event | category | flops | bytes accessed | tf_op | source)
XLA Modules:
  0.0 504.0 jit_solution(12432624446219624061)
XLA Ops:
  0.7 0.1 maximum_bitcast_fusion
  0.8 1.4 pad_maximum_fusion
  2.2 1.3 fusion.2
  3.5 1.3 compare_select_fusion.1
  4.8 1.3 broadcast_select_fusion.meta
  6.1 215.7 %forward.1 = (bf16[128,1024]{1,0:T(8,128)(2,1)}, f32[128,1024]{1,0:T(8,128)}, f32[128,1024]{1,0:T(8,128)}, f32[128,1024]{1,0:T(8,128)}, bf16[4,128,1024]{2,1,0:T...) custom-call(bf16[128,1024]{1,0:T(8,128)(2,1)} %bitcast.10, ...), custom_call_target="tpu_custom_call" | custom-call | flops 10000000000 | bytes 60000000 | tf_op jit(solution)/shard_map/forward/pallas_call | solution.py:840
  221.8 220.4 %backward.1 = (f32[128,1024]{1,0:T(8,128)}, f32[16,1024]{1,0:T(8,128)}, bf16[64,8448]{1,0:T(8,128)(2,1)}, bf16[64,8960]{1,0:T(8,128)(2,1)}, bf16[64,16896]{1,0:T...) custom-call(bf16[128,1024]{1,0:T(8,128)(2,1)} %bitcast.13, ...), custom_call_target="tpu_custom_call" | custom-call | flops 20000000000 | bytes 100000000 | tf_op jit(solution)/shard_map/backward/pallas_call | solution.py:1543
  442.2 1.4 slice_add_fusion
  443.6 1.4 slice.9
  445.0 0.0 copy-start
  445.0 7.5 %multiply_subtract_fusion.1 = (f32[64,8448]{1,0:T(8,128)}, f32[64,8448]{1,0:T(8,128)}, f32[64,8448]{1,0:T(8,128)}, f32[64,8448]{1,0:T(8,128)}) fusion(f32[64,8448]{1,0:T(8,128)} %w_attn.1, f32[64,8448]{1,0:T(8,128)} %v_attn.1, f32[64,8448]{1,0:T(8,128)} %m_attn.1, bf16[64,8448]{1,0:T(8,128)(2,1)} %get-tuple-element.73), kind=kLoop, calls=%fused_computation.6 | loop fusion | flops 8650752 | bytes 16220160 | tf_op jit(solution)/shard_map/sub | solution.py:1598
  452.5 0.0 copy-done
  452.5 0.0 copy-done.1
  452.5 0.0 copy-done.2
  452.5 0.0 copy-done.4
  452.6 4.8 fusion.4
  457.3 40.0 %halves.1 = bf16[64,17920]{1,0:T(8,128)(2,1)} custom-call(bf16[64,8960]{1,0:T(8,128)(2,1)} %get-tuple-element.78.half), custom_call_target="tpu_custom_call" | custom-call | bytes 10000000 | tf_op jit(solution)/shard_map/halves/pallas_call | solution.py:1620
  497.4 0.0 copy-done.6
  497.4 0.7 copy.31
  498.1 0.0 copy-done.5
  498.1 0.8 copy.32
  498.9 3.3 copy.33
  502.2 0.0 copy-done.3
  502.2 1.3 copy.34
  (9 shorter events, 0.0 us)
Async XLA Ops:
  445.0 7.5 %copy-start = (f32[64,8960]{1,0:T(8,128)S(1)}, f32[64,8960]{1,0:T(8,128)}, u32[]{:S(2)}) copy-start(f32[64,8960]{1,0:T(8,128)} %param.20) | copy-start | bytes 6881284
  445.0 7.5 %copy-start.1 = (f32[64,8960]{1,0:T(8,128)S(1)}, f32[64,8960]{1,0:T(8,128)}, u32[]{:S(2)}) copy-start(f32[64,8960]{1,0:T(8,128)} %param.22) | copy-start | bytes 6881284
  445.0 7.5 %copy-start.2 = (f32[64,8960]{1,0:T(8,128)S(1)}, f32[64,8960]{1,0:T(8,128)}, u32[]{:S(2)}) copy-start(f32[64,8960]{1,0:T(8,128)} %param.21) | copy-start | bytes 6881284
  445.0 7.5 %copy-start.4 = (bf16[64,8960]{1,0:T(8,128)(2,1)S(1)}, bf16[64,8960]{1,0:T(8,128)(2,1)}, u32[]{:S(2)}) copy-start(bf16[64,8960]{1,0:T(8,128)(2,1)} %get-tuple-element.72) | copy-start | bytes 3440644
  457.3 40.0 %copy-start.6 = (bf16[128,1024]{1,0:T(8,128)(2,1)S(1)}, bf16[128,1024]{1,0:T(8,128)(2,1)}, u32[]{:S(2)}) copy-start(bf16[128,1024]{1,0:T(8,128)(2,1)} %get-tuple-element.45) | copy-start | bytes 786436
  457.3 40.7 %copy-start.5 = (f32[128,1024]{1,0:T(8,128)S(1)}, f32[128,1024]{1,0:T(8,128)}, u32[]{:S(2)}) copy-start(f32[128,1024]{1,0:T(8,128)} %get-tuple-element.71) | copy-start | bytes 1572868
  498.9 3.3 copy-start.3

commit v3 on v2

--- a/solution.py
+++ b/solution.py
@@ -1,6 +1,7 @@
 import functools
 import jax
 import jax.numpy as jnp
+import numpy as np
 from jax import lax
 from jax.sharding import Mesh, PartitionSpec as P
 import jax.experimental.pallas as pl
@@ -504,8 +505,8 @@
 
 
 def forward_kernel(
-    O, tok, cot, vec, hg, meta, freq, wc_hbm, wa_hbm,
-    out_tok, x1, x2, x3, h1_out, h2_out, h3_out, h4_out, bcx, cz, gu1_out, gu2_out, qkr, kv_out, oab, lse, wc_out, wa_out, Q,
+    O, tok, cot, vec, head_gains, segments, freq, wc_hbm, wa_hbm,
+    out_tok, hg, x1, x2, x3, h1_out, h2_out, h3_out, h4_out, bcx, cz, gu1_out, gu2_out, qkr, kv_out, oab, lse, wc_out, wa_out, Q,
     tail_c, tail_z, cosb, sinb, start, start_row, cots_out,
     cots, h1, h2, h3, h4, gu1, gu2, kv, wc, wa,
     u, part, S, R, tails, acc, M1, M2, M3,
@@ -529,7 +530,12 @@
             {"f": w.fetch, "p": w.push, "b": w.pass_far, "l": w.land, "r": w.ready}[step[0]](g)
 
     z_meta, core_meta, plane_meta = meta_copies(here, M1, M2, M3, ms, mr)
-    M1[z] = meta[...]
+    row = lax.broadcasted_iota(jnp.int32, (8, T), 0)
+    seg = segments[...]
+    count = [jnp.sum(jnp.where(seg == i, 1.0, 0.0), axis=1, keepdims=True).astype(jnp.int32) for i in (0, 2)]
+    M1[z] = jnp.where(row == 0, seg, jnp.where(row == 1, count[0], count[1]))
+    hg[:, 0:64] = head_gains[...]
+    hg[:, 64:128] = head_gains[...]
     z_meta(lambda cp: cp.start())
     saving = []
 
@@ -820,11 +826,11 @@
     return pl.BlockSpec(memory_space=pltpu.VMEM)
 
 
-def forward(O, tok, cot, vec, hg, meta, freq, wc_hbm, wa_hbm):
+def forward(O, tok, cot, vec, hg, segments, freq, wc_hbm, wa_hbm):
     sds = jax.ShapeDtypeStruct
     G = 4 * T
     outs = (
-        sds((T, D), BF),
+        sds((T, D), BF), sds((2, 128), F32),
         *(sds((T, D), F32) for _ in range(3)),
         *(sds((4, T, D), BF) for _ in range(4)),
         sds((3, G, QD), F32), sds((G, QD), F32),
@@ -835,7 +841,7 @@
         sds((G, T), F32), sds((G, T), F32), sds((G, T), jnp.int32), sds((8, G), jnp.int32),
         sds((4, T, D), BF),
     )
-    big = (len(outs) - 1, 4, 5, 6, 7, 10, 11, 13, 16, 17)
+    big = (len(outs) - 1, 5, 6, 7, 8, 11, 12, 14, 17, 18)
     dma = pltpu.SemaphoreType.DMA
     return pl.pallas_call(
         functools.partial(forward_kernel, O),
@@ -857,17 +863,14 @@
         ),
         cost_estimate=pl.CostEstimate(flops=10**10, bytes_accessed=6 * 10**7, transcendentals=10**7),
         name="forward",
-    )(tok, cot, vec, hg, meta, freq, wc_hbm, wa_hbm)
-
-
-def tables(segments):
-    zero = jnp.sum((segments == 0).astype(jnp.int32))
-    two = jnp.sum((segments == 2).astype(jnp.int32))
-    row = lax.broadcasted_iota(jnp.int32, (8, T), 0)
-    meta = jnp.where(row == 0, segments, jnp.where(row == 1, zero, two))
-    inverse_freq = rope_base ** (-(jnp.arange(HEAD_DIM // 2, dtype=F32) * 2.0) / HEAD_DIM)
-    sign = jnp.where(jnp.arange(T) % HEAD_DIM < HEAD_DIM // 2, -1.0, 1.0).astype(F32)
-    return meta, jnp.stack([jnp.concatenate([inverse_freq] * 4), sign])
+    )(tok, cot, vec, hg, segments, freq, wc_hbm, wa_hbm)
+
+
+def rotary_rows():
+    lane = np.arange(T)
+    freq = rope_base ** (-((lane % (HEAD_DIM // 2)).astype(np.float32) * 2.0) / HEAD_DIM)
+    sign = np.where(lane % HEAD_DIM < HEAD_DIM // 2, -1.0, 1.0)
+    return jnp.asarray(np.stack([freq, sign]), F32)
 
 
 def rms_back(x, gain, dh):
@@ -1046,7 +1049,7 @@
             dst = self.out.at[:, pl.ds(pl.multiple_of(at, 128), width)]
             for dy in (1, 0):
                 src = self.plane.at[lax.rem(h.y + dy, 2), :, pl.ds(place, width)]
-                cp = remote(src, dst, self.ps.at[u], self.pr, h.at(dx=dx, dy=dy))
+                cp = remote(src, dst, self.ps.at[u], self.pr.at[u], h.at(dx=dx, dy=dy))
                 if dy:
                     act(cp)
                     continue
@@ -1059,7 +1062,7 @@
 
                     @pl.when(dx == 0)
                     def _():
-                        pltpu.make_async_copy(src, dst, self.pr).start()
+                        pltpu.make_async_copy(src, dst, self.pr.at[u]).start()
 
     def sent(self):
         h = self.here
@@ -1087,10 +1090,38 @@
             def _():
                 self.hop(u, 3, 0).wait_send()
 
+    def spans_at(self, u, x):
+        half = self.half
+        begin, size = self.units[u]
+        out = []
+        for base, stride, width, place, _ in self.parts:
+            if begin <= place < begin + size:
+                for chip in range(4):
+                    lo = max(base + chip * stride, x * half)
+                    hi = min(base + chip * stride + width, (x + 1) * half)
+                    if lo < hi:
+                        out.append((lo - x * half, hi - lo))
+        joined = []
+        for at, width in sorted(out):
+            if joined and joined[-1][0] + joined[-1][1] == at:
+                joined[-1] = (joined[-1][0], joined[-1][1] + width)
+            else:
+                joined.append((at, width))
+        return joined
+
+    def owned(self, u):
+        for x in (0, 1):
+            width = sum(w for _, w in self.spans_at(u, x))
+            if width:
+
+                @pl.when(self.here.x == x)
+                def _():
+                    all_of = self.out.at[:, pl.ds(0, width)]
+                    pltpu.make_async_copy(all_of, all_of, self.pr.at[u]).wait()
+
     def finish(self):
         for u in range(len(self.units)):
             self.each(u, lambda cp: cp.wait_send(), False)
-        pltpu.make_async_copy(self.out, self.out, self.pr).wait()
 
 
 class Slots:
@@ -1115,7 +1146,8 @@
         self.here, self.g, self.state, self.out = here, g, (w, m, v), out
         self.f32_room, self.bf_room, self.new = f32_room, bf_room, new
         self.ls, self.ss, self.rs = ls, ss, rs
-        self.flying = []
+        self.next = [0, 0]
+        self.flying = ([], [])
 
     def loads(self, k, at, width):
         rows = self.g.shape[0]
@@ -1134,35 +1166,64 @@
         )
         return out
 
-    def run(self, spans):
-        rows = self.g.shape[0]
-        x = self.here.x
-        half = self.g.shape[1]
-        for cp in self.loads(0, *spans[0][1:]):
-            cp.start()
-        for k, (n, at, width) in enumerate(spans):
-            if k + 1 < len(spans):
-                for cp in self.loads(k + 1, *spans[k + 1][1:]):
-                    cp.start()
-            wait_all(self.loads(k, at, width))
-            slot = k % 2
-            w, m, v = (self.f32_room[(3 * slot + i) * rows : (3 * slot + i + 1) * rows, 0:width] for i in range(3))
-            g = self.bf_room[slot * rows : (slot + 1) * rows, 0:width].astype(F32)
-            new, _, _ = adam_update(w, m, v, g, STEP)
-            place = self.new.at[n, 0, :, pl.ds(0, width)]
-            place[...] = new.astype(BF)
-            to = self.out.at[:, pl.ds(pl.multiple_of(x * half + at, 128), width)]
-            self.flying.append(pltpu.make_async_copy(place, to, self.ls.at[2 + n, 0]))
-            self.flying.append(remote(place, to, self.ss.at[n], self.rs.at[n], self.here.at(dx=1)))
-            self.flying[-2].start()
-            self.flying[-1].start()
+    def steps(self, x, spans):
+        out = []
+        for at, width in spans:
+            parts = -(-width // WIDE)
+            while width % (128 * parts):
+                parts += 1
+            for p in range(parts):
+                n = self.next[x]
+                self.next[x] += 1
+                w, to = width // parts, at + p * (width // parts)
+                place = self.new(n, w)
+                dst = self.out.at[:, pl.ds(x * self.g.shape[1] + to, w)]
+                out.append((
+                    to, w, place, pltpu.make_async_copy(place, dst, self.ls.at[2 + n, 0]),
+                    remote(place, dst, self.ss.at[n], self.rs.at[n], self.here.at(dx=1)),
+                ))
+        self.flying[x].extend(out)
+        return out
+
+    def run(self, x, spans):
+        steps = self.steps(x, spans)
+        if not steps:
+            return
+
+        @pl.when(self.here.x == x)
+        def _():
+            rows = self.g.shape[0]
+            for cp in self.loads(0, *steps[0][:2]):
+                cp.start()
+            for k, (at, width, place, keep, give) in enumerate(steps):
+                if k + 1 < len(steps):
+                    for cp in self.loads(k + 1, *steps[k + 1][:2]):
+                        cp.start()
+                wait_all(self.loads(k, at, width))
+                slot = k % 2
+                w, m, v = (self.f32_room[(3 * slot + i) * rows : (3 * slot + i + 1) * rows, 0:width] for i in range(3))
+                g = self.bf_room[slot * rows : (slot + 1) * rows, 0:width].astype(F32)
+                place[...] = adam_update(w, m, v, g, STEP)[0].astype(BF)
+                keep.start()
+                give.start()
+
+    def wait(self):
+        for x in (0, 1):
+
+            @pl.when(self.here.x == x)
+            def _():
+                for _, _, _, keep, give in self.flying[x]:
+                    keep.wait()
+                    give.wait_send()
+                for _, _, _, _, give in self.flying[1 - x]:
+                    give.wait_recv()
 
 
 def backward_kernel(
     O, cot, tok, vec, hg, x1, x2, x3, h1, h2, h3, h4, bcx, cz, gu1, gu2, qkr, kv, oab, lse, wc, wa, Q, tail_c, tail_z,
     cosb, sinb, start, start_row, cots,
-    w_attn, m_attn, v_attn,
-    dtok, total, ga, gc, new_attn, zb, dkc, dkz,
+    w_attn, m_attn, v_attn, w_conv, m_conv, v_conv,
+    dtok, vectors, gains, ga, gc, new_attn, new_conv, zb, dkc, dkz,
     W, gu, DG, HH, dgu, mx, sm, LT, other_lt, other_mx, other_sm, other_gu, own_a, *rest,
 ):
     few = O == 4
@@ -1189,10 +1250,17 @@
 
     done = []
 
+    def move(kind, red, u):
+        if kind == "n":
+            red.owned(u)
+            for x_ in (0, 1):
+                renew_c.run(x_, red.spans_at(u, x_))
+        else:
+            {"s": red.send, "r": red.relay, "t": red.total}[kind](u)
+
     def at(point):
         for step in REDUCTIONS[point]:
-            red = A if step[1] == "a" else C
-            {"s": red.send, "r": red.relay, "t": red.total}[step[0]](int(step[2]))
+            move(step[0], A if step[1] == "a" else C, int(step[2]))
 
     def flat(H):
         return H[...].reshape(4 * T, D)
@@ -1429,6 +1497,15 @@
         back.start()
 
     at("halo")
+    rows = ga.shape[0]
+    renew_a = Renew(here, ga, w_attn, m_attn, v_attn, new_attn, gu, dgu,
+                    lambda n, w: other_gu.at[pl.ds(n * rows, rows), pl.ds(0, w)], rls.at[0], rss2.at[0], rrs.at[0])
+    renew_c = Renew(here, gc, w_conv, m_conv, v_conv, new_conv, gu, dgu,
+                    lambda n, w: W.at[n // 2, n % 2, :, pl.ds(0, w)], rls.at[1], rss2.at[1], rrs.at[1])
+    for u in range(5):
+        A.owned(u)
+    for x_ in (0, 1):
+        renew_a.run(x_, [(0, 2 * AW)])
     lt = turned(6, DD)
     tap_at = pl.ds(pl.multiple_of(r * QD, 128), QD)
     vg[4:5, tap_at] = g0
@@ -1456,13 +1533,13 @@
     lt.wait_recv()
     mixed.wait()
     C.make(3, LT, other_lt.at[2], sm, other_sm, 0)
-    C.send(3)
-    sums.relay()
     lt = turned_saved(3, 7)
     lt.wait_recv()
     grads.wait()
     C.make(4, LT, other_lt.at[3], sm, other_sm, QD)
-    C.send(4)
+    at("made")
+    sums.relay()
+    at("sums relayed")
     dx, dgain = rms_back(tok[...].astype(F32), vec[0:1, :], sums.wait())
     vg[0:1, :] = dgain
     dtok[...] = dprev[...] + dx
@@ -1471,11 +1548,6 @@
     cp = remote(v0.at[c], v0.at[c], vs.at[0], vr.at[0], here.at(dc=1))
     cp.start()
     at("end")
-    A.finish()
-    renew = Renew(here, ga, w_attn, m_attn, v_attn, new_attn, gu, dgu, W, rls, rss2, rrs)
-    step = 2 * AW // 6
-    renew.run([(k, k * step, step) for k in range(6)])
-    at("end 0")
     cp.wait()
     v1[r] = v0[0] + v0[1]
     copies = [
@@ -1502,7 +1574,9 @@
     t = v2[0]
     for i in range(1, O):
         t = t + v2[i]
-    total[...] = t
+    vectors[...] = t[0:7, :]
+    gains[...] = t[8:10, 0:64] + pltpu.roll(t[8:10, 0:128], 64, 1)[:, 0:64]
+    at("end 3")
 
     def keys_sent(zz, carry):
         for s in (0, 1):
@@ -1519,8 +1593,10 @@
     if few:
         A.sent()
     C.sent()
+    A.finish()
     C.finish()
-    wait_all(renew.flying)
+    renew_a.wait()
+    renew_c.wait()
 
 
 def backward(O, cot, tok, vec, hg, saved, state):
@@ -1534,8 +1610,8 @@
     V = pltpu.VMEM
     keys = sds((O, 4, T, 256), BF)
     outs = (
-        sds((T, D), F32), sds((16, D), F32), sds((rows, 2 * AW), BF), sds((rows, 2 * CW), BF),
-        sds((rows, 4 * AW), BF), sds((O, 2, rows, AW + CW), BF), keys, keys,
+        sds((T, D), F32), sds((7, D), F32), sds((2, HEAD_DIM), F32), sds((rows, 2 * AW), BF), sds((rows, 2 * CW), BF),
+        sds((rows, 4 * AW), BF), sds((rows, 4 * CW), BF), sds((O, 2, rows, AW + CW), BF), keys, keys,
     )
     args = (cot, tok, vec, hg, *saved, *state)
     hbm = {id(a) for a in (*state, gu1, gu2, wc, wa, kv, h1, h2, h3, h4, cots)}
@@ -1544,7 +1620,7 @@
         functools.partial(backward_kernel, O),
         out_shape=outs,
         in_specs=[any_spec() if id(a) in hbm else vmem() for a in args],
-        out_specs=(vmem(), vmem(), *[any_spec()] * 4, keys_at, keys_at),
+        out_specs=(vmem(), vmem(), vmem(), *[any_spec()] * 5, keys_at, keys_at),
         scratch_shapes=[
             V((2 * O, 2, rows, CW), BF), V((G, WIDE), F32), V((2, 4, T, D), BF), V((4, T, D), BF),
             V((G, WIDE), BF), V((G, QF), BF), V((G, D), BF), V((2 * O, 2, rows, G), BF),
@@ -1558,15 +1634,15 @@
             V((2, 16, D), F32), V((4, 16, D), F32), V((O, 16, D), F32), V((2, T, 256), BF),
             dma((4, 6)), dma((4, 6)), dma((4, 2, 6)), dma((4, 2, 6)), dma((2,)), dma((2,)),
             dma((2, O)), dma((2, O)), dma((2,)), dma((4,)), dma((4,)), dma((16,)), dma((16,)),
-            dma((2, 5, O)), dma((2, 5, O)), dma((O,)), dma((2, 5)), dma((2,)), dma((O + 3,)), dma((O + 3,)), dma,
-            dma((8, 4)), dma((6,)), dma((6,)),
+            dma((2, 5, O)), dma((2, 5, O)), dma((O,)), dma((2, 5)), dma((2, 5)), dma((O + 3,)), dma((O + 3,)), dma,
+            dma((2, 20, 4)), dma((2, 20)), dma((2, 20)),
         ],
         compiler_params=pltpu.CompilerParams(
             collective_id=2, has_side_effects=True, vmem_limit_bytes=int(63.5 * 2**20)
         ),
         cost_estimate=pl.CostEstimate(flops=2 * 10**10, bytes_accessed=10**8, transcendentals=10**7),
         name="backward",
-    )(*args)[:5]
+    )(*args)[:7]
 
 
 REDUCTIONS = {
@@ -1582,11 +1658,13 @@
     "ffn1 down": ("ta2", "ta3", "ta4"),
     "ffn1 wide": (),
     "ffn1 end": ("rc0",),
-    "halo": ("sc1", "sc2"),
-    "end": ("rc1", "rc2"),
-    "end 0": ("tc0",),
-    "end 1": ("tc1",),
-    "end 2": ("rc3", "rc4", "tc2", "tc3", "tc4"),
+    "halo": ("sc1",),
+    "made": ("sc2", "tc0"),
+    "sums relayed": ("rc1", "nc0"),
+    "end": ("tc1", "sc3", "sc4"),
+    "end 1": ("rc2", "nc1"),
+    "end 2": ("tc2", "rc3", "rc4", "nc2", "tc3", "tc4"),
+    "end 3": ("nc3", "nc4"),
 }
 
 
@@ -1601,52 +1679,19 @@
     return (master_new, first_new, second_new)
 
 
-def halves_kernel(half, whole, ls, ss, rs):
-    x = lax.axis_index("dp")
-    other = {"dp": 1 - x}
-    barrier = pltpu.get_barrier_semaphore()
-    pl.semaphore_signal(barrier, inc=1, device_id=other, device_id_type=MESH)
-    pl.semaphore_wait(barrier, 1)
-    width = half.shape[1]
-    at = whole.at[:, pl.ds(pl.multiple_of(x * width, 128), width)]
-    flying = [remote(half, at, ss, rs, other), pltpu.make_async_copy(half, at, ls)]
-    for cp in flying:
-        cp.start()
-    wait_all(flying)
-
-
-def halves(half):
-    dma = pltpu.SemaphoreType.DMA
-    return pl.pallas_call(
-        halves_kernel,
-        out_shape=jax.ShapeDtypeStruct((half.shape[0], 2 * half.shape[1]), half.dtype),
-        in_specs=[any_spec()],
-        out_specs=any_spec(),
-        scratch_shapes=[dma, dma, dma],
-        compiler_params=pltpu.CompilerParams(collective_id=3, has_side_effects=True),
-        cost_estimate=pl.CostEstimate(flops=0, bytes_accessed=10**7, transcendentals=0),
-        name="halves",
-    )(half)
-
-
 def shards(
     tokens, segments, cotangent, conv_weights, attn_weights, vectors, head_gains,
     master_conv, first_conv, second_conv, master_attn, first_attn, second_attn,
 ):
     O = lax.axis_size("z")
-    hg = jnp.concatenate([head_gains, head_gains], axis=1)
     tok = tokens[0]
-    out_tok, *saved = forward(O, tok, cotangent[0], vectors, hg, *tables(segments), conv_weights, attn_weights)
-    dtok, total, ga, gc, attn_all = backward(
-        O, cotangent[0], tok, vectors, hg, saved, (master_attn, first_attn, second_attn)
-    )
+    out_tok, hg, *saved = forward(O, tok, cotangent[0], vectors, head_gains, segments, rotary_rows(), conv_weights, attn_weights)
+    state = (master_attn, first_attn, second_attn, master_conv, first_conv, second_conv)
+    dtok, grad_vectors, grad_gains, ga, gc, attn_all, conv_all = backward(O, cotangent[0], tok, vectors, hg, saved, state)
     grad_attn, grad_conv = ga.astype(F32), gc.astype(F32)
-    grad_vectors = total[0:7]
-    grad_gains = total[8:10, 0:64] + total[8:10, 64:128]
     step_value = jnp.float32(STEP)
     new_conv = adam_update(master_conv, first_conv, second_conv, grad_conv, step_value)
     new_attn = adam_update(master_attn, first_attn, second_attn, grad_attn, step_value)
-    conv_all = halves(new_conv[0].astype(BF))
     return (
         out_tok[None], dtok[None], grad_conv, grad_attn, grad_vectors, grad_gains, *new_conv, *new_attn,
         conv_all, attn_all,

time: 513 us -> 490 us (0.955)
  the two profiles are of different devices: /device:TPU:26 before, /device:TPU:10 now
where the time goes in v3:
time: 490 us; the launch traced here: 481 us
  Pallas kernels  461 us (94%)
  other arithmetic  11.5 us (2%)
  local copies, waits for them, and re-layouts  6.49 us (1%)
    pallas_call x1, Pallas kernels, backward(): pl.pallas_call(functools.partial(backward_kernel, O), out_shape=outs, in_...  255 us
    pallas_call x1, Pallas kernels, forward(): pl.pallas_call(functools.partial(forward_kernel, O), out_shape=outs, in_s...  207 us
    sub x2, other arithmetic, adam_update(): master - learn_rate * (first_hat / (jnp.sqrt(second_hat) + adam_eps) + de...  11.5 us

profile of v3, /device:TPU:10, one launch (start us, length us, event | category | flops | bytes accessed | tf_op | source)
XLA Modules:
  0.0 480.6 jit_solution(17811920226187804929)
XLA Ops:
  0.6 206.8 %forward.1 = (bf16[128,1024]{1,0:T(8,128)(2,1)}, f32[2,128]{1,0:T(2,128)}, f32[128,1024]{1,0:T(8,128)}, f32[128,1024]{1,0:T(8,128)}, f32[128,1024]{1,0:T(8,128)}...) custom-call(bf16[128,1024]{1,0:T(8,128)(2,1)} %bitcast.6, ...), custom_call_target="tpu_custom_call" | custom-call | flops 10000000000 | bytes 60000000 | tf_op jit(solution)/shard_map/forward/pallas_call | solution.py:846
  207.5 254.6 %backward.1 = (f32[128,1024]{1,0:T(8,128)}, f32[7,1024]{1,0:T(8,128)}, f32[2,64]{1,0:T(2,128)}, bf16[64,8448]{1,0:T(8,128)(2,1)}, bf16[64,8960]{1,0:T(8,128)(2,1...) custom-call(bf16[128,1024]{1,0:T(8,128)(2,1)} %bitcast.9, ...), custom_call_target="tpu_custom_call" | custom-call | flops 20000000000 | bytes 100000000 | tf_op jit(solution)/shard_map/backward/pallas_call | solution.py:1619
  462.1 0.0 copy-start.1
  462.1 0.0 copy-start.2
  462.1 0.0 copy-start.3
  462.1 0.0 copy-start.5
  462.1 7.4 %multiply_subtract_fusion.1 = (f32[64,8448]{1,0:T(8,128)}, f32[64,8448]{1,0:T(8,128)}, f32[64,8448]{1,0:T(8,128)}, f32[64,8448]{1,0:T(8,128)}) fusion(f32[64,8448]{1,0:T(8,128)} %w_attn.1, f32[64,8448]{1,0:T(8,128)} %v_attn.1, f32[64,8448]{1,0:T(8,128)} %m_attn.1, bf16[64,8448]{1,0:T(8,128)(2,1)} %get-tuple-element.77), kind=kLoop, calls=%fused_computation.6 | loop fusion | flops 8650752 | bytes 16220160 | tf_op jit(solution)/shard_map/sub | solution.py:1676
  469.6 0.0 copy-done.1
  469.6 0.0 copy-done.2
  469.6 0.0 copy-done.3
  469.6 0.0 copy-done.5
  469.6 0.0 copy-start.7
  469.6 0.0 copy-start.6
  469.6 0.0 copy-start.8
  469.6 4.0 multiply_subtract_fusion
  473.7 0.7 copy.34
  474.4 0.8 copy.35
  475.2 0.0 copy-done.8
  475.2 0.6 copy.36
  475.8 0.6 copy.37
  476.4 0.0 copy-done
  476.4 1.4 copy.38
  477.8 1.1 copy-done.4
  478.8 1.3 copy.39
  (6 shorter events, 0.0 us)
Async XLA Ops:
  462.1 7.5 %copy-start.1 = (f32[64,8960]{1,0:T(8,128)S(1)}, f32[64,8960]{1,0:T(8,128)}, u32[]{:S(2)}) copy-start(f32[64,8960]{1,0:T(8,128)} %w_conv.1) | copy-start | bytes 6881284
  462.1 7.5 %copy-start.2 = (f32[64,8960]{1,0:T(8,128)S(1)}, f32[64,8960]{1,0:T(8,128)}, u32[]{:S(2)}) copy-start(f32[64,8960]{1,0:T(8,128)} %m_conv.1) | copy-start | bytes 6881284
  462.1 7.5 %copy-start.3 = (f32[64,8960]{1,0:T(8,128)S(1)}, f32[64,8960]{1,0:T(8,128)}, u32[]{:S(2)}) copy-start(f32[64,8960]{1,0:T(8,128)} %v_conv.1) | copy-start | bytes 6881284
  462.1 7.5 %copy-start.5 = (bf16[64,8960]{1,0:T(8,128)(2,1)S(1)}, bf16[64,8960]{1,0:T(8,128)(2,1)}, u32[]{:S(2)}) copy-start(bf16[64,8960]{1,0:T(8,128)(2,1)} %get-tuple-element.76) | copy-start | bytes 3440644
  469.6 4.1 copy-start.7
  469.6 4.8 copy-start.6
  469.6 5.6 %copy-start.8 = (f32[7,1024]{1,0:T(8,128)S(1)}, f32[7,1024]{1,0:T(8,128)}, u32[]{:S(2)}) copy-start(f32[7,1024]{1,0:T(8,128)} %get-tuple-element.108) | copy-start | bytes 86020
  469.6 6.2 %copy-start.9 = (f32[2,64]{1,0:T(2,128)S(1)}, f32[2,64]{1,0:T(2,128)}, u32[]{:S(2)}) copy-start(f32[2,64]{1,0:T(2,128)} %get-tuple-element.109) | copy-start | bytes 1540
  469.6 6.7 %copy-start = (bf16[64,17920]{1,0:T(8,128)(2,1)S(1)}, bf16[64,17920]{1,0:T(8,128)(2,1)}, u32[]{:S(2)}) copy-start(bf16[64,17920]{1,0:T(8,128)(2,1)} %get-tuple-element.116) | copy-start | bytes 6881284
  476.4 2.4 copy-start.4

commit v4 on v3

--- a/solution.py
+++ b/solution.py
@@ -34,8 +34,9 @@
     "in": ("f0", "f1",),
     "start": ("p0", "p1", "f2",),
     "h1 sent": ("f3", "p2",),
-    "h1 relayed": ("f4", "b0", "p3",),
-    "h1": ("f5", "l0", "p4", "l1", "r0",),
+    "h1 relayed": ("f4", "b0",),
+    "h1": ("f5", "l0", "l1", "r0",),
+    "halo": ("p3", "p4",),
     "conv": ("r1", "p5",),
     "x1 sent": (),
     "x1 relayed": ("b2", "f6", "f7",),
@@ -47,10 +48,10 @@
     "down1": ("p6", "l5", "p7", "r5", "p8",),
     "x2 sent": (),
     "x2 relayed": ("f9", "b6",),
-    "h3 sent": ("p9", "f10", "b7",),
+    "h3 sent": ("f10", "b7",),
     "h3 relayed": ("f11", "l6", "l7",),
     "qkv": ("r6",),
-    "kv sent": ("b8",),
+    "kv sent": ("p9", "b8",),
     "kv": ("p10",),
     "half": ("p11", "b9",),
     "attended": ("l8", "r7",),
@@ -579,15 +580,12 @@
     def _():
         ahead.start()
 
+    at("halo")
     over.wait()
 
     @pl.when((c == 0) & (z > 0))
     def _():
         ahead.wait_recv()
-
-    @pl.when((c == 1) & (z < O - 1))
-    def _():
-        ahead.wait_send()
 
     tap0, tap1, tap2 = taps(here, vec)
     from_c, from_z = tail_c[...], jnp.where(z > 0, tail_z[...], 0.0)
@@ -655,7 +653,7 @@
         kv[z, b, c, :, 128:256] = values[b * T : (b + 1) * T]
     mine = kv.at[z, :, c]
 
-    bridged = O == 4
+    bridged = False
 
     def far(dz):
         return bridged and dz == 3
@@ -798,6 +796,10 @@
     sums.relay()
     at("x4 relayed")
     out_tok[...] = (x3[...] + sums.wait()).astype(BF)
+
+    @pl.when((c == 1) & (z < O - 1))
+    def _():
+        ahead.wait_send()
 
     def up_sent(dz):
         if not far(dz):

time: 490 us -> 476 us (0.971)
  Pallas kernels: 461 us -> 447 us
    pallas_call x1, Pallas kernels: 207 us -> 188 us  [forward(): pl.pallas_call(functools.partial(forward_kernel, O), out_shape=outs, in_s...]
where the time goes in v4:
time: 476 us; the launch traced here: 466 us
  Pallas kernels  447 us (94%)
  other arithmetic  11.5 us (2%)
  local copies, waits for them, and re-layouts  6.49 us (1%)
    pallas_call x1, Pallas kernels, backward(): pl.pallas_call(functools.partial(backward_kernel, O), out_shape=outs, in_...  259 us
    pallas_call x1, Pallas kernels, forward(): pl.pallas_call(functools.partial(forward_kernel, O), out_shape=outs, in_s...  188 us
    sub x2, other arithmetic, adam_update(): master - learn_rate * (first_hat / (jnp.sqrt(second_hat) + adam_eps) + de...  11.5 us

profile of v4, /device:TPU:10, one launch (start us, length us, event | category | flops | bytes accessed | tf_op | source)
XLA Modules:
  0.0 466.4 jit_solution(15763490855466710116)
XLA Ops:
  0.6 188.2 %forward.1 = (bf16[128,1024]{1,0:T(8,128)(2,1)}, f32[2,128]{1,0:T(2,128)}, f32[128,1024]{1,0:T(8,128)}, f32[128,1024]{1,0:T(8,128)}, f32[128,1024]{1,0:T(8,128)}...) custom-call(bf16[128,1024]{1,0:T(8,128)(2,1)} %bitcast.6, ...), custom_call_target="tpu_custom_call" | custom-call | flops 10000000000 | bytes 60000000 | tf_op jit(solution)/shard_map/forward/pallas_call | solution.py:848
  188.9 259.0 %backward.1 = (f32[128,1024]{1,0:T(8,128)}, f32[7,1024]{1,0:T(8,128)}, f32[2,64]{1,0:T(2,128)}, bf16[64,8448]{1,0:T(8,128)(2,1)}, bf16[64,8960]{1,0:T(8,128)(2,1...) custom-call(bf16[128,1024]{1,0:T(8,128)(2,1)} %bitcast.9, ...), custom_call_target="tpu_custom_call" | custom-call | flops 20000000000 | bytes 100000000 | tf_op jit(solution)/shard_map/backward/pallas_call | solution.py:1621
  447.9 0.0 copy-start.1
  447.9 0.0 copy-start.2
  447.9 0.0 copy-start.3
  447.9 0.0 copy-start.5
  447.9 7.4 %multiply_subtract_fusion.1 = (f32[64,8448]{1,0:T(8,128)}, f32[64,8448]{1,0:T(8,128)}, f32[64,8448]{1,0:T(8,128)}, f32[64,8448]{1,0:T(8,128)}) fusion(f32[64,8448]{1,0:T(8,128)} %w_attn.1, f32[64,8448]{1,0:T(8,128)} %v_attn.1, f32[64,8448]{1,0:T(8,128)} %m_attn.1, bf16[64,8448]{1,0:T(8,128)(2,1)} %get-tuple-element.77), kind=kLoop, calls=%fused_computation.6 | loop fusion | flops 8650752 | bytes 16220160 | tf_op jit(solution)/shard_map/sub | solution.py:1678
  455.4 0.0 copy-done.1
  455.4 0.0 copy-done.2
  455.4 0.0 copy-done.3
  455.4 0.0 copy-done.5
  455.4 0.0 copy-start.7
  455.4 0.0 copy-start.6
  455.4 0.0 copy-start.8
  455.4 0.0 copy-start.9
  455.4 0.0 copy-start
  455.4 4.0 multiply_subtract_fusion
  459.5 0.7 copy.34
  460.2 0.8 copy.35
  461.0 0.6 copy.36
  461.6 0.6 copy.37
  462.2 1.4 copy.38
  463.5 1.1 copy-done.4
  464.6 1.3 copy.39
  (6 shorter events, 0.0 us)
Async XLA Ops:
  447.9 7.5 %copy-start.1 = (f32[64,8960]{1,0:T(8,128)S(1)}, f32[64,8960]{1,0:T(8,128)}, u32[]{:S(2)}) copy-start(f32[64,8960]{1,0:T(8,128)} %w_conv.1) | copy-start | bytes 6881284
  447.9 7.5 %copy-start.2 = (f32[64,8960]{1,0:T(8,128)S(1)}, f32[64,8960]{1,0:T(8,128)}, u32[]{:S(2)}) copy-start(f32[64,8960]{1,0:T(8,128)} %m_conv.1) | copy-start | bytes 6881284
  447.9 7.5 %copy-start.3 = (f32[64,8960]{1,0:T(8,128)S(1)}, f32[64,8960]{1,0:T(8,128)}, u32[]{:S(2)}) copy-start(f32[64,8960]{1,0:T(8,128)} %v_conv.1) | copy-start | bytes 6881284
  447.9 7.5 %copy-start.5 = (bf16[64,8960]{1,0:T(8,128)(2,1)S(1)}, bf16[64,8960]{1,0:T(8,128)(2,1)}, u32[]{:S(2)}) copy-start(bf16[64,8960]{1,0:T(8,128)(2,1)} %get-tuple-element.76) | copy-start | bytes 3440644
  455.4 4.1 copy-start.7
  455.4 4.8 %copy-start.6 = (f32[128,1024]{1,0:T(8,128)S(1)}, f32[128,1024]{1,0:T(8,128)}, u32[]{:S(2)}) copy-start(f32[128,1024]{1,0:T(8,128)} %get-tuple-element.75) | copy-start | bytes 1572868
  455.4 5.6 %copy-start.8 = (f32[7,1024]{1,0:T(8,128)S(1)}, f32[7,1024]{1,0:T(8,128)}, u32[]{:S(2)}) copy-start(f32[7,1024]{1,0:T(8,128)} %get-tuple-element.108) | copy-start | bytes 86020
  455.4 6.2 %copy-start.9 = (f32[2,64]{1,0:T(2,128)S(1)}, f32[2,64]{1,0:T(2,128)}, u32[]{:S(2)}) copy-start(f32[2,64]{1,0:T(2,128)} %get-tuple-element.109) | copy-start | bytes 1540
  455.4 6.7 %copy-start = (bf16[64,17920]{1,0:T(8,128)(2,1)S(1)}, bf16[64,17920]{1,0:T(8,128)(2,1)}, u32[]{:S(2)}) copy-start(bf16[64,17920]{1,0:T(8,128)(2,1)} %get-tuple-element.116) | copy-start | bytes 6881284
  462.2 2.4 copy-start.4
